TPU v7x, 512 devices: a whole 4x4x16 slice. The times are simulated.
512 devices in a mesh: inst: 64 (over x, z), tp: 8 (over y, core).
Axes of the slice: x: 4, y: 4, z: 16, core: 2. Of those that a mesh axis runs over, the one named last changes fastest.
Arguments:
- kv_cache: bfloat16 [1024, 64, 2048], P('inst', 'tp'), may hold values from -6 to 6
- route: int32 [1024], P('inst'), may hold values from 0 to 63, as said below
- queries: bfloat16 [4096, 6144], P('inst', 'tp'), may hold values from -110 to 110
- fresh_kv: bfloat16 [4096, 2048], P('inst', 'tp'), may hold values from -6 to 6
- picked: int32 [2048, 2], P('inst'), may hold values from 0 to 63, as said below
Outputs:
- attn_out: bfloat16 [4096, 6144], P('inst', 'tp')
- updated_cache: bfloat16 [1024, 64, 2048], P('inst', 'tp')
Inputs may be any that keep to these rules, and one draw needn't show every extreme that they name: `route`: one holder's 16 blocks go at most 2 to one executor, and some holder sends exactly 2 to some executor. One executor receives at most 32 blocks in all, and some executor exactly 32; every executor receives at least one. `picked`: the 2 positions of one row are distinct.
All inputs are finite; a program needn't handle non-finite values.
Results may differ from a plain program's by a relative error of at most 0.013.
Values may be sent and summed in bfloat16 or wider, within the bound.
No kernel may reach another device: no remote copies, remote signals or barrier semaphores. Data moves between devices by JAX's collectives and lax.ppermute only.
A program may use at most 64 MiB of HBM per device.

v0:
```python
import math

import jax
import jax.numpy as jnp
from jax import lax
from jax.sharding import PartitionSpec as P

HD = 128
QH = 6


THETA = 1000000.0


def rotate_pairs(values, shift):
    half = values.shape[-1] // 2
    freqs = jnp.power(
        jnp.float32(THETA), -2.0 * jnp.arange(half, dtype=jnp.float32) / values.shape[-1]
    )
    angle = shift * freqs
    cosine = jnp.cos(angle)
    sine = jnp.sin(angle)
    first = values[..., :half]
    second = values[..., half:]
    return jnp.concatenate(
        [first * cosine - second * sine, second * cosine + first * sine], axis=-1
    )


def ranks_within(table):
    equal = table[..., :, None] == table[..., None, :]
    index = jnp.arange(table.shape[-1], dtype=jnp.int32)
    earlier = index[:, None] > index[None, :]
    return jnp.sum((equal & earlier).astype(jnp.int32), axis=-1)


def context_slots(table, owner, maxrec):
    matched = table == owner
    counts = jnp.sum(matched.astype(jnp.int32), axis=1)
    inclusive = jnp.cumsum(counts)
    starts = inclusive - counts
    total = inclusive[-1]
    position = jnp.arange(maxrec, dtype=jnp.int32)
    holder_of = jnp.sum((inclusive[None, :] <= position[:, None]).astype(jnp.int32), axis=1)
    holder_of = jnp.minimum(holder_of, table.shape[0] - 1)
    slot_of = position - starts[holder_of]
    live = position < total
    return (holder_of, slot_of, live, total)


def blend_context(context, fresh_rows, chosen, block_len):
    maxrec = context.shape[0]
    shift = (jnp.arange(maxrec, dtype=jnp.float32) * block_len).reshape(maxrec, 1, 1, 1)
    keys = rotate_pairs(context[:, :, :, 0, :].astype(jnp.float32), shift).astype(jnp.bfloat16)
    merged = jnp.stack([keys, context[:, :, :, 1, :]], axis=3)
    index = jnp.arange(maxrec, dtype=jnp.int32)[:, None]
    return merged.at[index, chosen].set(fresh_rows)


def return_rows(fresh_rows, block_len):
    maxrec = fresh_rows.shape[0]
    shift = (jnp.arange(maxrec, dtype=jnp.float32) * block_len).reshape(maxrec, 1, 1, 1)
    keys = rotate_pairs(fresh_rows[:, :, :, 0, :].astype(jnp.float32), -shift).astype(jnp.bfloat16)
    merged = jnp.stack([keys, fresh_rows[:, :, :, 1, :]], axis=3)
    return merged.reshape(maxrec, fresh_rows.shape[1], -1)


def attend_heads(query_heads, key_heads, value_heads, group, allowed):
    scale = 1.0 / math.sqrt(query_heads.shape[-1])

    def one_head(head_idx):
        query_rows = query_heads[head_idx]
        key_rows = key_heads[head_idx // group]
        value_rows = value_heads[head_idx // group]
        scores = (
            lax.dot_general(
                query_rows, key_rows, (((1,), (1,)), ((), ())), preferred_element_type=jnp.float32
            )
            * scale
        )
        scores = jnp.where(allowed, scores, -1e30)
        peak = jnp.max(scores, axis=1, keepdims=True)
        weights = jnp.exp(scores - peak)
        total = jnp.sum(weights, axis=1, keepdims=True)
        mixed = jnp.dot(
            weights.astype(jnp.bfloat16), value_rows, preferred_element_type=jnp.float32
        )
        return mixed / total

    return lax.map(one_head, jnp.arange(query_heads.shape[0], dtype=jnp.int32))


def attention_block(merged, queries_dev, chosen, live, total, block_len, group):
    maxrec = merged.shape[0]
    heads_kv = merged.shape[2]
    head_size = merged.shape[4]
    rows = queries_dev.shape[0]
    key_heads = (
        merged[:, :, :, 0, :].reshape(maxrec * block_len, heads_kv, head_size).transpose(1, 0, 2)
    )
    value_heads = (
        merged[:, :, :, 1, :].reshape(maxrec * block_len, heads_kv, head_size).transpose(1, 0, 2)
    )
    query_heads = queries_dev.reshape(rows, heads_kv * group, head_size).transpose(1, 0, 2)
    key_pos = jnp.arange(maxrec * block_len, dtype=jnp.int32)
    key_live = key_pos < total * block_len
    query_pos = (jnp.arange(maxrec, dtype=jnp.int32)[:, None] * block_len + chosen).reshape(rows)
    allowed = key_live[None, :] & (key_pos[None, :] <= query_pos[:, None])
    mixed = attend_heads(query_heads, key_heads, value_heads, group, allowed)
    mixed = mixed.transpose(1, 0, 2).reshape(rows, heads_kv * group * head_size)
    row_live = jnp.repeat(live, chosen.shape[1])
    return jnp.where(row_live[:, None], mixed, 0.0).astype(jnp.bfloat16)


def local(kv_cache, route, queries, fresh_kv, picked):
    nodes = lax.axis_size("inst")
    tp_count = lax.axis_size("tp")
    own_inst = lax.axis_index("inst")
    tp_index = lax.axis_index("tp")
    hold = route.shape[0]
    slots = max(2, 2 * hold // nodes)
    block_rows = kv_cache.shape[1]
    block_len = block_rows * tp_count
    maxrec = picked.shape[0]
    heads_kv = fresh_kv.shape[1] // (2 * HD)
    num_slots = nodes * slots
    full_route = lax.all_gather(route, "inst", axis=0, tiled=True)
    dest = route * slots + ranks_within(route)
    slot_match = dest[None, :] == jnp.arange(num_slots, dtype=jnp.int32)[:, None]
    filled = jnp.any(slot_match, axis=1)
    source = jnp.sum(jnp.where(slot_match, jnp.arange(hold, dtype=jnp.int32)[None, :], 0), axis=1)
    outgoing = jnp.where(filled[:, None, None], kv_cache[source], jnp.zeros((), jnp.bfloat16))
    received = lax.all_to_all(
        lax.all_to_all(outgoing, "inst", split_axis=0, concat_axis=0, tiled=True),
        "tp",
        split_axis=2,
        concat_axis=1,
        tiled=True,
    )
    table = full_route.reshape(nodes, hold)
    holder_of, slot_of, live, total = context_slots(table, own_inst, maxrec)
    slot_index = jnp.clip(holder_of * slots + slot_of, 0, num_slots - 1)
    context = received[slot_index].reshape(maxrec, block_len, heads_kv, 2, HD)
    fresh_rows = fresh_kv.reshape(maxrec, picked.shape[1], heads_kv, 2, HD)
    merged = blend_context(context, fresh_rows, picked, block_len)
    attn_out = attention_block(merged, queries, picked, live, total, block_len, QH)
    back = return_rows(fresh_rows, block_len)
    target = jnp.where(live, slot_index, num_slots)
    send_rows = (
        jnp.zeros((num_slots, picked.shape[1], back.shape[2]), jnp.bfloat16)
        .at[target]
        .set(back, mode="drop")
    )
    send_pos = (
        jnp.zeros((num_slots, picked.shape[1]), jnp.bfloat16)
        .at[target]
        .set(picked.astype(jnp.bfloat16), mode="drop")
    )
    got_rows, got_pos = (
        lax.all_to_all(send_rows, "inst", split_axis=0, concat_axis=0, tiled=True),
        lax.all_to_all(send_pos, "inst", split_axis=0, concat_axis=0, tiled=True),
    )
    every_head = lax.all_gather(got_rows, "tp", axis=2, tiled=True)
    local_row = got_pos.astype(jnp.int32) - tp_index * block_rows
    fits = filled[:, None] & (local_row >= 0) & (local_row < block_rows)
    target_block = jnp.where(fits, source[:, None], hold)
    updated_cache = kv_cache.at[target_block, jnp.clip(local_row, 0, block_rows - 1)].set(
        every_head, mode="drop"
    )
    return (attn_out, updated_cache)


def solution(mesh):
    placed = (P("inst", "tp", None), P("inst"), P("inst", "tp"), P("inst", "tp"), P("inst", None))
    return jax.shard_map(
        local,
        mesh=mesh,
        in_specs=placed,
        out_specs=(P("inst", "tp"), P("inst", "tp", None)),
        check_vma=False,
    )
```

profile of v0, /device:TPU:1, one launch (start us, length us, event | category | flops | bytes accessed | tf_op | source)
XLA Modules:
  0.0 405.2 jit_solution(7942400906550745202)
XLA Ops:
  7.2 1.0 copy.197
  8.2 1.3 dynamic-slice
  10.1 0.9 dynamic-update-slice
  11.0 29.8 %all-reduce = s32[1024]{0:T(1024)S(1)} all-reduce(s32[1024]{0:T(1024)S(1)} %dynamic-update-slice), channel_id=1, replica_groups=mesh['inst'=64,'tp'=8] {'inst'}, use_global_device_ids=true, to_apply=%add | all-reduce | flops 1024 | bytes 8192
  42.0 0.8 fusion.40
  44.9 1.1 copy.165
  46.0 7.5 %all-to-all-start.2 = ((bf16[64,2,2]{1,2,0:T(2,128)(2,1)}), bf16[64,2,2]{1,2,0:T(2,128)(2,1)S(1)}, u32[]{:S(2)}, u32[]{:S(2)}) async-start(bf16[64,2,2]{1,2,0:T(2,128)(2,1)} %copy.165), calls=%async_computation.2 | async-start | bytes 65536 | tf_op jit(solution)/shard_map/all_to_all | solution.py:161
  53.5 0.9 convert_reduce_fusion.1
  55.3 2.8 gather_fusion
  58.0 4.5 %broadcast_select_fusion = bf16[128,8,2048]{2,1,0:T(8,128)(2,1)} fusion(bf16[128,8,2048]{2,1,0:T(8,128)(2,1)} %gather_fusion, pred[128]{0:T(512)(128)(4,1)S(1)} %fusion.22), kind=kLoop, calls=%fused_computation.24 | loop fusion | flops 2097152 | bytes 8388736 | tf_op jit(solution)/shard_map/jit(_where)/select_n | solution.py:132
  62.6 4.1 %all-to-all-done.2 = bf16[64,2,2]{1,2,0:T(2,128)(2,1)S(1)} async-done(((bf16[64,2,2]{1,2,0:T(2,128)(2,1)}), bf16[64,2,2]{1,2,0:T(2,128)(2,1)S(1)}, u32[]{:S(2)}, u32[]{:S(2)}) %all-to-all-start.2) | async-done | bytes 544 | tf_op jit(solution)/shard_map/all_to_all | solution.py:161
  66.7 10.8 %all-to-all-start = ((bf16[128,8,2048]{2,1,0:T(8,128)(2,1)}), bf16[128,8,2048]{2,1,0:T(8,128)(2,1)}, u32[]{:S(2)}, u32[]{:S(2)}) async-start(bf16[128,8,2048]{2,1,0:T(8,128)(2,1)} %broadcast_select_fusion), calls=%async_computation | async-start | bytes 8388608 | tf_op jit(solution)/shard_map/all_to_all | solution.py:134
  78.2 0.7 broadcast_in_dim.121
  78.9 4.1 %scatter_fusion.1 = bf16[128,2,256]{2,1,0:T(2,128)(2,1)} fusion(bf16[128,2,256]{2,1,0:T(2,128)(2,1)} %broadcast_in_dim.121, s32[32]{0:T(128)S(1)} %get-tuple-element.166, bf16[32,2,256]{2,1,0:T(2,128)(2,1)S(1)} %reshape.568), kind=kCustom, calls=%fused_computation.5 | custom fusion | bytes 98432 | tf_op jit(solution)/shard_map/scatter | solution.py:152
  83.0 174.3 %all-to-all-done = bf16[128,8,2048]{2,1,0:T(8,128)(2,1)} async-done(((bf16[128,8,2048]{2,1,0:T(8,128)(2,1)}), bf16[128,8,2048]{2,1,0:T(8,128)(2,1)}, u32[]{:S(2)}, u32[]{:S(2)}) %all-to-all-start) | async-done | bytes 4194336 | tf_op jit(solution)/shard_map/all_to_all | solution.py:134
  257.3 13.5 %all-to-all-start.3 = ((bf16[128,2,256]{2,1,0:T(2,128)(2,1)}), bf16[128,2,256]{2,1,0:T(2,128)(2,1)S(1)}, u32[]{:S(2)}, u32[]{:S(2)}) async-start(bf16[128,2,256]{2,1,0:T(2,128)(2,1)} %scatter_fusion.1), calls=%async_computation.3 | async-start | bytes 262144 | tf_op jit(solution)/shard_map/all_to_all | solution.py:160
  270.8 7.2 %copy.155 = bf16[128,8,2048]{0,1,2:T(8,128)(2,1)} copy(bf16[128,8,2048]{2,1,0:T(8,128)(2,1)} %all-to-all-done) | data formatting | bytes 8388608 | tf_op jit(solution)/shard_map/all_to_all | solution.py:134
  278.0 6.9 %all-to-all-done.3 = bf16[128,2,256]{2,1,0:T(2,128)(2,1)S(1)} async-done(((bf16[128,2,256]{2,1,0:T(2,128)(2,1)}), bf16[128,2,256]{2,1,0:T(2,128)(2,1)S(1)}, u32[]{:S(2)}, u32[]{:S(2)}) %all-to-all-start.3) | async-done | bytes 131104 | tf_op jit(solution)/shard_map/all_to_all | solution.py:160
  285.5 8.6 %all-to-all-start.1 = ((bf16[128,8,2048]{0,1,2:T(8,128)(2,1)}), bf16[128,8,2048]{0,1,2:T(8,128)(2,1)}, u32[]{:S(2)}, u32[]{:S(2)}) async-start(bf16[128,8,2048]{0,1,2:T(8,128)(2,1)} %copy.155), calls=%async_computation.1 | async-start | bytes 8388608 | tf_op jit(solution)/shard_map/all_to_all | solution.py:133
  298.2 28.6 %all-gather.2.cloned.1.call-done = bf16[128,2,2048]{2,1,0:T(2,128)(2,1)} async-done(((bf16[128,2,256]{2,1,0:T(2,128)(2,1)}), bf16[128,2,2048]{2,1,0:T(2,128)(2,1)}) %all-gather.2.cloned.1.call-update) | async-done | bytes 1048592 | tf_op jit(solution)/shard_map/all_gather | solution.py:163
  326.8 1.5 reshape.557
  328.2 22.4 %scatter_fusion.2 = bf16[16,8,2048]{2,1,0:T(8,128)(2,1)S(1)} fusion(bf16[16,8,2048]{2,1,0:T(8,128)(2,1)S(1)} %copy.197, s32[256]{0:T(256)S(1)} %reshape.555, bf16[256,2048]{1,0:T(8,128)(2,1)S(1)} %reshape.557), kind=kCustom, calls=%fused_computation.6 | custom fusion | bytes 3147776 | tf_op jit(solution)/shard_map/scatter | solution.py:167
  350.6 7.5 %copy.157 = bf16[128,8,8,256]{3,2,1,0:T(8,128)(2,1)} copy(bf16[128,8,8,256]{0,2,3,1:T(8,128)(2,1)} %bitcast.8) | data formatting | bytes 8388608 | tf_op jit(solution)/shard_map/all_to_all | solution.py:133
  358.1 2.8 gather_fusion.2
  361.2 1.5 slice_convert_fusion
  363.3 1.0 copy.158
  364.3 1.0 copy.159
  365.3 4.3 %maximum_bitcast_fusion = bf16[32,64,2,128]{3,2,1,0:T(2,128)(2,1)S(1)} fusion(bf16[32,64,1,1,128]{4,3,1,0,2:T(2,128)(2,1)S(1)} %get-tuple-element.155, bf16[32,64,1,1,64]{4,3,1,0,2:T(2,128)(2,1)S(1)} %copy.159, bf16[32,64,1,1,64]{4,3,1,0,2:T(2,128)(2,1)S(1)} %copy.158), kind=kLoop, calls=%fused_computation.26 | loop fusion | flops 3145728 | bytes 2097152 | tf_op jit(solution)/shard_map/stack | solution.py:55
  369.6 3.2 scatter_fusion
  372.8 2.3 fusion.39
  375.2 22.4 %while.11 = (s32[]{:T(128)}, bf16[6,64,128]{2,1,0:T(8,128)(2,1)S(1)}, s32[6]{0:T(128)S(1)}, bf16[6,64,128]{2,1,0:T(8,128)(2,1)S(1)}, bf16[1,2048,128]{2,1,0:T(8,...) while((s32[]{:T(128)}, ...), condition=%wide.region_10.11_spmd.clone, body=%wide.region_7.10_spmd.clone.sunk | while | flops 68296576 | bytes 2675107 | solution.py:90
  397.6 0.7 fusion.17
  (100 shorter events, 19.5 us)
Async XLA Ops:
  46.0 20.7 %all-to-all-start.2 = ((bf16[64,2,2]{1,2,0:T(2,128)(2,1)}), bf16[64,2,2]{1,2,0:T(2,128)(2,1)S(1)}, u32[]{:S(2)}, u32[]{:S(2)}) async-start(bf16[64,2,2]{1,2,0:T(2,128)(2,1)} %copy.165), calls=%async_computation.2 | async-start | bytes 65536 | tf_op jit(solution)/shard_map/all_to_all | solution.py:161
  62.6 15.0 %copy-start.2 = (bf16[64,256]{1,0:T(8,128)(2,1)S(1)}, bf16[64,256]{1,0:T(8,128)(2,1)}, u32[]{:S(2)}) copy-start(bf16[64,256]{1,0:T(8,128)(2,1)} %param.10) | copy-start | bytes 98308
  66.7 190.5 %all-to-all-start = ((bf16[128,8,2048]{2,1,0:T(8,128)(2,1)}), bf16[128,8,2048]{2,1,0:T(8,128)(2,1)}, u32[]{:S(2)}, u32[]{:S(2)}) async-start(bf16[128,8,2048]{2,1,0:T(8,128)(2,1)} %broadcast_select_fusion), calls=%async_computation | async-start | bytes 8388608 | tf_op jit(solution)/shard_map/all_to_all | solution.py:134
  257.3 27.6 %all-to-all-start.3 = ((bf16[128,2,256]{2,1,0:T(2,128)(2,1)}), bf16[128,2,256]{2,1,0:T(2,128)(2,1)S(1)}, u32[]{:S(2)}, u32[]{:S(2)}) async-start(bf16[128,2,256]{2,1,0:T(2,128)(2,1)} %scatter_fusion.1), calls=%async_computation.3 | async-start | bytes 262144 | tf_op jit(solution)/shard_map/all_to_all | solution.py:160
  284.8 0.7 copy-start.1
  284.9 10.0 %copy-start.4 = (s32[32,2]{0,1:T(2,128)S(1)}, s32[32,2]{0,1:T(2,128)}, u32[]{:S(2)}) copy-start(s32[32,2]{0,1:T(2,128)} %param.11) | copy-start | bytes 772
  284.9 11.0 %copy-start.3 = (bf16[64,768]{1,0:T(8,128)(2,1)S(1)}, bf16[64,768]{1,0:T(8,128)(2,1)}, u32[]{:S(2)}) copy-start(bf16[64,768]{1,0:T(8,128)(2,1)} %param.9) | copy-start | bytes 294916
  285.5 65.1 %all-to-all-start.1 = ((bf16[128,8,2048]{0,1,2:T(8,128)(2,1)}), bf16[128,8,2048]{0,1,2:T(8,128)(2,1)}, u32[]{:S(2)}, u32[]{:S(2)}) async-start(bf16[128,8,2048]{0,1,2:T(8,128)(2,1)} %copy.155), calls=%async_computation.1 | async-start | bytes 8388608 | tf_op jit(solution)/shard_map/all_to_all | solution.py:133
  294.1 32.7 %all-gather.2.cloned.1.call-start = ((), (), s32[]{:S(2)}) async-start(), calls=%async_computation.4 | async-start | bytes 1179648 | tf_op jit(solution)/shard_map/all_gather | solution.py:163
  350.6 7.5 %copy-start = (bf16[16,8,2048]{2,1,0:T(8,128)(2,1)}, bf16[16,8,2048]{2,1,0:T(8,128)(2,1)S(1)}, u32[]{:S(2)}) copy-start(bf16[16,8,2048]{2,1,0:T(8,128)(2,1)S(1)} %scatter_fusion.2) | copy-start | bytes 1572868
Sparse Core Ops, SparseCore 0:
  297.6 29.1 all-gather.1
where the time goes:
time: 406 us; the launch traced here: 405 us
  waiting for transfers between devices  215 us (53%)
  local copies, waits for them, and re-layouts  70 us (17%)
  starting transfers between devices  40.4 us (10%)
  blocking collectives  29.8 us (7%)
  other arithmetic  17.8 us (4%)
  between operations  15.7 us (4%)
  loops' own time  12.5 us (3%)
  matrix products  4.3 us (1%)
    all_to_all x1, waiting for transfers between devices, local(): lax.all_to_all(outgoing, 'inst', split_axis=0, concat_axis=0, tiled=True)  174 us
    unnamed x1, blocking collectives  29.8 us
    all_gather x1, waiting for transfers between devices, local(): every_head = lax.all_gather(got_rows, 'tp', axis=2, tiled=True)  28.6 us
    scatter x1, local copies, waits for them, and re-layouts, local(): kv_cache.at[target_block, jnp.clip(local_row, 0, block_rows - 1)]  22.4 us
    all_to_all x1, starting transfers between devices, local(): lax.all_to_all(send_rows, 'inst', split_axis=0, concat_axis=0, tiled=True)  13.5 us
    another operation x1, loops' own time, attend_heads(): return lax.map(one_head, jnp.arange(query_heads.shape[0], dtype=jnp.int32))  12.5 us
    all_to_all x1, starting transfers between devices, local(): lax.all_to_all(outgoing, 'inst', split_axis=0, concat_axis=0, tiled=True)  10.8 us
    all_to_all x1, starting transfers between devices, local(): lax.all_to_all(lax.all_to_all(outgoing, 'inst', split_axis=0, concat_axis...  8.57 us
  transfers between devices with their start and end apart: 5, of which 4 were waited for; matrix products, arithmetic and copies ran while one was open for 12% of the time, Pallas kernels for 0%

commit v1 on v0

v1 whole, which is shorter than its diff:
```python
import functools
import math

import jax
import jax.numpy as jnp
from jax import lax
from jax.experimental import pallas as pl
from jax.experimental.pallas import tpu as pltpu
from jax.sharding import PartitionSpec as P

HD = 128
QH = 6
THETA = 1000000.0
CTX = 32
UNITS = 36
VMEM = pl.BlockSpec(memory_space=pltpu.VMEM)
SMEM = pl.BlockSpec(memory_space=pltpu.SMEM)
PARAMS = pltpu.CompilerParams(vmem_limit_bytes=40 * 1024 * 1024)


def spread_kernel(own_ref, x_ref, ctrl_ref, out_ref):
    y = own_ref[1]

    def step(g, carry):
        for k in range(2):
            block = lax.rem(g - y + 8, 8) + 8 * k
            for head in range(8):
                for kv in range(2):
                    lane = head * 256 + kv * 128
                    for pair in range(4):
                        dest = (kv * 32 + g * 4 + pair) * 8 + head
                        out_ref[dest, k] = x_ref[
                            block, pl.ds(2 * pair, 2), pl.ds(lane, 128)
                        ]
        return carry

    lax.fori_loop(0, 8, step, 0)
    ctrl = ctrl_ref[...]

    def fill(d, carry):
        out_ref[d, 2] = ctrl
        return carry

    lax.fori_loop(0, 512, fill, 0, unroll=16)


def tables_kernel(own_ref, ctrl_ref, tab_ref, slot_ref):
    own = own_ref[0].astype(jnp.float32)
    ctrl = ctrl_ref[...].astype(jnp.float32)
    lane = lax.broadcasted_iota(jnp.int32, (64, 128), 1)
    lanef = lane.astype(jnp.float32)
    routes = [ctrl[:, l : l + 1] for l in range(16)]
    masks = [jnp.where(r == lanef, 1.0, 0.0) for r in routes]
    counts = functools.reduce(lambda a, b: a + b, masks)
    row = lax.broadcasted_iota(jnp.int32, (64, 64), 0)
    col = lax.broadcasted_iota(jnp.int32, (64, 64), 1)
    lower = jnp.where(col < row, 1.0, 0.0).astype(jnp.bfloat16)
    starts = jnp.dot(
        lower, counts.astype(jnp.bfloat16), preferred_element_type=jnp.float32
    )
    tab = jnp.zeros((64, 128), jnp.float32)
    slots = jnp.zeros((64, 128), jnp.float32)
    seen = jnp.zeros((64, 128), jnp.float32)
    for l in range(16):
        within = jnp.sum(masks[l] * seen, axis=1, keepdims=True)
        rank = jnp.sum(masks[l] * starts, axis=1, keepdims=True) + within
        seen = seen + masks[l]
        tab = jnp.where(lane == l, routes[l] * UNITS + rank, tab)
        tab = jnp.where(lane == 32 + l, within, tab)
        tab = jnp.where(lane == 48 + l, rank, tab)
        mine = (routes[l] == own) & (rank == lanef)
        slots = slots + jnp.where(mine, float(l), 0.0)
    own_lane = lanef == own
    first = jnp.sum(jnp.where(own_lane, starts, 0.0), axis=1, keepdims=True)
    tab = jnp.where(lane == 16, first, tab)
    tab_ref[...] = tab.astype(jnp.int32)
    locals_ = jnp.sum(slots, axis=0, keepdims=True)
    total = jnp.sum(jnp.where(own_lane, counts, 0.0))
    row8 = lax.broadcasted_iota(jnp.int32, (8, 128), 0)
    slot_ref[...] = jnp.where(row8 == 0, locals_, total).astype(jnp.int32)


def dispatch_kernel(own_ref, tab_ref, r_ref, back_ref, out_ref):
    g = lax.rem(own_ref[0] // 4, 8)

    def step(h, carry):
        for y in range(8):
            block = lax.rem(g - y + 8, 8)
            for k in range(2):
                out_ref[tab_ref[h, block + 8 * k]] = r_ref[h * 8 + y, k]
        first = tab_ref[h, 16]
        for s in range(2):
            slot = jnp.minimum(first + s, CTX - 1)
            for kv in range(2):
                out_ref[h * UNITS + CTX + 2 * s + kv] = back_ref[slot, kv]
        return carry

    lax.fori_loop(0, 64, step, 0)


def attention_kernel(
    total_ref, recv_ref, q_ref, f0_ref, f1_ref, i0_ref, i1_ref,
    cos_ref, sin_ref, kpos_ref, qpos_ref, out_ref, keys, vals,
):
    total = total_ref[0]
    cos = cos_ref[...]
    sin = sin_ref[...]
    pick0 = i0_ref[...]
    pick1 = i1_ref[...]
    live = lax.broadcasted_iota(jnp.int32, (64, 128), 0) < 2 * total
    k0 = f0_ref[:, :128].astype(jnp.float32)
    k1 = f1_ref[:, :128].astype(jnp.float32)
    v0 = f0_ref[:, 128:].astype(jnp.float32)
    v1 = f1_ref[:, 128:].astype(jnp.float32)
    for i in range(32):
        at0 = pick0 == i
        at1 = pick1 == i
        k = recv_ref[i, :CTX].reshape(64, 128).astype(jnp.float32)
        k = k * cos + pltpu.roll(k, 64, 1) * sin
        k = jnp.where(at0, k0, jnp.where(at1, k1, k))
        keys[i * 64 : i * 64 + 64, :] = k.astype(jnp.bfloat16)
        v = recv_ref[32 + i, :CTX].reshape(64, 128).astype(jnp.float32)
        v = jnp.where(at0, v0, jnp.where(at1, v1, v))
        v = jnp.where(live, v, 0.0)
        vals[i * 64 : i * 64 + 64, :] = v.astype(jnp.bfloat16)
    scale = 1.0 / math.sqrt(HD)
    allowed = kpos_ref[...] <= qpos_ref[...]
    rowlive = lax.broadcasted_iota(jnp.int32, (64, 128), 0) < 2 * total
    for head in range(QH):
        q = q_ref[:, head * HD : head * HD + HD]
        s = lax.dot_general(
            q, keys[...], (((1,), (1,)), ((), ())),
            preferred_element_type=jnp.float32,
        )
        s = jnp.where(allowed, s * scale, -1e30)
        peak = jnp.max(s, axis=1, keepdims=True)
        w = jnp.exp(s - peak)
        norm = jnp.sum(w, axis=1, keepdims=True)
        mixed = jnp.dot(
            w.astype(jnp.bfloat16), vals[...], preferred_element_type=jnp.float32
        )
        out = jnp.where(rowlive, mixed / norm, 0.0)
        out_ref[:, head * HD : head * HD + HD] = out.astype(jnp.bfloat16)


def update_kernel(pos_ref, x_ref, rows_ref, out_ref):
    row = lax.broadcasted_iota(jnp.int32, (8, 128), 0)

    def step(l, carry):
        at0 = row == pos_ref[2 * l]
        at1 = row == pos_ref[2 * l + 1]
        for head in range(8):
            for kv in range(2):
                lanes = pl.ds(head * 256 + kv * 128, 128)
                pairf = rows_ref[head, l, kv].astype(jnp.float32)
                old = x_ref[l, :, lanes].astype(jnp.float32)
                new = jnp.where(at0, pairf[0:1], jnp.where(at1, pairf[1:2], old))
                out_ref[l, :, lanes] = new.astype(jnp.bfloat16)
        return carry

    lax.fori_loop(0, 16, step, 0)


def local(kv_cache, route, queries, fresh_kv, picked):
    own = lax.axis_index("inst").astype(jnp.int32)
    y = lax.axis_index("tp").astype(jnp.int32)
    me = jnp.stack([own, y])
    bf = jnp.bfloat16
    ctrl = jnp.concatenate([route, picked.reshape(64)]).astype(bf)
    ctrl = jnp.pad(ctrl[None, :], ((0, 1), (0, 48)))
    spread = pl.pallas_call(
        spread_kernel,
        out_shape=jax.ShapeDtypeStruct((512, 3, 2, 128), bf),
        in_specs=[SMEM, VMEM, VMEM],
        out_specs=VMEM,
        compiler_params=PARAMS,
        name="spread",
    )(me, kv_cache, ctrl)
    got = lax.all_to_all(
        spread, ("inst", "tp"), split_axis=0, concat_axis=0, tiled=True
    )

    half = HD // 2
    freqs = jnp.power(
        jnp.float32(THETA), -2.0 * jnp.arange(half, dtype=jnp.float32) / HD
    )
    shift = (jnp.arange(64, dtype=jnp.int32) // 2 * 64).astype(jnp.float32)
    angle = shift[:, None] * freqs[None, :]
    cos = jnp.cos(angle)
    sin = jnp.sin(angle)
    cos2 = jnp.concatenate([cos, cos], axis=1)
    sin2 = jnp.concatenate([-sin, sin], axis=1)

    fk = fresh_kv[:, :HD].astype(jnp.float32)
    swapped = jnp.concatenate([fk[:, half:], fk[:, :half]], axis=1)
    back_k = (fk * cos2 - swapped * sin2).astype(bf)
    back = jnp.stack(
        [back_k.reshape(32, 2, HD), fresh_kv[:, HD:].reshape(32, 2, HD)], axis=1
    )

    every = got.reshape(64, 8, 3, 2, 128)[:, 0, 2, 0, :]
    tab, slot = pl.pallas_call(
        tables_kernel,
        out_shape=(
            jax.ShapeDtypeStruct((64, 128), jnp.int32),
            jax.ShapeDtypeStruct((8, 128), jnp.int32),
        ),
        in_specs=[SMEM, VMEM],
        out_specs=(VMEM, VMEM),
        compiler_params=PARAMS,
        name="tables",
    )(me, every)
    send = pl.pallas_call(
        dispatch_kernel,
        out_shape=jax.ShapeDtypeStruct((64 * UNITS, 2, 128), bf),
        in_specs=[SMEM, SMEM, VMEM, VMEM],
        out_specs=VMEM,
        compiler_params=PARAMS,
        name="dispatch",
    )(me, tab, got, back)
    recv = lax.all_to_all(
        send.reshape(64, UNITS, 2, 128), "inst", split_axis=0, concat_axis=0,
        tiled=True,
    )

    mine = lax.dynamic_index_in_dim(tab, own, 0, keepdims=False)
    block_exec = route
    within = mine[32:48]
    rank = mine[48:64]
    units = recv.reshape(64, UNITS // 2, 2, 2, 128)
    rows = units[block_exec, CTX // 2 + within]
    rows = jnp.broadcast_to(rows[None], (8,) + rows.shape)
    rows = lax.all_to_all(rows, "tp", split_axis=0, concat_axis=0, tiled=True)
    picks = every[:, 16:80].reshape(64, 32, 2).astype(jnp.int32)
    pos = picks[block_exec, rank].reshape(32) - 8 * y
    updated = pl.pallas_call(
        update_kernel,
        out_shape=jax.ShapeDtypeStruct(kv_cache.shape, bf),
        in_specs=[SMEM, VMEM, VMEM],
        out_specs=VMEM,
        compiler_params=PARAMS,
        name="update",
    )(pos, kv_cache, rows)

    total = slot[1, :1]
    lj = slot[0, :32]
    g = jnp.arange(8, dtype=jnp.int32)[:, None, None, None]
    pair = jnp.arange(4, dtype=jnp.int32)[None, :, None, None]
    j = jnp.arange(32, dtype=jnp.int32)[None, None, :, None]
    r2 = jnp.arange(2, dtype=jnp.int32)
    kpos = j * 64 + ((g - lj[:, None]) & 7) * 8 + pair * 2 + r2
    kpos = jnp.where(j < total[0], kpos, 1 << 20).reshape(1, 2048)
    qpos = (jnp.arange(32, dtype=jnp.int32)[:, None] * 64 + picked).reshape(64, 1)
    unit = ((picked // 8 + lj[:, None]) & 7) * 4 + (picked & 7) // 2
    hit = (picked & 1)[:, None, :] == r2[None, :, None]
    where = jnp.where(hit, unit[:, None, :], -1).reshape(64, 2)
    i0 = jnp.broadcast_to(where[:, 0:1], (64, 128))
    i1 = jnp.broadcast_to(where[:, 1:2], (64, 128))
    fr = fresh_kv.reshape(32, 2, 256)
    f0 = jnp.repeat(fr[:, 0], 2, axis=0)
    f1 = jnp.repeat(fr[:, 1], 2, axis=0)
    attn_out = pl.pallas_call(
        attention_kernel,
        out_shape=jax.ShapeDtypeStruct(queries.shape, bf),
        in_specs=[SMEM] + [VMEM] * 10,
        out_specs=VMEM,
        scratch_shapes=[
            pltpu.VMEM((2048, HD), bf),
            pltpu.VMEM((2048, HD), bf),
        ],
        compiler_params=PARAMS,
        cost_estimate=pl.CostEstimate(
            flops=4 * 384 * 2048 * 128, bytes_accessed=1500000,
            transcendentals=384 * 2048,
        ),
        name="attend",
    )(total, recv, queries, f0, f1, i0, i1, cos2, sin2, kpos, qpos)
    return attn_out, updated


def solution(mesh):
    placed = (P("inst", "tp", None), P("inst"), P("inst", "tp"), P("inst", "tp"), P("inst", None))
    return jax.shard_map(
        local,
        mesh=mesh,
        in_specs=placed,
        out_specs=(P("inst", "tp"), P("inst", "tp", None)),
        check_vma=False,
    )
```

time: 406 us -> 164 us (0.40)
  waiting for transfers between devices: 215 us -> 97.4 us
  local copies, waits for them, and re-layouts: 70 us -> 6.22 us
  blocking collectives: 29.8 us -> 0 us
  Pallas kernels: 0 us -> 18.2 us
  between operations: 15.7 us -> 0.91 us
  other arithmetic: 17.8 us -> 3.07 us
  loops' own time: 12.5 us -> 0 us
  matrix products: 4.3 us -> 0 us
    all_to_all x4 -> x3, waiting for transfers between devices: 185 us -> 97.4 us  [the longest x1 51.2 us: local(): lax.all_to_all(send.reshape(64, UNITS, 2, 128), 'inst', split_axis=0, con...]
    scatter x4 -> x0, local copies, waits for them, and re-layouts: 30.3 us -> none  [the longest x1 22.4 us: local(): kv_cache.at[target_block, jnp.clip(local_row, 0, block_rows - 1)]]
    unnamed x1 -> x0, blocking collectives: 29.8 us -> none
    all_gather x1 -> x0, waiting for transfers between devices: 28.6 us -> none  [local(): every_head = lax.all_gather(got_rows, 'tp', axis=2, tiled=True)]
    pallas_call x0 -> x5, Pallas kernels: none -> 18.2 us  [the longest x1 5.87 us: local(): pl.pallas_call(attention_kernel, out_shape=jax.ShapeDtypeStruct(queries.s...]
    all_to_all x4 -> x0, local copies, waits for them, and re-layouts: 15.9 us -> none  [the longest x1 7.48 us: local(): lax.all_to_all(lax.all_to_all(outgoing, 'inst', split_axis=0, concat_axis...]
    another operation x1 -> x0, loops' own time: 12.5 us -> none  [attend_heads(): return lax.map(one_head, jnp.arange(query_heads.shape[0], dtype=jnp.int32))]
    gather x3 -> x2, local copies, waits for them, and re-layouts: 6.28 us -> 1.24 us  [the longest x1 0.62 us: local(): pos = picks[block_exec, rank].reshape(32) - 8 * y]
  transfers between devices with their start and end apart: 5 -> 3, of which waited for: 4 -> 2; matrix products, arithmetic and copies ran while one was open for 12% -> 3% of each run, Pallas kernels for 0% -> 4%
where the time goes in v1:
time: 164 us; the launch traced here: 163 us
  waiting for transfers between devices  97.4 us (59%)
  starting transfers between devices  37.4 us (23%)
  Pallas kernels  18.2 us (11%)
  local copies, waits for them, and re-layouts  6.22 us (4%)
  other arithmetic  3.07 us (2%)
    all_to_all x1, waiting for transfers between devices, local(): lax.all_to_all(send.reshape(64, UNITS, 2, 128), 'inst', split_axis=0, con...  51.2 us
    all_to_all x1, waiting for transfers between devices, local(): lax.all_to_all(spread, ('inst', 'tp'), split_axis=0, concat_axis=0, tiled...  46.2 us
    all_to_all x1, starting transfers between devices, local(): lax.all_to_all(spread, ('inst', 'tp'), split_axis=0, concat_axis=0, tiled...  24.3 us
    all_to_all x1, starting transfers between devices, local(): rows = lax.all_to_all(rows, 'tp', split_axis=0, concat_axis=0, tiled=True)  8.32 us
    pallas_call x1, Pallas kernels, local(): pl.pallas_call(attention_kernel, out_shape=jax.ShapeDtypeStruct(queries.s...  5.87 us
    pallas_call x1, Pallas kernels, local(): pl.pallas_call(dispatch_kernel, out_shape=jax.ShapeDtypeStruct((64 * UNIT...  5.54 us
    all_to_all x1, starting transfers between devices, local(): lax.all_to_all(send.reshape(64, UNITS, 2, 128), 'inst', split_axis=0, con...  4.82 us
  transfers between devices with their start and end apart: 3, of which 2 were waited for; matrix products, arithmetic and copies ran while one was open for 3% of the time, Pallas kernels for 4%

profile of v1, /device:TPU:1, one launch (start us, length us, event | category | flops | bytes accessed | tf_op | source)
XLA Modules:
  0.0 163.2 jit_solution(12442140461999822323)
XLA Ops:
  0.6 0.8 broadcast_add_fusion.1
  1.4 0.1 copy.19
  1.5 0.1 concatenate.31
  1.6 0.7 convert_bitcast_fusion
  2.4 1.0 copy-done
  3.5 2.3 %spread.1 = bf16[512,3,2,128]{3,2,1,0:T(2,128)(2,1)} custom-call(s32[2]{0:T(128)S(1)} %pad_add_fusion.own_ref, bf16[16,8,2048]{2,1,0:T(8,128)(2,1)S(1)} %copy-done, bf16[2,128]{1,0:T(2,128)(2,1)S(1)} %fusion.9.ctrl_ref), custom_call_target="tpu_custom_call" | custom-call | tf_op jit(solution)/shard_map/spread/pallas_call | solution.py:171
  5.8 24.3 %all-to-all-start = ((bf16[512,3,2,128]{3,2,1,0:T(2,128)(2,1)}), bf16[512,3,2,128]{3,2,1,0:T(2,128)(2,1)S(1)}, u32[]{:S(2)}, u32[]{:S(2)}) async-start(bf16[512,3,2,128]{3,2,1,0:T(2,128)(2,1)} %spread.1), calls=%async_computation | async-start | bytes 1572864 | tf_op jit(solution)/shard_map/all_to_all | solution.py:179
  30.1 0.2 fusion.2
  30.4 0.1 fusion.1
  30.5 46.2 %all-to-all-done.r_ref = bf16[512,3,2,128]{3,2,1,0:T(2,128)(2,1)S(1)} async-done(((bf16[512,3,2,128]{3,2,1,0:T(2,128)(2,1)}), bf16[512,3,2,128]{3,2,1,0:T(2,128)(2,1)S(1)}, u32[]{:S(2)}, u32[]{:S(2)}) %all-to-all-start) | async-done | bytes 786464 | tf_op jit(solution)/shard_map/all_to_all | solution.py:179
  76.7 2.8 %tables.1 = (s32[64,128]{1,0:T(8,128)S(1)}, s32[8,128]{1,0:T(8,128)S(1)}) custom-call(s32[2]{0:T(128)S(1)} %pad_add_fusion.own_ref, bf16[64,128]{1,0:T(8,128)(2,1)S(1)} %bitcast.57), custom_call_target="tpu_custom_call" | custom-call | tf_op jit(solution)/shard_map/tables/pallas_call | solution.py:202
  79.5 5.5 %dispatch.1 = bf16[2304,2,128]{2,1,0:T(2,128)(2,1)} custom-call(s32[2]{0:T(128)S(1)} %pad_add_fusion.own_ref, s32[64,128]{1,0:T(8,128)S(1)} %get-tuple-element.5.tab_ref, bf16[512,3,2,128]{3,2,1,0:T(2,128)(2,1)S(1)} %all-to-all-done.r_ref, bf16[32,2,2,128]{3,2,1,0:T(2,128)(2,1)S(1)} %pad_maximum_fusion.2.back_ref), custom_call_target="tpu_custom_call" | custom-call | tf_op jit(solution)/shard_map/dispatch/pallas_call | solution.py:213
  85.0 4.8 %all-to-all-start.1 = ((bf16[64,36,2,128]{3,2,1,0:T(2,128)(2,1)}), bf16[64,36,2,128]{3,2,1,0:T(2,128)(2,1)S(1)}, u32[]{:S(2)}, u32[]{:S(2)}) async-start(bf16[64,36,2,128]{3,2,1,0:T(2,128)(2,1)} %bitcast.9), calls=%async_computation.1 | async-start | bytes 2359296 | tf_op jit(solution)/shard_map/all_to_all | solution.py:221
  90.0 0.1 eq.21
  90.1 0.1 eq.23
  90.4 0.1 copy.22
  90.6 0.1 slice_convert_fusion
  90.7 1.0 copy.25
  91.7 0.5 slice.47
  92.4 0.1 broadcast_in_dim.72
  92.5 0.1 or_bitcast_fusion
  92.6 0.6 gather_fusion
  93.2 0.6 iota_compare_fusion.1
  94.0 0.2 add_select_fusion
  94.2 51.2 %all-to-all-done.1.recv_ref = bf16[64,36,2,128]{3,2,1,0:T(2,128)(2,1)S(1)} async-done(((bf16[64,36,2,128]{3,2,1,0:T(2,128)(2,1)}), bf16[64,36,2,128]{3,2,1,0:T(2,128)(2,1)S(1)}, u32[]{:S(2)}, u32[]{:S(2)}) %all-to-all-start.1) | async-done | bytes 1179680 | tf_op jit(solution)/shard_map/all_to_all | solution.py:221
  145.4 0.6 gather_fusion.1
  146.0 0.7 broadcast_in_dim.81
  146.8 8.3 %all-to-all-start.2 = ((bf16[8,16,2,2,128]{4,3,2,1,0:T(2,128)(2,1)}), bf16[8,16,2,2,128]{4,3,2,1,0:T(2,128)(2,1)S(1)}, u32[]{:S(2)}, u32[]{:S(2)}) async-start(bf16[8,16,2,2,128]{4,3,2,1,0:T(2,128)(2,1)} %broadcast_in_dim.81), calls=%async_computation.2 | async-start | bytes 262144 | tf_op jit(solution)/shard_map/all_to_all | solution.py:233
  155.1 0.1 sub.60.pos_ref
  155.2 0.3 select_n.75.kpos_ref
  155.7 5.9 %attend.1 = bf16[64,768]{1,0:T(8,128)(2,1)} custom-call(s32[1]{0:T(128)} %bitcast.5.total_ref, bf16[64,36,2,128]{3,2,1,0:T(2,128)(2,1)S(1)} %all-to-all-done.1.recv_ref, bf16[64,768]{1,0:T(8,128)(2,1)S(1)} %copy-done.2, bf16[64,256]{1,0:T(8,128)(2,1)S(1)} %reshape.261.f0_ref, bf16[64,256]{1,0:T(8,128)(2,1)S(1)} %reshape.262.f1_ref, ...), custom_call_target="tpu_custom_call" | custom-call | flops 402653184 | bytes 1500000 | tf_op jit(solution)/shard_map/attend/pallas_call | solution.py:262
  161.5 1.7 %update.1 = bf16[16,8,2048]{2,1,0:T(8,128)(2,1)} custom-call(s32[32]{0:T(128)S(1)} %sub.60.pos_ref, bf16[16,8,2048]{2,1,0:T(8,128)(2,1)S(1)} %copy-done.1, bf16[8,16,2,2,128]{4,3,2,1,0:T(2,128)(2,1)S(1)} %all-to-all-done.2.rows_ref), custom_call_target="tpu_custom_call" | custom-call | tf_op jit(solution)/shard_map/update/pallas_call | solution.py:236
  (44 shorter events, 1.0 us)
Async XLA Ops:
  2.4 1.0 copy-start
  3.5 26.6 %copy-start.3 = (bf16[64,256]{1,0:T(8,128)(2,1)S(1)}, bf16[64,256]{1,0:T(8,128)(2,1)}, u32[]{:S(2)}) copy-start(bf16[64,256]{1,0:T(8,128)(2,1)} %param.8) | copy-start | bytes 98308
  5.8 70.9 %all-to-all-start = ((bf16[512,3,2,128]{3,2,1,0:T(2,128)(2,1)}), bf16[512,3,2,128]{3,2,1,0:T(2,128)(2,1)S(1)}, u32[]{:S(2)}, u32[]{:S(2)}) async-start(bf16[512,3,2,128]{3,2,1,0:T(2,128)(2,1)} %spread.1), calls=%async_computation | async-start | bytes 1572864 | tf_op jit(solution)/shard_map/all_to_all | solution.py:179
  85.0 60.4 %all-to-all-start.1 = ((bf16[64,36,2,128]{3,2,1,0:T(2,128)(2,1)}), bf16[64,36,2,128]{3,2,1,0:T(2,128)(2,1)S(1)}, u32[]{:S(2)}, u32[]{:S(2)}) async-start(bf16[64,36,2,128]{3,2,1,0:T(2,128)(2,1)} %bitcast.9), calls=%async_computation.1 | async-start | bytes 2359296 | tf_op jit(solution)/shard_map/all_to_all | solution.py:221
  89.9 2.4 %copy-start.4 = (s32[32,2]{0,1:T(2,128)S(1)}, s32[32,2]{0,1:T(2,128)}, u32[]{:S(2)}) copy-start(s32[32,2]{0,1:T(2,128)} %param.9) | copy-start | bytes 772
  89.9 2.6 %copy-start.5 = (s32[16]{0:T(128)S(1)}, s32[16]{0:T(128)}, u32[]{:S(2)}) copy-start(s32[16]{0:T(128)} %param.6) | copy-start | bytes 196
  91.7 63.9 %copy-start.2 = (bf16[64,768]{1,0:T(8,128)(2,1)S(1)}, bf16[64,768]{1,0:T(8,128)(2,1)}, u32[]{:S(2)}) copy-start(bf16[64,768]{1,0:T(8,128)(2,1)} %q_ref.1) | copy-start | bytes 294916
  146.8 14.8 %all-to-all-start.2 = ((bf16[8,16,2,2,128]{4,3,2,1,0:T(2,128)(2,1)}), bf16[8,16,2,2,128]{4,3,2,1,0:T(2,128)(2,1)S(1)}, u32[]{:S(2)}, u32[]{:S(2)}) async-start(bf16[8,16,2,2,128]{4,3,2,1,0:T(2,128)(2,1)} %broadcast_in_dim.81), calls=%async_computation.2 | async-start | bytes 262144 | tf_op jit(solution)/shard_map/all_to_all | solution.py:233
  155.1 6.4 %copy-start.1 = (bf16[16,8,2048]{2,1,0:T(8,128)(2,1)S(1)}, bf16[16,8,2048]{2,1,0:T(8,128)(2,1)}, u32[]{:S(2)}) copy-start(bf16[16,8,2048]{2,1,0:T(8,128)(2,1)} %x_ref.3) | copy-start | bytes 1572868

commit v2 on v1

v2 whole, which is shorter than its diff:
```python
import functools
import math

import jax
import jax.numpy as jnp
from jax import lax
from jax.experimental import pallas as pl
from jax.experimental.pallas import tpu as pltpu
from jax.sharding import PartitionSpec as P

HD = 128
QH = 6
THETA = 1000000.0
CTX = 32
UNITS = 36
VMEM = pl.BlockSpec(memory_space=pltpu.VMEM)
SMEM = pl.BlockSpec(memory_space=pltpu.SMEM)
PARAMS = pltpu.CompilerParams(vmem_limit_bytes=40 * 1024 * 1024)


def spread_kernel(x_ref, route_ref, picked_ref, out_ref):
    def step(block, carry):
        for head in range(8):
            for kv in range(2):
                lane = head * 256 + kv * 128
                for pair in range(4):
                    out_ref[head * 8 + kv * 4 + pair, block] = x_ref[
                        block, pl.ds(2 * pair, 2), pl.ds(lane, 128)
                    ]
        return carry

    lax.fori_loop(0, 16, step, 0)
    row = lax.broadcasted_iota(jnp.int32, (2, 128), 0)
    ctrl = jnp.where(row == 0, route_ref[...], picked_ref[...])
    ctrl = ctrl.astype(jnp.float32).astype(jnp.bfloat16)
    for d in range(64):
        out_ref[d, 16] = ctrl


def dispatch_kernel(own_ref, r_ref, back_ref, out_ref, tab_ref, tabs, sem):
    own = own_ref[0].astype(jnp.float32)
    ctrl = r_ref[:, 16, 0, :].astype(jnp.float32)
    lane = lax.broadcasted_iota(jnp.int32, (64, 128), 1)
    lanef = lane.astype(jnp.float32)
    routes = [ctrl[:, l : l + 1] for l in range(16)]
    masks = [jnp.where(r == lanef, 1.0, 0.0) for r in routes]
    counts = functools.reduce(lambda a, b: a + b, masks)
    row = lax.broadcasted_iota(jnp.int32, (64, 64), 0)
    col = lax.broadcasted_iota(jnp.int32, (64, 64), 1)
    lower = jnp.where(col < row, 1.0, 0.0).astype(jnp.bfloat16)
    starts = jnp.dot(
        lower, counts.astype(jnp.bfloat16), preferred_element_type=jnp.float32
    )
    tab = jnp.zeros((64, 128), jnp.float32)
    seen = jnp.zeros((64, 128), jnp.float32)
    for l in range(16):
        within = jnp.sum(masks[l] * seen, axis=1, keepdims=True)
        rank = jnp.sum(masks[l] * starts, axis=1, keepdims=True) + within
        seen = seen + masks[l]
        tab = jnp.where(lane == l, routes[l] * UNITS + rank, tab)
        tab = jnp.where(lane == 32 + l, within, tab)
        tab = jnp.where(lane == 48 + l, rank, tab)
    own_lane = lanef == own
    first = jnp.sum(jnp.where(own_lane, starts, 0.0), axis=1, keepdims=True)
    total = jnp.sum(jnp.where(own_lane, counts, 0.0))
    tab = jnp.where(lane == 16, first, tab)
    tab = jnp.where(lane == 17, total, tab)
    tab_ref[...] = tab.astype(jnp.int32)
    copy = pltpu.make_async_copy(tab_ref, tabs, sem)
    copy.start()
    copy.wait()

    def step(h, carry):
        place = [tabs[h, l] for l in range(16)]
        units = [r_ref[h, l] for l in range(16)]
        first = tabs[h, 16]
        slots = [jnp.minimum(first + s, CTX - 1) for s in range(2)]
        backs = [back_ref[slots[s], kv] for s in range(2) for kv in range(2)]
        for l in range(16):
            out_ref[place[l]] = units[l]
        for n in range(4):
            out_ref[h * UNITS + CTX + n] = backs[n]
        return carry

    lax.fori_loop(0, 64, step, 0, unroll=2)


def attention_kernel(
    total_ref, recv_ref, q_ref, f0_ref, f1_ref, i0_ref, i1_ref,
    cos_ref, sin_ref, qpos_ref, out_ref, keys, vals,
):
    total = total_ref[0]
    cos = cos_ref[...]
    sin = sin_ref[...]
    pick0 = i0_ref[...]
    pick1 = i1_ref[...]
    live = lax.broadcasted_iota(jnp.int32, (64, 128), 0) < 2 * total
    k0 = f0_ref[:, :128].astype(jnp.float32)
    k1 = f1_ref[:, :128].astype(jnp.float32)
    v0 = f0_ref[:, 128:].astype(jnp.float32)
    v1 = f1_ref[:, 128:].astype(jnp.float32)
    for i in range(32):
        at0 = pick0 == i
        at1 = pick1 == i
        src = i // 4 * 8 + i % 4
        k = recv_ref[src, : 2 * CTX, :].astype(jnp.float32)
        k = k * cos + pltpu.roll(k, 64, 1) * sin
        k = jnp.where(at0, k0, jnp.where(at1, k1, k))
        keys[i * 64 : i * 64 + 64, :] = k.astype(jnp.bfloat16)
        v = recv_ref[src + 4, : 2 * CTX, :].astype(jnp.float32)
        v = jnp.where(at0, v0, jnp.where(at1, v1, v))
        v = jnp.where(live, v, 0.0)
        vals[i * 64 : i * 64 + 64, :] = v.astype(jnp.bfloat16)
    scale = 1.0 / math.sqrt(HD)
    col = lax.broadcasted_iota(jnp.int32, (64, 2048), 1)
    kpos = (col & 63) // 2 * 64 + (col >> 6) * 2 + (col & 1)
    allowed = (kpos <= qpos_ref[...]) & (kpos < total * 64)
    rowlive = lax.broadcasted_iota(jnp.int32, (64, 128), 0) < 2 * total
    for head in range(QH):
        q = q_ref[:, head * HD : head * HD + HD]
        s = lax.dot_general(
            q, keys[...], (((1,), (1,)), ((), ())),
            preferred_element_type=jnp.float32,
        )
        s = jnp.where(allowed, s * scale, -1e30)
        peak = jnp.max(s, axis=1, keepdims=True)
        w = jnp.exp(s - peak)
        norm = jnp.sum(w, axis=1, keepdims=True)
        mixed = jnp.dot(
            w.astype(jnp.bfloat16), vals[...], preferred_element_type=jnp.float32
        )
        out = jnp.where(rowlive, mixed / norm, 0.0)
        out_ref[:, head * HD : head * HD + HD] = out.astype(jnp.bfloat16)


def update_kernel(pos_ref, x_ref, rows_ref, out_ref):
    row = lax.broadcasted_iota(jnp.int32, (8, 128), 0)

    def step(l, carry):
        at0 = row == pos_ref[2 * l]
        at1 = row == pos_ref[2 * l + 1]
        for head in range(8):
            for kv in range(2):
                lanes = pl.ds(head * 256 + kv * 128, 128)
                pairf = rows_ref[head, l, kv].astype(jnp.float32)
                old = x_ref[l, :, lanes].astype(jnp.float32)
                new = jnp.where(at0, pairf[0:1], jnp.where(at1, pairf[1:2], old))
                out_ref[l, :, lanes] = new.astype(jnp.bfloat16)
        return carry

    lax.fori_loop(0, 16, step, 0)


def local(kv_cache, route, queries, fresh_kv, picked):
    own = lax.axis_index("inst").astype(jnp.int32)
    y = lax.axis_index("tp").astype(jnp.int32)
    bf = jnp.bfloat16
    spread = pl.pallas_call(
        spread_kernel,
        out_shape=jax.ShapeDtypeStruct((64, 17, 2, 128), bf),
        in_specs=[VMEM, VMEM, VMEM],
        out_specs=VMEM,
        compiler_params=PARAMS,
        name="spread",
    )(
        kv_cache,
        jnp.pad(route, (0, 112))[None, :],
        jnp.pad(picked.reshape(64), (0, 64))[None, :],
    )
    got = lax.all_to_all(spread, "tp", split_axis=0, concat_axis=0, tiled=True)
    got = lax.all_to_all(got, "inst", split_axis=0, concat_axis=0, tiled=True)

    half = HD // 2
    freqs = jnp.power(
        jnp.float32(THETA), -2.0 * jnp.arange(half, dtype=jnp.float32) / HD
    )
    shift = (jnp.arange(64, dtype=jnp.int32) // 2 * 64).astype(jnp.float32)
    angle = shift[:, None] * freqs[None, :]
    cos = jnp.cos(angle)
    sin = jnp.sin(angle)
    cos2 = jnp.concatenate([cos, cos], axis=1)
    sin2 = jnp.concatenate([-sin, sin], axis=1)

    fk = fresh_kv[:, :HD].astype(jnp.float32)
    swapped = jnp.concatenate([fk[:, half:], fk[:, :half]], axis=1)
    back_k = (fk * cos2 - swapped * sin2).astype(bf)
    back = jnp.stack(
        [back_k.reshape(32, 2, HD), fresh_kv[:, HD:].reshape(32, 2, HD)], axis=1
    )

    send, tab = pl.pallas_call(
        dispatch_kernel,
        out_shape=(
            jax.ShapeDtypeStruct((64 * UNITS, 2, 128), bf),
            jax.ShapeDtypeStruct((64, 128), jnp.int32),
        ),
        in_specs=[SMEM, VMEM, VMEM],
        out_specs=(VMEM, VMEM),
        scratch_shapes=[pltpu.SMEM((64, 128), jnp.int32), pltpu.SemaphoreType.DMA],
        compiler_params=PARAMS,
        name="dispatch",
    )(own[None], got, back)
    recv = lax.all_to_all(
        send.reshape(64, UNITS, 2, 128), "inst", split_axis=0, concat_axis=0,
        tiled=True,
    )

    mine = lax.dynamic_index_in_dim(tab, own, 0, keepdims=False)
    units = recv.reshape(64, UNITS // 2, 2, 2, 128)
    rows = units[route, CTX // 2 + mine[32:48]]
    rows = jnp.broadcast_to(rows[None], (8,) + rows.shape)
    rows = lax.all_to_all(rows, "tp", split_axis=0, concat_axis=0, tiled=True)
    picks = got[:, 16, 1, :64].reshape(64, 32, 2).astype(jnp.int32)
    pos = picks[route, mine[48:64]].reshape(32) - 8 * y
    updated = pl.pallas_call(
        update_kernel,
        out_shape=jax.ShapeDtypeStruct(kv_cache.shape, bf),
        in_specs=[SMEM, VMEM, VMEM],
        out_specs=VMEM,
        compiler_params=PARAMS,
        name="update",
    )(pos, kv_cache, rows)

    r2 = jnp.arange(2, dtype=jnp.int32)
    qpos = (jnp.arange(32, dtype=jnp.int32)[:, None] * 64 + picked).reshape(64, 1)
    hit = (picked & 1)[:, None, :] == r2[None, :, None]
    where = jnp.where(hit, (picked // 2)[:, None, :], -1).reshape(64, 2)
    i0 = jnp.broadcast_to(where[:, 0:1], (64, 128))
    i1 = jnp.broadcast_to(where[:, 1:2], (64, 128))
    fr = fresh_kv.reshape(32, 2, 256)
    f0 = jnp.repeat(fr[:, 0], 2, axis=0)
    f1 = jnp.repeat(fr[:, 1], 2, axis=0)
    attn_out = pl.pallas_call(
        attention_kernel,
        out_shape=jax.ShapeDtypeStruct(queries.shape, bf),
        in_specs=[SMEM] + [VMEM] * 9,
        out_specs=VMEM,
        scratch_shapes=[
            pltpu.VMEM((2048, HD), bf),
            pltpu.VMEM((2048, HD), bf),
        ],
        compiler_params=PARAMS,
        cost_estimate=pl.CostEstimate(
            flops=4 * 384 * 2048 * 128, bytes_accessed=1500000,
            transcendentals=384 * 2048,
        ),
        name="attend",
    )(
        mine[17:18], recv.reshape(64, 2 * UNITS, 128), queries, f0, f1, i0, i1,
        cos2, sin2, qpos,
    )
    return attn_out, updated


def solution(mesh):
    placed = (P("inst", "tp", None), P("inst"), P("inst", "tp"), P("inst", "tp"), P("inst", None))
    return jax.shard_map(
        local,
        mesh=mesh,
        in_specs=placed,
        out_specs=(P("inst", "tp"), P("inst", "tp", None)),
        check_vma=False,
    )
```

time: 164 us -> 156 us (0.951)
  blocking collectives: 0 us -> 20.1 us
  waiting for transfers between devices: 97.4 us -> 82.8 us
  Pallas kernels: 18.2 us -> 12.4 us
  starting transfers between devices: 37.4 us -> 31.6 us
  other arithmetic: 3.07 us -> 0.53 us
    all_to_all x0 -> x1, blocking collectives: none -> 20.1 us  [local(): got = lax.all_to_all(spread, 'tp', split_axis=0, concat_axis=0, tiled=True)]
    all_to_all x1, waiting for transfers between devices: 46.2 us -> 30.2 us  [local(): got = lax.all_to_all(got, 'inst', split_axis=0, concat_axis=0, tiled=True)]
    all_to_all x1, starting transfers between devices: 24.3 us -> 14.2 us  [local(): got = lax.all_to_all(got, 'inst', split_axis=0, concat_axis=0, tiled=True)]
    pallas_call x3 -> x2, Pallas kernels: 10.6 us -> 5.95 us  [the longest x1 5.27 us: local(): pl.pallas_call(dispatch_kernel, out_shape=(jax.ShapeDtypeStruct((64 * UNI...]
    all_to_all x1, starting transfers between devices: 4.82 us -> 8.85 us  [local(): lax.all_to_all(send.reshape(64, UNITS, 2, 128), 'inst', split_axis=0, con...]
  transfers between devices with their start and end apart: 3 -> 3, of which waited for: 2 -> 2; matrix products, arithmetic and copies ran while one was open for 3% -> 2% of each run, Pallas kernels for 4% -> 3%
where the time goes in v2:
time: 156 us
  waiting for transfers between devices  82.8 us (53%)
  starting transfers between devices  31.6 us (20%)
  blocking collectives  20.1 us (13%)
  Pallas kernels  12.4 us (8%)
  local copies, waits for them, and re-layouts  7.24 us (5%)
    all_to_all x1, waiting for transfers between devices, local(): lax.all_to_all(send.reshape(64, UNITS, 2, 128), 'inst', split_axis=0, con...  52.6 us
    all_to_all x1, waiting for transfers between devices, local(): got = lax.all_to_all(got, 'inst', split_axis=0, concat_axis=0, tiled=True)  30.2 us
    all_to_all x1, blocking collectives, local(): got = lax.all_to_all(spread, 'tp', split_axis=0, concat_axis=0, tiled=True)  20.1 us
    all_to_all x1, starting transfers between devices, local(): got = lax.all_to_all(got, 'inst', split_axis=0, concat_axis=0, tiled=True)  14.2 us
    all_to_all x1, starting transfers between devices, local(): lax.all_to_all(send.reshape(64, UNITS, 2, 128), 'inst', split_axis=0, con...  8.85 us
    all_to_all x1, starting transfers between devices, local(): rows = lax.all_to_all(rows, 'tp', split_axis=0, concat_axis=0, tiled=True)  8.51 us
    pallas_call x1, Pallas kernels, local(): pl.pallas_call(dispatch_kernel, out_shape=(jax.ShapeDtypeStruct((64 * UNI...  5.27 us
    pallas_call x1, Pallas kernels, local(): pl.pallas_call(attention_kernel, out_shape=jax.ShapeDtypeStruct(queries.s...  4.82 us
  transfers between devices with their start and end apart: 3, of which 2 were waited for; matrix products, arithmetic and copies ran while one was open for 2% of the time, Pallas kernels for 3%

profile of v2, /device:TPU:1, one launch (start us, length us, event | category | flops | bytes accessed | tf_op | source)
XLA Modules:
  0.0 155.6 jit_solution(5219924730973264956)
XLA Ops:
  0.6 0.8 copy.23
  1.4 0.1 reshape.125
  1.5 0.7 pad_bitcast_fusion
  2.2 1.0 copy-done
  3.2 0.7 spread.1
  3.9 20.1 %all_to_all.20 = bf16[64,17,2,128]{3,2,1,0:T(2,128)(2,1)} all-to-all(bf16[64,17,2,128]{3,2,1,0:T(2,128)(2,1)S(1)} %spread.1), channel_id=1, replica_groups=mesh['inst'=64,'tp'=8] {'tp'}, dimensions={0} | all-to-all | bytes 1114112 | tf_op jit(solution)/shard_map/all_to_all | solution.py:170
  24.0 14.2 %all-to-all-start.1 = ((bf16[64,17,2,128]{3,2,1,0:T(2,128)(2,1)}), bf16[64,17,2,128]{3,2,1,0:T(2,128)(2,1)S(1)}, u32[]{:S(2)}, u32[]{:S(2)}) async-start(bf16[64,17,2,128]{3,2,1,0:T(2,128)(2,1)} %all_to_all.20), calls=%async_computation.1 | async-start | bytes 1114112 | tf_op jit(solution)/shard_map/all_to_all | solution.py:171
  38.3 0.2 fusion.2
  38.5 0.1 fusion.1
  38.7 30.2 %all-to-all-done.1.r_ref = bf16[64,17,2,128]{3,2,1,0:T(2,128)(2,1)S(1)} async-done(((bf16[64,17,2,128]{3,2,1,0:T(2,128)(2,1)}), bf16[64,17,2,128]{3,2,1,0:T(2,128)(2,1)S(1)}, u32[]{:S(2)}, u32[]{:S(2)}) %all-to-all-start.1) | async-done | bytes 557088 | tf_op jit(solution)/shard_map/all_to_all | solution.py:171
  68.8 5.3 %dispatch.1 = (bf16[2304,2,128]{2,1,0:T(2,128)(2,1)}, s32[64,128]{1,0:T(8,128)S(1)}) custom-call(s32[1]{0:T(128)} %bitcast.own_ref, bf16[64,17,2,128]{3,2,1,0:T(2,128)(2,1)S(1)} %all-to-all-done.1.r_ref, bf16[32,2,2,128]{3,2,1,0:T(2,128)(2,1)S(1)} %pad_maximum_fusion.2.back_ref), custom_call_target="tpu_custom_call" | custom-call | tf_op jit(solution)/shard_map/dispatch/pallas_call | solution.py:191
  74.1 8.9 %all-to-all-start.2 = ((bf16[64,36,2,128]{3,2,1,0:T(2,128)(2,1)}), bf16[64,36,2,128]{3,2,1,0:T(2,128)(2,1)S(1)}, u32[]{:S(2)}, u32[]{:S(2)}) async-start(bf16[64,36,2,128]{3,2,1,0:T(2,128)(2,1)} %bitcast.7), calls=%async_computation.2 | async-start | bytes 2359296 | tf_op jit(solution)/shard_map/all_to_all | solution.py:203
  83.1 0.1 copy.25
  83.2 0.1 reshape.151.qpos_ref
  83.2 0.1 eq.23
  83.3 0.1 eq.20
  83.4 0.1 eq.21
  83.5 0.1 broadcast_in_dim.66
  83.6 0.1 broadcast_in_dim.67
  84.0 0.1 copy.27
  84.1 1.0 copy.28
  85.1 0.1 or_bitcast_fusion
  85.2 0.6 gather_fusion
  85.8 52.6 %all-to-all-done.2 = bf16[64,36,2,128]{3,2,1,0:T(2,128)(2,1)S(1)} async-done(((bf16[64,36,2,128]{3,2,1,0:T(2,128)(2,1)}), bf16[64,36,2,128]{3,2,1,0:T(2,128)(2,1)S(1)}, u32[]{:S(2)}, u32[]{:S(2)}) %all-to-all-start.2) | async-done | bytes 1179680 | tf_op jit(solution)/shard_map/all_to_all | solution.py:203
  138.4 0.6 gather_fusion.1
  139.0 0.7 broadcast_in_dim.74
  139.8 8.5 %all-to-all-start.3 = ((bf16[8,16,2,2,128]{4,3,2,1,0:T(2,128)(2,1)}), bf16[8,16,2,2,128]{4,3,2,1,0:T(2,128)(2,1)S(1)}, u32[]{:S(2)}, u32[]{:S(2)}) async-start(bf16[8,16,2,2,128]{4,3,2,1,0:T(2,128)(2,1)} %broadcast_in_dim.74), calls=%async_computation.3 | async-start | bytes 262144 | tf_op jit(solution)/shard_map/all_to_all | solution.py:212
  148.3 0.6 slice.47
  148.9 0.1 sub.34.pos_ref
  149.0 0.1 broadcast_in_dim.72.i1_ref
  149.1 4.8 %attend.1 = bf16[64,768]{1,0:T(8,128)(2,1)} custom-call(s32[1]{0:T(128)} %bitcast.6.total_ref, bf16[64,72,128]{2,1,0:T(8,128)(2,1)S(1)} %bitcast.49, bf16[64,768]{1,0:T(8,128)(2,1)S(1)} %copy-done.2, bf16[64,256]{1,0:T(8,128)(2,1)S(1)} %reshape.129.f0_ref, bf16[64,256]{1,0:T(8,128)(2,1)S(1)} %reshape.130.f1_ref, s32[64,128]{1,0:T(8,128)S(1)} %broadcast_in_dim.70.i0_ref, ...), custom_call_target="tpu_custom_call" | custom-call | flops 402653184 | bytes 1500000 | tf_op jit(solution)/shard_map/attend/pallas_call | solution.py:233
  153.9 1.7 %update.1 = bf16[16,8,2048]{2,1,0:T(8,128)(2,1)} custom-call(s32[32]{0:T(128)S(1)} %sub.34.pos_ref, bf16[16,8,2048]{2,1,0:T(8,128)(2,1)S(1)} %copy-done.1, bf16[8,16,2,2,128]{4,3,2,1,0:T(2,128)(2,1)S(1)} %all-to-all-done.3.rows_ref), custom_call_target="tpu_custom_call" | custom-call | tf_op jit(solution)/shard_map/update/pallas_call | solution.py:215
  (32 shorter events, 0.4 us)
Async XLA Ops:
  2.2 1.0 copy-start
  3.9 34.4 %copy-start.3 = (bf16[64,256]{1,0:T(8,128)(2,1)S(1)}, bf16[64,256]{1,0:T(8,128)(2,1)}, u32[]{:S(2)}) copy-start(bf16[64,256]{1,0:T(8,128)(2,1)} %param.8) | copy-start | bytes 98308
  24.0 44.8 %all-to-all-start.1 = ((bf16[64,17,2,128]{3,2,1,0:T(2,128)(2,1)}), bf16[64,17,2,128]{3,2,1,0:T(2,128)(2,1)S(1)}, u32[]{:S(2)}, u32[]{:S(2)}) async-start(bf16[64,17,2,128]{3,2,1,0:T(2,128)(2,1)} %all_to_all.20), calls=%async_computation.1 | async-start | bytes 1114112 | tf_op jit(solution)/shard_map/all_to_all | solution.py:171
  74.1 8.9 %copy-start.4 = (s32[32,2]{0,1:T(2,128)S(1)}, s32[32,2]{0,1:T(2,128)}, u32[]{:S(2)}) copy-start(s32[32,2]{0,1:T(2,128)} %param.9) | copy-start | bytes 772
  74.1 64.3 %all-to-all-start.2 = ((bf16[64,36,2,128]{3,2,1,0:T(2,128)(2,1)}), bf16[64,36,2,128]{3,2,1,0:T(2,128)(2,1)S(1)}, u32[]{:S(2)}, u32[]{:S(2)}) async-start(bf16[64,36,2,128]{3,2,1,0:T(2,128)(2,1)} %bitcast.7), calls=%async_computation.2 | async-start | bytes 2359296 | tf_op jit(solution)/shard_map/all_to_all | solution.py:203
  83.0 2.1 %copy-start.5 = (s32[16]{0:T(128)S(1)}, s32[16]{0:T(128)}, u32[]{:S(2)}) copy-start(s32[16]{0:T(128)} %param.6) | copy-start | bytes 196
  83.6 65.5 %copy-start.2 = (bf16[64,768]{1,0:T(8,128)(2,1)S(1)}, bf16[64,768]{1,0:T(8,128)(2,1)}, u32[]{:S(2)}) copy-start(bf16[64,768]{1,0:T(8,128)(2,1)} %q_ref.1) | copy-start | bytes 294916
  85.1 68.9 %copy-start.1 = (bf16[16,8,2048]{2,1,0:T(8,128)(2,1)S(1)}, bf16[16,8,2048]{2,1,0:T(8,128)(2,1)}, u32[]{:S(2)}) copy-start(bf16[16,8,2048]{2,1,0:T(8,128)(2,1)} %x_ref.3) | copy-start | bytes 1572868
  139.8 14.2 %all-to-all-start.3 = ((bf16[8,16,2,2,128]{4,3,2,1,0:T(2,128)(2,1)}), bf16[8,16,2,2,128]{4,3,2,1,0:T(2,128)(2,1)S(1)}, u32[]{:S(2)}, u32[]{:S(2)}) async-start(bf16[8,16,2,2,128]{4,3,2,1,0:T(2,128)(2,1)} %broadcast_in_dim.74), calls=%async_computation.3 | async-start | bytes 262144 | tf_op jit(solution)/shard_map/all_to_all | solution.py:212

commit v3 on v2

--- a/solution.py
+++ b/solution.py
@@ -15,10 +15,34 @@
 UNITS = 36
 VMEM = pl.BlockSpec(memory_space=pltpu.VMEM)
 SMEM = pl.BlockSpec(memory_space=pltpu.SMEM)
+DISPATCH_SCRATCH = [
+    pltpu.VMEM((24, 128), jnp.int32),
+    pltpu.SMEM((24, 128), jnp.int32),
+    pltpu.SemaphoreType.DMA,
+]
+ATTEND_SCRATCH = [
+    pltpu.VMEM((2048, HD), jnp.bfloat16),
+    pltpu.VMEM((2048, HD), jnp.bfloat16),
+]
 PARAMS = pltpu.CompilerParams(vmem_limit_bytes=40 * 1024 * 1024)
 
 
 def spread_kernel(x_ref, route_ref, picked_ref, out_ref):
+    lane = lax.broadcasted_iota(jnp.int32, (8, 128), 1)
+    ctrl = jnp.zeros((8, 128), jnp.int32)
+    picks = jnp.zeros((8, 128), jnp.int32)
+    for l in range(16):
+        ctrl = jnp.where(lane == l, route_ref[l], ctrl)
+        ctrl = ctrl + jnp.where(lane == 64 + route_ref[l], 1, 0)
+    for j in range(32):
+        for w in range(2):
+            picks = jnp.where(lane == 2 * j + w, picked_ref[j, w], picks)
+    row = lax.broadcasted_iota(jnp.int32, (8, 128), 0)
+    ctrl = jnp.where(row == 0, ctrl, picks)[:2]
+    ctrl = ctrl.astype(jnp.float32).astype(jnp.bfloat16)
+    for d in range(64):
+        out_ref[d, 16] = ctrl
+
     def step(block, carry):
         for head in range(8):
             for kv in range(2):
@@ -30,66 +54,76 @@
         return carry
 
     lax.fori_loop(0, 16, step, 0)
-    row = lax.broadcasted_iota(jnp.int32, (2, 128), 0)
-    ctrl = jnp.where(row == 0, route_ref[...], picked_ref[...])
-    ctrl = ctrl.astype(jnp.float32).astype(jnp.bfloat16)
-    for d in range(64):
-        out_ref[d, 16] = ctrl
-
-
-def dispatch_kernel(own_ref, r_ref, back_ref, out_ref, tab_ref, tabs, sem):
-    own = own_ref[0].astype(jnp.float32)
+
+
+def dispatch_kernel(own_ref, r_ref, back_ref, out_ref, tab_ref, info_ref, packed, tabs, sem):
+    own = own_ref[0]
     ctrl = r_ref[:, 16, 0, :].astype(jnp.float32)
     lane = lax.broadcasted_iota(jnp.int32, (64, 128), 1)
-    lanef = lane.astype(jnp.float32)
-    routes = [ctrl[:, l : l + 1] for l in range(16)]
-    masks = [jnp.where(r == lanef, 1.0, 0.0) for r in routes]
-    counts = functools.reduce(lambda a, b: a + b, masks)
+    counts = pltpu.roll(ctrl, 64, 1)
     row = lax.broadcasted_iota(jnp.int32, (64, 64), 0)
     col = lax.broadcasted_iota(jnp.int32, (64, 64), 1)
     lower = jnp.where(col < row, 1.0, 0.0).astype(jnp.bfloat16)
     starts = jnp.dot(
         lower, counts.astype(jnp.bfloat16), preferred_element_type=jnp.float32
-    )
-    tab = jnp.zeros((64, 128), jnp.float32)
-    seen = jnp.zeros((64, 128), jnp.float32)
-    for l in range(16):
-        within = jnp.sum(masks[l] * seen, axis=1, keepdims=True)
-        rank = jnp.sum(masks[l] * starts, axis=1, keepdims=True) + within
-        seen = seen + masks[l]
-        tab = jnp.where(lane == l, routes[l] * UNITS + rank, tab)
-        tab = jnp.where(lane == 32 + l, within, tab)
-        tab = jnp.where(lane == 48 + l, rank, tab)
-    own_lane = lanef == own
-    first = jnp.sum(jnp.where(own_lane, starts, 0.0), axis=1, keepdims=True)
-    total = jnp.sum(jnp.where(own_lane, counts, 0.0))
-    tab = jnp.where(lane == 16, first, tab)
-    tab = jnp.where(lane == 17, total, tab)
-    tab_ref[...] = tab.astype(jnp.int32)
-    copy = pltpu.make_async_copy(tab_ref, tabs, sem)
+    ).astype(jnp.int32)
+    routes = jnp.where(lane < 16, ctrl, 0.0).astype(jnp.int32)
+    within = jnp.zeros((64, 128), jnp.int32)
+    for d in range(1, 16):
+        same = (pltpu.roll(ctrl, d, 1) == ctrl) & (lane >= d)
+        within = within + jnp.where(same, 1, 0)
+    slot = jnp.take_along_axis(starts, routes, axis=1) + within
+    place = routes * UNITS + slot
+    ret = routes * UNITS + CTX + 2 * within
+    tab_ref[...] = jnp.where(lane < 16, within, pltpu.roll(slot, 16, 1))
+    own_lane = lane == own
+    first = jnp.sum(jnp.where(own_lane, starts, 0), axis=1, keepdims=True)
+    lane8 = lax.broadcasted_iota(jnp.int32, (8, 128), 1)
+    for n, table in enumerate((place, ret, jnp.broadcast_to(first, (64, 128)))):
+        acc = jnp.zeros((8, 128), jnp.int32)
+        for a in range(8):
+            part = table[8 * a : 8 * a + 8]
+            if a:
+                part = pltpu.roll(part, 16 * a, 1)
+            acc = jnp.where(lane8 // 16 == a, part, acc)
+        packed[8 * n : 8 * n + 8] = acc
+    copy = pltpu.make_async_copy(packed, tabs, sem)
     copy.start()
     copy.wait()
 
-    def step(h, carry):
-        place = [tabs[h, l] for l in range(16)]
-        units = [r_ref[h, l] for l in range(16)]
-        first = tabs[h, 16]
-        slots = [jnp.minimum(first + s, CTX - 1) for s in range(2)]
-        backs = [back_ref[slots[s], kv] for s in range(2) for kv in range(2)]
-        for l in range(16):
-            out_ref[place[l]] = units[l]
-        for n in range(4):
-            out_ref[h * UNITS + CTX + n] = backs[n]
+    def step(a, carry):
+        for r in range(8):
+            h = a * 8 + r
+            place = [tabs[r, a * 16 + l] for l in range(16)]
+            units = [r_ref[h, l] for l in range(16)]
+            first = tabs[16 + r, a * 16]
+            slots = [jnp.minimum(first + s, CTX - 1) for s in range(2)]
+            backs = [back_ref[slots[s], kv] for s in range(2) for kv in range(2)]
+            for l in range(16):
+                out_ref[place[l]] = units[l]
+            for n in range(4):
+                out_ref[h * UNITS + CTX + n] = backs[n]
         return carry
 
-    lax.fori_loop(0, 64, step, 0, unroll=2)
+    lax.fori_loop(0, 8, step, 0)
+    for l in range(16):
+        info_ref[l] = tabs[8 + lax.rem(own, 8), own // 8 * 16 + l]
+    info_ref[16] = jnp.sum(jnp.where(own_lane, counts, 0.0)).astype(jnp.int32)
+
+
+def collect_kernel(info_ref, recv_ref, out_ref):
+    for l in range(16):
+        for kv in range(2):
+            unit = recv_ref[info_ref[l] + kv]
+            for t in range(8):
+                out_ref[t * 32 + l * 2 + kv] = unit
 
 
 def attention_kernel(
-    total_ref, recv_ref, q_ref, f0_ref, f1_ref, i0_ref, i1_ref,
+    info_ref, recv_ref, q_ref, f0_ref, f1_ref, i0_ref, i1_ref,
     cos_ref, sin_ref, qpos_ref, out_ref, keys, vals,
 ):
-    total = total_ref[0]
+    total = info_ref[16]
     cos = cos_ref[...]
     sin = sin_ref[...]
     pick0 = i0_ref[...]
@@ -111,26 +145,30 @@
         v = jnp.where(at0, v0, jnp.where(at1, v1, v))
         v = jnp.where(live, v, 0.0)
         vals[i * 64 : i * 64 + 64, :] = v.astype(jnp.bfloat16)
-    scale = 1.0 / math.sqrt(HD)
     col = lax.broadcasted_iota(jnp.int32, (64, 2048), 1)
     kpos = (col & 63) // 2 * 64 + (col >> 6) * 2 + (col & 1)
     allowed = (kpos <= qpos_ref[...]) & (kpos < total * 64)
     rowlive = lax.broadcasted_iota(jnp.int32, (64, 128), 0) < 2 * total
-    for head in range(QH):
-        q = q_ref[:, head * HD : head * HD + HD]
+    factor = math.log2(math.e) / math.sqrt(HD)
+    group = 3
+    for base in range(0, QH, group):
+        heads = range(base, base + group)
+        q = jnp.concatenate([q_ref[:, h * HD : h * HD + HD] for h in heads], axis=0)
         s = lax.dot_general(
             q, keys[...], (((1,), (1,)), ((), ())),
             preferred_element_type=jnp.float32,
         )
-        s = jnp.where(allowed, s * scale, -1e30)
-        peak = jnp.max(s, axis=1, keepdims=True)
-        w = jnp.exp(s - peak)
-        norm = jnp.sum(w, axis=1, keepdims=True)
+        s = jnp.where(allowed[None], s.reshape(group, 64, 2048), -1e30)
+        peak = jnp.max(s, axis=2, keepdims=True)
+        w = jnp.exp2((s - peak) * factor)
+        norm = jnp.sum(w, axis=2, keepdims=True)
         mixed = jnp.dot(
-            w.astype(jnp.bfloat16), vals[...], preferred_element_type=jnp.float32
-        )
-        out = jnp.where(rowlive, mixed / norm, 0.0)
-        out_ref[:, head * HD : head * HD + HD] = out.astype(jnp.bfloat16)
+            w.astype(jnp.bfloat16).reshape(group * 64, 2048), vals[...],
+            preferred_element_type=jnp.float32,
+        ).reshape(group, 64, HD)
+        out = jnp.where(rowlive[None], mixed / norm, 0.0)
+        for n, h in enumerate(heads):
+            out_ref[:, h * HD : h * HD + HD] = out[n].astype(jnp.bfloat16)
 
 
 def update_kernel(pos_ref, x_ref, rows_ref, out_ref):
@@ -158,15 +196,11 @@
     spread = pl.pallas_call(
         spread_kernel,
         out_shape=jax.ShapeDtypeStruct((64, 17, 2, 128), bf),
-        in_specs=[VMEM, VMEM, VMEM],
+        in_specs=[VMEM, SMEM, SMEM],
         out_specs=VMEM,
         compiler_params=PARAMS,
         name="spread",
-    )(
-        kv_cache,
-        jnp.pad(route, (0, 112))[None, :],
-        jnp.pad(picked.reshape(64), (0, 64))[None, :],
-    )
+    )(kv_cache, route, picked)
     got = lax.all_to_all(spread, "tp", split_axis=0, concat_axis=0, tiled=True)
     got = lax.all_to_all(got, "inst", split_axis=0, concat_axis=0, tiled=True)
 
@@ -188,15 +222,16 @@
         [back_k.reshape(32, 2, HD), fresh_kv[:, HD:].reshape(32, 2, HD)], axis=1
     )
 
-    send, tab = pl.pallas_call(
+    send, tab, info = pl.pallas_call(
         dispatch_kernel,
         out_shape=(
             jax.ShapeDtypeStruct((64 * UNITS, 2, 128), bf),
             jax.ShapeDtypeStruct((64, 128), jnp.int32),
+            jax.ShapeDtypeStruct((32,), jnp.int32),
         ),
         in_specs=[SMEM, VMEM, VMEM],
-        out_specs=(VMEM, VMEM),
-        scratch_shapes=[pltpu.SMEM((64, 128), jnp.int32), pltpu.SemaphoreType.DMA],
+        out_specs=(VMEM, VMEM, SMEM),
+        scratch_shapes=DISPATCH_SCRATCH,
         compiler_params=PARAMS,
         name="dispatch",
     )(own[None], got, back)
@@ -206,12 +241,17 @@
     )
 
     mine = lax.dynamic_index_in_dim(tab, own, 0, keepdims=False)
-    units = recv.reshape(64, UNITS // 2, 2, 2, 128)
-    rows = units[route, CTX // 2 + mine[32:48]]
-    rows = jnp.broadcast_to(rows[None], (8,) + rows.shape)
+    rows = pl.pallas_call(
+        collect_kernel,
+        out_shape=jax.ShapeDtypeStruct((256, 2, 128), bf),
+        in_specs=[SMEM, VMEM],
+        out_specs=VMEM,
+        compiler_params=PARAMS,
+        name="collect",
+    )(info, recv.reshape(64 * UNITS, 2, 128)).reshape(8, 16, 2, 2, 128)
     rows = lax.all_to_all(rows, "tp", split_axis=0, concat_axis=0, tiled=True)
     picks = got[:, 16, 1, :64].reshape(64, 32, 2).astype(jnp.int32)
-    pos = picks[route, mine[48:64]].reshape(32) - 8 * y
+    pos = picks[route, mine[16:32]].reshape(32) - 8 * y
     updated = pl.pallas_call(
         update_kernel,
         out_shape=jax.ShapeDtypeStruct(kv_cache.shape, bf),
@@ -235,10 +275,7 @@
         out_shape=jax.ShapeDtypeStruct(queries.shape, bf),
         in_specs=[SMEM] + [VMEM] * 9,
         out_specs=VMEM,
-        scratch_shapes=[
-            pltpu.VMEM((2048, HD), bf),
-            pltpu.VMEM((2048, HD), bf),
-        ],
+        scratch_shapes=ATTEND_SCRATCH,
         compiler_params=PARAMS,
         cost_estimate=pl.CostEstimate(
             flops=4 * 384 * 2048 * 128, bytes_accessed=1500000,
@@ -246,7 +283,7 @@
         ),
         name="attend",
     )(
-        mine[17:18], recv.reshape(64, 2 * UNITS, 128), queries, f0, f1, i0, i1,
+        info, recv.reshape(64, 2 * UNITS, 128), queries, f0, f1, i0, i1,
         cos2, sin2, qpos,
     )
     return attn_out, updated

time: 156 us -> 156 us (level)
  local copies, waits for them, and re-layouts: 7.24 us -> 5.18 us
  waiting for transfers between devices: 82.8 us -> 84.5 us
    all_to_all x1, waiting for transfers between devices: 0.01 us -> 1.64 us  [local(): rows = lax.all_to_all(rows, 'tp', split_axis=0, concat_axis=0, tiled=True)]
  transfers between devices with their start and end apart: 3 -> 3, of which waited for: 2 -> 3; matrix products, arithmetic and copies ran while one was open for 2% -> 2% of each run, Pallas kernels for 3% -> 2%
where the time goes in v3:
time: 156 us; the launch traced here: 155 us
  waiting for transfers between devices  84.5 us (54%)
  starting transfers between devices  31.7 us (20%)
  blocking collectives  20.1 us (13%)
  Pallas kernels  12.2 us (8%)
  local copies, waits for them, and re-layouts  5.18 us (3%)
    all_to_all x1, waiting for transfers between devices, local(): lax.all_to_all(send.reshape(64, UNITS, 2, 128), 'inst', split_axis=0, con...  52.6 us
    all_to_all x1, waiting for transfers between devices, local(): got = lax.all_to_all(got, 'inst', split_axis=0, concat_axis=0, tiled=True)  30.2 us
    all_to_all x1, blocking collectives, local(): got = lax.all_to_all(spread, 'tp', split_axis=0, concat_axis=0, tiled=True)  20.1 us
    all_to_all x1, starting transfers between devices, local(): got = lax.all_to_all(got, 'inst', split_axis=0, concat_axis=0, tiled=True)  14.2 us
    all_to_all x1, starting transfers between devices, local(): lax.all_to_all(send.reshape(64, UNITS, 2, 128), 'inst', split_axis=0, con...  8.85 us
    all_to_all x1, starting transfers between devices, local(): rows = lax.all_to_all(rows, 'tp', split_axis=0, concat_axis=0, tiled=True)  8.64 us
    pallas_call x1, Pallas kernels, local(): pl.pallas_call(dispatch_kernel, out_shape=(jax.ShapeDtypeStruct((64 * UNI...  4.31 us
    pallas_call x1, Pallas kernels, local(): pl.pallas_call(attention_kernel, out_shape=jax.ShapeDtypeStruct(queries.s...  3.41 us
  transfers between devices with their start and end apart: 3, of which 3 were waited for; matrix products, arithmetic and copies ran while one was open for 2% of the time, Pallas kernels for 2%

profile of v3, /device:TPU:1, one launch (start us, length us, event | category | flops | bytes accessed | tf_op | source)
XLA Modules:
  0.0 155.1 jit_solution(3715597779460245009)
XLA Ops:
  0.6 0.8 copy.23.picked_ref
  1.4 1.0 copy-done
  2.4 0.7 copy-done.3
  3.1 1.5 spread.1
  4.6 20.1 %all_to_all.20 = bf16[64,17,2,128]{3,2,1,0:T(2,128)(2,1)} all-to-all(bf16[64,17,2,128]{3,2,1,0:T(2,128)(2,1)S(1)} %spread.1), channel_id=1, replica_groups=mesh['inst'=64,'tp'=8] {'tp'}, dimensions={0} | all-to-all | bytes 1114112 | tf_op jit(solution)/shard_map/all_to_all | solution.py:204
  24.8 14.2 %all-to-all-start.1 = ((bf16[64,17,2,128]{3,2,1,0:T(2,128)(2,1)}), bf16[64,17,2,128]{3,2,1,0:T(2,128)(2,1)S(1)}, u32[]{:S(2)}, u32[]{:S(2)}) async-start(bf16[64,17,2,128]{3,2,1,0:T(2,128)(2,1)} %all_to_all.20), calls=%async_computation.1 | async-start | bytes 1114112 | tf_op jit(solution)/shard_map/all_to_all | solution.py:205
  39.0 0.2 fusion.2
  39.2 0.1 fusion.1
  39.4 30.2 %all-to-all-done.1.r_ref = bf16[64,17,2,128]{3,2,1,0:T(2,128)(2,1)S(1)} async-done(((bf16[64,17,2,128]{3,2,1,0:T(2,128)(2,1)}), bf16[64,17,2,128]{3,2,1,0:T(2,128)(2,1)S(1)}, u32[]{:S(2)}, u32[]{:S(2)}) %all-to-all-start.1) | async-done | bytes 557088 | tf_op jit(solution)/shard_map/all_to_all | solution.py:205
  69.6 4.3 %dispatch.1 = (bf16[2304,2,128]{2,1,0:T(2,128)(2,1)}, s32[64,128]{1,0:T(8,128)S(1)}, s32[32]{0:T(128)S(1)}) custom-call(s32[1]{0:T(128)} %bitcast.own_ref, bf16[64,17,2,128]{3,2,1,0:T(2,128)(2,1)S(1)} %all-to-all-done.1.r_ref, bf16[32,2,2,128]{3,2,1,0:T(2,128)(2,1)S(1)} %pad_maximum_fusion.2.back_ref), custom_call_target="tpu_custom_call" | custom-call | tf_op jit(solution)/shard_map/dispatch/pallas_call | solution.py:225
  73.9 8.9 %all-to-all-start.2 = ((bf16[64,36,2,128]{3,2,1,0:T(2,128)(2,1)}), bf16[64,36,2,128]{3,2,1,0:T(2,128)(2,1)S(1)}, u32[]{:S(2)}, u32[]{:S(2)}) async-start(bf16[64,36,2,128]{3,2,1,0:T(2,128)(2,1)} %bitcast.4), calls=%async_computation.2 | async-start | bytes 2359296 | tf_op jit(solution)/shard_map/all_to_all | solution.py:238
  82.8 0.1 copy.25
  82.9 0.1 reshape.113.qpos_ref
  83.0 0.1 eq.23
  83.1 0.1 eq.20
  83.2 0.1 eq.21
  83.3 0.1 broadcast_in_dim.50
  83.4 0.1 broadcast_in_dim.51
  83.7 0.1 slice_convert_fusion
  83.8 0.1 copy.27
  83.9 1.0 copy.28
  84.9 0.1 fusion.11
  84.9 0.6 gather_fusion
  85.6 52.6 %all-to-all-done.2 = bf16[64,36,2,128]{3,2,1,0:T(2,128)(2,1)S(1)} async-done(((bf16[64,36,2,128]{3,2,1,0:T(2,128)(2,1)}), bf16[64,36,2,128]{3,2,1,0:T(2,128)(2,1)S(1)}, u32[]{:S(2)}, u32[]{:S(2)}) %all-to-all-start.2) | async-done | bytes 1179680 | tf_op jit(solution)/shard_map/all_to_all | solution.py:238
  138.2 1.3 collect.1
  139.5 8.6 %all-to-all-start.3 = ((bf16[8,16,2,2,128]{4,3,2,1,0:T(2,128)(2,1)}), bf16[8,16,2,2,128]{4,3,2,1,0:T(2,128)(2,1)S(1)}, u32[]{:S(2)}, u32[]{:S(2)}) async-start(bf16[8,16,2,2,128]{4,3,2,1,0:T(2,128)(2,1)} %bitcast.13), calls=%async_computation.3 | async-start | bytes 262144 | tf_op jit(solution)/shard_map/all_to_all | solution.py:252
  148.1 0.1 sub.34.pos_ref
  148.2 0.1 broadcast_in_dim.56.i1_ref
  148.3 0.1 broadcast_in_dim.54.i0_ref
  148.3 3.4 %attend.1 = bf16[64,768]{1,0:T(8,128)(2,1)} custom-call(s32[32]{0:T(128)S(1)} %get-tuple-element.5.info_ref, bf16[64,72,128]{2,1,0:T(8,128)(2,1)S(1)} %bitcast.35, bf16[64,768]{1,0:T(8,128)(2,1)S(1)} %copy-done.2, bf16[64,256]{1,0:T(8,128)(2,1)S(1)} %reshape.96.f0_ref, bf16[64,256]{1,0:T(8,128)(2,1)S(1)} %reshape.97.f1_ref, ...), custom_call_target="tpu_custom_call" | custom-call | flops 402653184 | bytes 1500000 | tf_op jit(solution)/shard_map/attend/pallas_call | solution.py:273
  151.8 1.6 %all-to-all-done.3.rows_ref = bf16[8,16,2,2,128]{4,3,2,1,0:T(2,128)(2,1)S(1)} async-done(((bf16[8,16,2,2,128]{4,3,2,1,0:T(2,128)(2,1)}), bf16[8,16,2,2,128]{4,3,2,1,0:T(2,128)(2,1)S(1)}, u32[]{:S(2)}, u32[]{:S(2)}) %all-to-all-start.3) | async-done | bytes 131104 | tf_op jit(solution)/shard_map/all_to_all | solution.py:252
  153.4 1.7 %update.1 = bf16[16,8,2048]{2,1,0:T(8,128)(2,1)} custom-call(s32[32]{0:T(128)S(1)} %sub.34.pos_ref, bf16[16,8,2048]{2,1,0:T(8,128)(2,1)S(1)} %copy-done.1, bf16[8,16,2,2,128]{4,3,2,1,0:T(2,128)(2,1)S(1)} %all-to-all-done.3.rows_ref), custom_call_target="tpu_custom_call" | custom-call | tf_op jit(solution)/shard_map/update/pallas_call | solution.py:255
  (30 shorter events, 0.3 us)
Async XLA Ops:
  1.4 1.0 copy-start
  2.4 0.7 copy-start.3
  4.6 34.4 %copy-start.5 = (bf16[64,256]{1,0:T(8,128)(2,1)S(1)}, bf16[64,256]{1,0:T(8,128)(2,1)}, u32[]{:S(2)}) copy-start(bf16[64,256]{1,0:T(8,128)(2,1)} %param.8) | copy-start | bytes 98308
  24.8 44.8 %all-to-all-start.1 = ((bf16[64,17,2,128]{3,2,1,0:T(2,128)(2,1)}), bf16[64,17,2,128]{3,2,1,0:T(2,128)(2,1)S(1)}, u32[]{:S(2)}, u32[]{:S(2)}) async-start(bf16[64,17,2,128]{3,2,1,0:T(2,128)(2,1)} %all_to_all.20), calls=%async_computation.1 | async-start | bytes 1114112 | tf_op jit(solution)/shard_map/all_to_all | solution.py:205
  73.9 8.9 %copy-start.6 = (s32[32,2]{0,1:T(2,128)S(1)}, s32[32,2]{0,1:T(2,128)}, u32[]{:S(2)}) copy-start(s32[32,2]{0,1:T(2,128)} %param.9) | copy-start | bytes 772
  73.9 64.3 %all-to-all-start.2 = ((bf16[64,36,2,128]{3,2,1,0:T(2,128)(2,1)}), bf16[64,36,2,128]{3,2,1,0:T(2,128)(2,1)S(1)}, u32[]{:S(2)}, u32[]{:S(2)}) async-start(bf16[64,36,2,128]{3,2,1,0:T(2,128)(2,1)} %bitcast.4), calls=%async_computation.2 | async-start | bytes 2359296 | tf_op jit(solution)/shard_map/all_to_all | solution.py:238
  82.8 2.1 %copy-start.4 = (s32[16]{0:T(128)S(1)}, s32[16]{0:T(128)}, u32[]{:S(2)}) copy-start(s32[16]{0:T(128)} %route_ref.1) | copy-start | bytes 196
  83.8 64.5 %copy-start.2 = (bf16[64,768]{1,0:T(8,128)(2,1)S(1)}, bf16[64,768]{1,0:T(8,128)(2,1)}, u32[]{:S(2)}) copy-start(bf16[64,768]{1,0:T(8,128)(2,1)} %q_ref.1) | copy-start | bytes 294916
  139.5 13.9 %copy-start.1 = (bf16[16,8,2048]{2,1,0:T(8,128)(2,1)S(1)}, bf16[16,8,2048]{2,1,0:T(8,128)(2,1)}, u32[]{:S(2)}) copy-start(bf16[16,8,2048]{2,1,0:T(8,128)(2,1)} %x_ref.3) | copy-start | bytes 1572868
  139.5 13.9 %all-to-all-start.3 = ((bf16[8,16,2,2,128]{4,3,2,1,0:T(2,128)(2,1)}), bf16[8,16,2,2,128]{4,3,2,1,0:T(2,128)(2,1)S(1)}, u32[]{:S(2)}, u32[]{:S(2)}) async-start(bf16[8,16,2,2,128]{4,3,2,1,0:T(2,128)(2,1)} %bitcast.13), calls=%async_computation.3 | async-start | bytes 262144 | tf_op jit(solution)/shard_map/all_to_all | solution.py:252

commit v4 on v3

--- a/solution.py
+++ b/solution.py
@@ -16,8 +16,8 @@
 VMEM = pl.BlockSpec(memory_space=pltpu.VMEM)
 SMEM = pl.BlockSpec(memory_space=pltpu.SMEM)
 DISPATCH_SCRATCH = [
-    pltpu.VMEM((24, 128), jnp.int32),
-    pltpu.SMEM((24, 128), jnp.int32),
+    pltpu.VMEM((8, 128), jnp.int32),
+    pltpu.SMEM((8, 128), jnp.int32),
     pltpu.SemaphoreType.DMA,
 ]
 ATTEND_SCRATCH = [
@@ -28,17 +28,16 @@
 
 
 def spread_kernel(x_ref, route_ref, picked_ref, out_ref):
-    lane = lax.broadcasted_iota(jnp.int32, (8, 128), 1)
-    ctrl = jnp.zeros((8, 128), jnp.int32)
-    picks = jnp.zeros((8, 128), jnp.int32)
+    lane = lax.broadcasted_iota(jnp.int32, (2, 128), 1)
+    ctrl = jnp.zeros((2, 128), jnp.int32)
     for l in range(16):
         ctrl = jnp.where(lane == l, route_ref[l], ctrl)
         ctrl = ctrl + jnp.where(lane == 64 + route_ref[l], 1, 0)
-    for j in range(32):
-        for w in range(2):
-            picks = jnp.where(lane == 2 * j + w, picked_ref[j, w], picks)
-    row = lax.broadcasted_iota(jnp.int32, (8, 128), 0)
-    ctrl = jnp.where(row == 0, ctrl, picks)[:2]
+    picks = jnp.concatenate(
+        [picked_ref[0:1, :], picked_ref[1:2, :], jnp.zeros((1, 64), jnp.int32)], axis=1
+    )
+    row = lax.broadcasted_iota(jnp.int32, (2, 128), 0)
+    ctrl = jnp.where(row == 0, ctrl, picks)
     ctrl = ctrl.astype(jnp.float32).astype(jnp.bfloat16)
     for d in range(64):
         out_ref[d, 16] = ctrl
@@ -56,7 +55,7 @@
     lax.fori_loop(0, 16, step, 0)
 
 
-def dispatch_kernel(own_ref, r_ref, back_ref, out_ref, tab_ref, info_ref, packed, tabs, sem):
+def dispatch_kernel(own_ref, r_ref, back_ref, out_ref, tab_ref, total_ref, packed, tabs, sem):
     own = own_ref[0]
     ctrl = r_ref[:, 16, 0, :].astype(jnp.float32)
     lane = lax.broadcasted_iota(jnp.int32, (64, 128), 1)
@@ -75,28 +74,31 @@
     slot = jnp.take_along_axis(starts, routes, axis=1) + within
     place = routes * UNITS + slot
     ret = routes * UNITS + CTX + 2 * within
-    tab_ref[...] = jnp.where(lane < 16, within, pltpu.roll(slot, 16, 1))
+    tab_ref[...] = jnp.where(lane < 16, ret, pltpu.roll(slot, 16, 1))
     own_lane = lane == own
     first = jnp.sum(jnp.where(own_lane, starts, 0), axis=1, keepdims=True)
+    table = place + 4096 * first
     lane8 = lax.broadcasted_iota(jnp.int32, (8, 128), 1)
-    for n, table in enumerate((place, ret, jnp.broadcast_to(first, (64, 128)))):
-        acc = jnp.zeros((8, 128), jnp.int32)
-        for a in range(8):
-            part = table[8 * a : 8 * a + 8]
-            if a:
-                part = pltpu.roll(part, 16 * a, 1)
-            acc = jnp.where(lane8 // 16 == a, part, acc)
-        packed[8 * n : 8 * n + 8] = acc
+    acc = jnp.zeros((8, 128), jnp.int32)
+    for a in range(8):
+        part = table[8 * a : 8 * a + 8]
+        if a:
+            part = pltpu.roll(part, 16 * a, 1)
+        acc = jnp.where(lane8 // 16 == a, part, acc)
+    packed[...] = acc
     copy = pltpu.make_async_copy(packed, tabs, sem)
     copy.start()
+    total = jnp.sum(jnp.where(own_lane, counts, 0.0)).astype(jnp.int32)
+    total_ref[...] = jnp.full((1, 128), total, jnp.int32)
     copy.wait()
 
     def step(a, carry):
         for r in range(8):
             h = a * 8 + r
-            place = [tabs[r, a * 16 + l] for l in range(16)]
+            both = [tabs[r, a * 16 + l] for l in range(16)]
+            place = [v & 4095 for v in both]
             units = [r_ref[h, l] for l in range(16)]
-            first = tabs[16 + r, a * 16]
+            first = both[0] >> 12
             slots = [jnp.minimum(first + s, CTX - 1) for s in range(2)]
             backs = [back_ref[slots[s], kv] for s in range(2) for kv in range(2)]
             for l in range(16):
@@ -106,9 +108,6 @@
         return carry
 
     lax.fori_loop(0, 8, step, 0)
-    for l in range(16):
-        info_ref[l] = tabs[8 + lax.rem(own, 8), own // 8 * 16 + l]
-    info_ref[16] = jnp.sum(jnp.where(own_lane, counts, 0.0)).astype(jnp.int32)
 
 
 def collect_kernel(info_ref, recv_ref, out_ref):
@@ -120,10 +119,10 @@
 
 
 def attention_kernel(
-    info_ref, recv_ref, q_ref, f0_ref, f1_ref, i0_ref, i1_ref,
+    total_ref, recv_ref, q_ref, f0_ref, f1_ref, i0_ref, i1_ref,
     cos_ref, sin_ref, qpos_ref, out_ref, keys, vals,
 ):
-    total = info_ref[16]
+    total = total_ref[0]
     cos = cos_ref[...]
     sin = sin_ref[...]
     pick0 = i0_ref[...]
@@ -196,11 +195,11 @@
     spread = pl.pallas_call(
         spread_kernel,
         out_shape=jax.ShapeDtypeStruct((64, 17, 2, 128), bf),
-        in_specs=[VMEM, SMEM, SMEM],
+        in_specs=[VMEM, SMEM, VMEM],
         out_specs=VMEM,
         compiler_params=PARAMS,
         name="spread",
-    )(kv_cache, route, picked)
+    )(kv_cache, route, picked.T)
     got = lax.all_to_all(spread, "tp", split_axis=0, concat_axis=0, tiled=True)
     got = lax.all_to_all(got, "inst", split_axis=0, concat_axis=0, tiled=True)
 
@@ -222,15 +221,15 @@
         [back_k.reshape(32, 2, HD), fresh_kv[:, HD:].reshape(32, 2, HD)], axis=1
     )
 
-    send, tab, info = pl.pallas_call(
+    send, tab, total = pl.pallas_call(
         dispatch_kernel,
         out_shape=(
             jax.ShapeDtypeStruct((64 * UNITS, 2, 128), bf),
             jax.ShapeDtypeStruct((64, 128), jnp.int32),
-            jax.ShapeDtypeStruct((32,), jnp.int32),
+            jax.ShapeDtypeStruct((1, 128), jnp.int32),
         ),
         in_specs=[SMEM, VMEM, VMEM],
-        out_specs=(VMEM, VMEM, SMEM),
+        out_specs=(VMEM, VMEM, VMEM),
         scratch_shapes=DISPATCH_SCRATCH,
         compiler_params=PARAMS,
         name="dispatch",
@@ -248,10 +247,10 @@
         out_specs=VMEM,
         compiler_params=PARAMS,
         name="collect",
-    )(info, recv.reshape(64 * UNITS, 2, 128)).reshape(8, 16, 2, 2, 128)
+    )(mine[:16], recv.reshape(64 * UNITS, 2, 128)).reshape(8, 16, 2, 2, 128)
     rows = lax.all_to_all(rows, "tp", split_axis=0, concat_axis=0, tiled=True)
-    picks = got[:, 16, 1, :64].reshape(64, 32, 2).astype(jnp.int32)
-    pos = picks[route, mine[16:32]].reshape(32) - 8 * y
+    picks = got[:, 16, 1, :64].reshape(64, 2, 32).astype(jnp.int32)
+    pos = picks[route, :, mine[16:32]].reshape(32) - 8 * y
     updated = pl.pallas_call(
         update_kernel,
         out_shape=jax.ShapeDtypeStruct(kv_cache.shape, bf),
@@ -283,7 +282,7 @@
         ),
         name="attend",
     )(
-        info, recv.reshape(64, 2 * UNITS, 128), queries, f0, f1, i0, i1,
+        total[0, :1], recv.reshape(64, 2 * UNITS, 128), queries, f0, f1, i0, i1,
         cos2, sin2, qpos,
     )
     return attn_out, updated

time: 156 us -> 155 us (level)
  no operation moved by 1% of the time
where the time goes in v4:
time: 155 us
  waiting for transfers between devices  85 us (55%)
  starting transfers between devices  31.7 us (20%)
  blocking collectives  20.1 us (13%)
  Pallas kernels  11.4 us (7%)
  local copies, waits for them, and re-layouts  5.04 us (3%)
    all_to_all x1, waiting for transfers between devices, local(): lax.all_to_all(send.reshape(64, UNITS, 2, 128), 'inst', split_axis=0, con...  52.7 us
    all_to_all x1, waiting for transfers between devices, local(): got = lax.all_to_all(got, 'inst', split_axis=0, concat_axis=0, tiled=True)  30.2 us
    all_to_all x1, blocking collectives, local(): got = lax.all_to_all(spread, 'tp', split_axis=0, concat_axis=0, tiled=True)  20.1 us
    all_to_all x1, starting transfers between devices, local(): got = lax.all_to_all(got, 'inst', split_axis=0, concat_axis=0, tiled=True)  14.2 us
    all_to_all x1, starting transfers between devices, local(): lax.all_to_all(send.reshape(64, UNITS, 2, 128), 'inst', split_axis=0, con...  8.85 us
    all_to_all x1, starting transfers between devices, local(): rows = lax.all_to_all(rows, 'tp', split_axis=0, concat_axis=0, tiled=True)  8.64 us
    pallas_call x1, Pallas kernels, local(): pl.pallas_call(dispatch_kernel, out_shape=(jax.ShapeDtypeStruct((64 * UNI...  4.3 us
  transfers between devices with their start and end apart: 3, of which 3 were waited for; matrix products, arithmetic and copies ran while one was open for 2% of the time, Pallas kernels for 2%

profile of v4, /device:TPU:1, one launch (start us, length us, event | category | flops | bytes accessed | tf_op | source)
XLA Modules:
  0.0 154.7 jit_solution(4231310328660699066)
XLA Ops:
  0.6 1.0 copy-done
  1.7 0.7 copy-done.3
  2.4 0.7 copy-done.5
  3.0 1.3 spread.1
  4.3 20.1 %all_to_all.20 = bf16[64,17,2,128]{3,2,1,0:T(2,128)(2,1)} all-to-all(bf16[64,17,2,128]{3,2,1,0:T(2,128)(2,1)S(1)} %spread.1), channel_id=1, replica_groups=mesh['inst'=64,'tp'=8] {'tp'}, dimensions={0} | all-to-all | bytes 1114112 | tf_op jit(solution)/shard_map/all_to_all | solution.py:203
  24.4 14.2 %all-to-all-start.1 = ((bf16[64,17,2,128]{3,2,1,0:T(2,128)(2,1)}), bf16[64,17,2,128]{3,2,1,0:T(2,128)(2,1)S(1)}, u32[]{:S(2)}, u32[]{:S(2)}) async-start(bf16[64,17,2,128]{3,2,1,0:T(2,128)(2,1)} %all_to_all.20), calls=%async_computation.1 | async-start | bytes 1114112 | tf_op jit(solution)/shard_map/all_to_all | solution.py:204
  38.7 0.2 fusion.2
  38.9 0.1 fusion.1
  39.1 30.2 %all-to-all-done.1.r_ref = bf16[64,17,2,128]{3,2,1,0:T(2,128)(2,1)S(1)} async-done(((bf16[64,17,2,128]{3,2,1,0:T(2,128)(2,1)}), bf16[64,17,2,128]{3,2,1,0:T(2,128)(2,1)S(1)}, u32[]{:S(2)}, u32[]{:S(2)}) %all-to-all-start.1) | async-done | bytes 557088 | tf_op jit(solution)/shard_map/all_to_all | solution.py:204
  69.3 4.3 %dispatch.1 = (bf16[2304,2,128]{2,1,0:T(2,128)(2,1)}, s32[64,128]{1,0:T(8,128)S(1)}, s32[1,128]{1,0:T(1,128)S(1)}) custom-call(s32[1]{0:T(128)} %bitcast.own_ref, bf16[64,17,2,128]{3,2,1,0:T(2,128)(2,1)S(1)} %all-to-all-done.1.r_ref, bf16[32,2,2,128]{3,2,1,0:T(2,128)(2,1)S(1)} %pad_maximum_fusion.2.back_ref), custom_call_target="tpu_custom_call" | custom-call | tf_op jit(solution)/shard_map/dispatch/pallas_call | solution.py:224
  73.6 8.9 %all-to-all-start.2 = ((bf16[64,36,2,128]{3,2,1,0:T(2,128)(2,1)}), bf16[64,36,2,128]{3,2,1,0:T(2,128)(2,1)S(1)}, u32[]{:S(2)}, u32[]{:S(2)}) async-start(bf16[64,36,2,128]{3,2,1,0:T(2,128)(2,1)} %bitcast.6), calls=%async_computation.2 | async-start | bytes 2359296 | tf_op jit(solution)/shard_map/all_to_all | solution.py:237
  82.5 0.1 copy.22
  82.6 0.1 reshape.114.qpos_ref
  82.7 0.1 eq.23
  82.8 0.1 eq.20
  82.9 0.1 eq.21
  83.0 0.1 broadcast_in_dim.50
  83.1 0.1 broadcast_in_dim.51
  83.4 0.1 slice_convert_fusion
  83.4 0.1 copy.24
  83.5 0.9 copy.25
  84.5 0.1 fusion.11
  84.6 0.6 gather_fusion
  85.2 52.7 %all-to-all-done.2 = bf16[64,36,2,128]{3,2,1,0:T(2,128)(2,1)S(1)} async-done(((bf16[64,36,2,128]{3,2,1,0:T(2,128)(2,1)}), bf16[64,36,2,128]{3,2,1,0:T(2,128)(2,1)S(1)}, u32[]{:S(2)}, u32[]{:S(2)}) %all-to-all-start.2) | async-done | bytes 1179680 | tf_op jit(solution)/shard_map/all_to_all | solution.py:237
  137.9 1.3 collect.1
  139.1 8.6 %all-to-all-start.3 = ((bf16[8,16,2,2,128]{4,3,2,1,0:T(2,128)(2,1)}), bf16[8,16,2,2,128]{4,3,2,1,0:T(2,128)(2,1)S(1)}, u32[]{:S(2)}, u32[]{:S(2)}) async-start(bf16[8,16,2,2,128]{4,3,2,1,0:T(2,128)(2,1)} %bitcast.16), calls=%async_computation.3 | async-start | bytes 262144 | tf_op jit(solution)/shard_map/all_to_all | solution.py:251
  147.8 0.1 sub.34.pos_ref
  147.9 0.1 broadcast_in_dim.56.i1_ref
  147.9 0.1 broadcast_in_dim.54.i0_ref
  148.0 2.9 %attend.1 = bf16[64,768]{1,0:T(8,128)(2,1)} custom-call(s32[1]{0:T(128)S(1)} %bitcast.42, bf16[64,72,128]{2,1,0:T(8,128)(2,1)S(1)} %bitcast.40, bf16[64,768]{1,0:T(8,128)(2,1)S(1)} %copy-done.2, bf16[64,256]{1,0:T(8,128)(2,1)S(1)} %reshape.97.f0_ref, bf16[64,256]{1,0:T(8,128)(2,1)S(1)} %reshape.98.f1_ref, s32[64,128]{1,0:T(8,128)S(1)} %broadcast_in_dim.54.i0_ref, ...), custom_call_target="tpu_custom_call" | custom-call | flops 402653184 | bytes 1500000 | tf_op jit(solution)/shard_map/attend/pallas_call | solution.py:272
  150.9 2.1 %all-to-all-done.3.rows_ref = bf16[8,16,2,2,128]{4,3,2,1,0:T(2,128)(2,1)S(1)} async-done(((bf16[8,16,2,2,128]{4,3,2,1,0:T(2,128)(2,1)}), bf16[8,16,2,2,128]{4,3,2,1,0:T(2,128)(2,1)S(1)}, u32[]{:S(2)}, u32[]{:S(2)}) %all-to-all-start.3) | async-done | bytes 131104 | tf_op jit(solution)/shard_map/all_to_all | solution.py:251
  153.1 1.7 %update.1 = bf16[16,8,2048]{2,1,0:T(8,128)(2,1)} custom-call(s32[32]{0:T(128)S(1)} %sub.34.pos_ref, bf16[16,8,2048]{2,1,0:T(8,128)(2,1)S(1)} %copy-done.1, bf16[8,16,2,2,128]{4,3,2,1,0:T(2,128)(2,1)S(1)} %all-to-all-done.3.rows_ref), custom_call_target="tpu_custom_call" | custom-call | tf_op jit(solution)/shard_map/update/pallas_call | solution.py:254
  (32 shorter events, 0.3 us)
Async XLA Ops:
  0.6 1.0 copy-start
  1.7 0.7 copy-start.3
  2.4 0.7 copy-start.5
  4.3 34.4 %copy-start.7 = (bf16[64,256]{1,0:T(8,128)(2,1)S(1)}, bf16[64,256]{1,0:T(8,128)(2,1)}, u32[]{:S(2)}) copy-start(bf16[64,256]{1,0:T(8,128)(2,1)} %param.8) | copy-start | bytes 98308
  24.4 44.8 %all-to-all-start.1 = ((bf16[64,17,2,128]{3,2,1,0:T(2,128)(2,1)}), bf16[64,17,2,128]{3,2,1,0:T(2,128)(2,1)S(1)}, u32[]{:S(2)}, u32[]{:S(2)}) async-start(bf16[64,17,2,128]{3,2,1,0:T(2,128)(2,1)} %all_to_all.20), calls=%async_computation.1 | async-start | bytes 1114112 | tf_op jit(solution)/shard_map/all_to_all | solution.py:204
  73.6 8.9 %copy-start.4 = (s32[32,2]{0,1:T(2,128)S(1)}, s32[32,2]{0,1:T(2,128)}, u32[]{:S(2)}) copy-start(s32[32,2]{0,1:T(2,128)} %param.9) | copy-start | bytes 772
  73.6 64.3 %all-to-all-start.2 = ((bf16[64,36,2,128]{3,2,1,0:T(2,128)(2,1)}), bf16[64,36,2,128]{3,2,1,0:T(2,128)(2,1)S(1)}, u32[]{:S(2)}, u32[]{:S(2)}) async-start(bf16[64,36,2,128]{3,2,1,0:T(2,128)(2,1)} %bitcast.6), calls=%async_computation.2 | async-start | bytes 2359296 | tf_op jit(solution)/shard_map/all_to_all | solution.py:237
  82.4 2.0 %copy-start.6 = (s32[16]{0:T(128)S(1)}, s32[16]{0:T(128)}, u32[]{:S(2)}) copy-start(s32[16]{0:T(128)} %route_ref.1) | copy-start | bytes 196
  83.5 64.5 %copy-start.2 = (bf16[64,768]{1,0:T(8,128)(2,1)S(1)}, bf16[64,768]{1,0:T(8,128)(2,1)}, u32[]{:S(2)}) copy-start(bf16[64,768]{1,0:T(8,128)(2,1)} %q_ref.1) | copy-start | bytes 294916
  139.1 13.9 %copy-start.1 = (bf16[16,8,2048]{2,1,0:T(8,128)(2,1)S(1)}, bf16[16,8,2048]{2,1,0:T(8,128)(2,1)}, u32[]{:S(2)}) copy-start(bf16[16,8,2048]{2,1,0:T(8,128)(2,1)} %x_ref.3) | copy-start | bytes 1572868
  139.1 13.9 %all-to-all-start.3 = ((bf16[8,16,2,2,128]{4,3,2,1,0:T(2,128)(2,1)}), bf16[8,16,2,2,128]{4,3,2,1,0:T(2,128)(2,1)S(1)}, u32[]{:S(2)}, u32[]{:S(2)}) async-start(bf16[8,16,2,2,128]{4,3,2,1,0:T(2,128)(2,1)} %bitcast.16), calls=%async_computation.3 | async-start | bytes 262144 | tf_op jit(solution)/shard_map/all_to_all | solution.py:251

commit v5 on v4

--- a/solution.py
+++ b/solution.py
@@ -24,6 +24,7 @@
     pltpu.VMEM((2048, HD), jnp.bfloat16),
     pltpu.VMEM((2048, HD), jnp.bfloat16),
 ]
+WHOLE = pltpu.CompilerParams(vmem_limit_bytes=66_400_000)
 PARAMS = pltpu.CompilerParams(vmem_limit_bytes=40 * 1024 * 1024)
 
 
@@ -197,7 +198,7 @@
         out_shape=jax.ShapeDtypeStruct((64, 17, 2, 128), bf),
         in_specs=[VMEM, SMEM, VMEM],
         out_specs=VMEM,
-        compiler_params=PARAMS,
+        compiler_params=WHOLE,
         name="spread",
     )(kv_cache, route, picked.T)
     got = lax.all_to_all(spread, "tp", split_axis=0, concat_axis=0, tiled=True)

time: 155 us -> 155 us (level)
  local copies, waits for them, and re-layouts: 5.04 us -> 2.67 us
    unnamed x17 -> x11, local copies, waits for them, and re-layouts: 2.4 us -> 0.03 us
where the time goes in v5:
time: 155 us; the launch traced here: 154 us
  waiting for transfers between devices  85 us (55%)
  starting transfers between devices  30.8 us (20%)
  blocking collectives  21.4 us (14%)
  Pallas kernels  12.8 us (8%)
  local copies, waits for them, and re-layouts  2.67 us (2%)
    all_to_all x1, waiting for transfers between devices, local(): lax.all_to_all(send.reshape(64, UNITS, 2, 128), 'inst', split_axis=0, con...  52.7 us
    all_to_all x1, waiting for transfers between devices, local(): got = lax.all_to_all(got, 'inst', split_axis=0, concat_axis=0, tiled=True)  30.2 us
    all_to_all x1, blocking collectives, local(): got = lax.all_to_all(spread, 'tp', split_axis=0, concat_axis=0, tiled=True)  21.4 us
    all_to_all x1, starting transfers between devices, local(): got = lax.all_to_all(got, 'inst', split_axis=0, concat_axis=0, tiled=True)  13.3 us
    all_to_all x1, starting transfers between devices, local(): lax.all_to_all(send.reshape(64, UNITS, 2, 128), 'inst', split_axis=0, con...  8.85 us
    all_to_all x1, starting transfers between devices, local(): rows = lax.all_to_all(rows, 'tp', split_axis=0, concat_axis=0, tiled=True)  8.64 us
    pallas_call x1, Pallas kernels, local(): pl.pallas_call(dispatch_kernel, out_shape=(jax.ShapeDtypeStruct((64 * UNI...  4.32 us
  transfers between devices with their start and end apart: 3, of which 3 were waited for; matrix products, arithmetic and copies ran while one was open for 2% of the time, Pallas kernels for 2%

profile of v5, /device:TPU:1, one launch (start us, length us, event | category | flops | bytes accessed | tf_op | source)
XLA Modules:
  0.0 154.0 jit_solution(10932064863264683311)
XLA Ops:
  0.6 2.6 %spread.1 = bf16[64,17,2,128]{3,2,1,0:T(2,128)(2,1)} custom-call(bf16[16,8,2048]{2,1,0:T(8,128)(2,1)} %x_ref.3, s32[16]{0:T(128)} %route_ref.1, s32[2,32]{1,0:T(2,128)} %bitcast.45), custom_call_target="tpu_custom_call" | custom-call | tf_op jit(solution)/shard_map/spread/pallas_call | solution.py:196
  3.2 21.4 %all_to_all.20 = bf16[64,17,2,128]{3,2,1,0:T(2,128)(2,1)} all-to-all(bf16[64,17,2,128]{3,2,1,0:T(2,128)(2,1)} %spread.1), channel_id=1, replica_groups=mesh['inst'=64,'tp'=8] {'tp'}, dimensions={0} | all-to-all | bytes 1114112 | tf_op jit(solution)/shard_map/all_to_all | solution.py:204
  24.6 13.3 %all-to-all-start.1 = ((bf16[64,17,2,128]{3,2,1,0:T(2,128)(2,1)}), bf16[64,17,2,128]{3,2,1,0:T(2,128)(2,1)S(1)}, u32[]{:S(2)}, u32[]{:S(2)}) async-start(bf16[64,17,2,128]{3,2,1,0:T(2,128)(2,1)} %all_to_all.20), calls=%async_computation.1 | async-start | bytes 1114112 | tf_op jit(solution)/shard_map/all_to_all | solution.py:205
  38.0 0.2 fusion.2
  38.2 0.1 fusion.1
  38.3 0.1 pad_maximum_fusion.2.back_ref
  38.3 30.2 %all-to-all-done.1.r_ref = bf16[64,17,2,128]{3,2,1,0:T(2,128)(2,1)S(1)} async-done(((bf16[64,17,2,128]{3,2,1,0:T(2,128)(2,1)}), bf16[64,17,2,128]{3,2,1,0:T(2,128)(2,1)S(1)}, u32[]{:S(2)}, u32[]{:S(2)}) %all-to-all-start.1) | async-done | bytes 557088 | tf_op jit(solution)/shard_map/all_to_all | solution.py:205
  68.5 4.3 %dispatch.1 = (bf16[2304,2,128]{2,1,0:T(2,128)(2,1)}, s32[64,128]{1,0:T(8,128)S(1)}, s32[1,128]{1,0:T(1,128)S(1)}) custom-call(s32[1]{0:T(128)} %bitcast.own_ref, bf16[64,17,2,128]{3,2,1,0:T(2,128)(2,1)S(1)} %all-to-all-done.1.r_ref, bf16[32,2,2,128]{3,2,1,0:T(2,128)(2,1)S(1)} %pad_maximum_fusion.2.back_ref), custom_call_target="tpu_custom_call" | custom-call | tf_op jit(solution)/shard_map/dispatch/pallas_call | solution.py:225
  72.9 8.9 %all-to-all-start.2 = ((bf16[64,36,2,128]{3,2,1,0:T(2,128)(2,1)}), bf16[64,36,2,128]{3,2,1,0:T(2,128)(2,1)S(1)}, u32[]{:S(2)}, u32[]{:S(2)}) async-start(bf16[64,36,2,128]{3,2,1,0:T(2,128)(2,1)} %bitcast.6), calls=%async_computation.2 | async-start | bytes 2359296 | tf_op jit(solution)/shard_map/all_to_all | solution.py:238
  81.7 0.0 copy-start.4
  81.8 0.1 copy.22
  81.9 0.1 reshape.114.qpos_ref
  82.0 0.1 eq.23
  82.1 0.1 eq.20
  82.1 0.1 eq.21
  82.3 0.1 broadcast_in_dim.50
  82.3 0.1 broadcast_in_dim.51
  82.4 0.1 fusion.12
  82.7 0.1 slice_convert_fusion
  82.7 0.1 copy.24
  82.8 0.9 copy.25
  83.8 0.1 fusion.11
  83.8 0.6 gather_fusion
  84.5 52.7 %all-to-all-done.2 = bf16[64,36,2,128]{3,2,1,0:T(2,128)(2,1)S(1)} async-done(((bf16[64,36,2,128]{3,2,1,0:T(2,128)(2,1)}), bf16[64,36,2,128]{3,2,1,0:T(2,128)(2,1)S(1)}, u32[]{:S(2)}, u32[]{:S(2)}) %all-to-all-start.2) | async-done | bytes 1179680 | tf_op jit(solution)/shard_map/all_to_all | solution.py:238
  137.1 1.3 collect.1
  138.4 8.6 %all-to-all-start.3 = ((bf16[8,16,2,2,128]{4,3,2,1,0:T(2,128)(2,1)}), bf16[8,16,2,2,128]{4,3,2,1,0:T(2,128)(2,1)S(1)}, u32[]{:S(2)}, u32[]{:S(2)}) async-start(bf16[8,16,2,2,128]{4,3,2,1,0:T(2,128)(2,1)} %bitcast.16), calls=%async_computation.3 | async-start | bytes 262144 | tf_op jit(solution)/shard_map/all_to_all | solution.py:252
  147.1 0.1 sub.34.pos_ref
  147.2 0.1 broadcast_in_dim.56.i1_ref
  147.2 0.1 broadcast_in_dim.54.i0_ref
  147.3 2.9 %attend.1 = bf16[64,768]{1,0:T(8,128)(2,1)} custom-call(s32[1]{0:T(128)S(1)} %bitcast.41, bf16[64,72,128]{2,1,0:T(8,128)(2,1)S(1)} %bitcast.40, bf16[64,768]{1,0:T(8,128)(2,1)S(1)} %copy-done.1, bf16[64,256]{1,0:T(8,128)(2,1)S(1)} %reshape.97.f0_ref, bf16[64,256]{1,0:T(8,128)(2,1)S(1)} %reshape.98.f1_ref, s32[64,128]{1,0:T(8,128)S(1)} %broadcast_in_dim.54.i0_ref, ...), custom_call_target="tpu_custom_call" | custom-call | flops 402653184 | bytes 1500000 | tf_op jit(solution)/shard_map/attend/pallas_call | solution.py:273
  150.2 2.1 %all-to-all-done.3.rows_ref = bf16[8,16,2,2,128]{4,3,2,1,0:T(2,128)(2,1)S(1)} async-done(((bf16[8,16,2,2,128]{4,3,2,1,0:T(2,128)(2,1)}), bf16[8,16,2,2,128]{4,3,2,1,0:T(2,128)(2,1)S(1)}, u32[]{:S(2)}, u32[]{:S(2)}) %all-to-all-start.3) | async-done | bytes 131104 | tf_op jit(solution)/shard_map/all_to_all | solution.py:252
  152.4 1.7 %update.1 = bf16[16,8,2048]{2,1,0:T(8,128)(2,1)} custom-call(s32[32]{0:T(128)S(1)} %sub.34.pos_ref, bf16[16,8,2048]{2,1,0:T(8,128)(2,1)S(1)} %copy-done, bf16[8,16,2,2,128]{4,3,2,1,0:T(2,128)(2,1)S(1)} %all-to-all-done.3.rows_ref), custom_call_target="tpu_custom_call" | custom-call | tf_op jit(solution)/shard_map/update/pallas_call | solution.py:255
  (26 shorter events, 0.2 us)
Async XLA Ops:
  3.2 34.7 %copy-start.2 = (bf16[64,256]{1,0:T(8,128)(2,1)S(1)}, bf16[64,256]{1,0:T(8,128)(2,1)}, u32[]{:S(2)}) copy-start(bf16[64,256]{1,0:T(8,128)(2,1)} %param.8) | copy-start | bytes 98308
  24.6 43.9 %all-to-all-start.1 = ((bf16[64,17,2,128]{3,2,1,0:T(2,128)(2,1)}), bf16[64,17,2,128]{3,2,1,0:T(2,128)(2,1)S(1)}, u32[]{:S(2)}, u32[]{:S(2)}) async-start(bf16[64,17,2,128]{3,2,1,0:T(2,128)(2,1)} %all_to_all.20), calls=%async_computation.1 | async-start | bytes 1114112 | tf_op jit(solution)/shard_map/all_to_all | solution.py:205
  72.8 8.9 %copy-start.3 = (s32[32,2]{0,1:T(2,128)S(1)}, s32[32,2]{0,1:T(2,128)}, u32[]{:S(2)}) copy-start(s32[32,2]{0,1:T(2,128)} %param.9) | copy-start | bytes 772
  72.9 64.3 %all-to-all-start.2 = ((bf16[64,36,2,128]{3,2,1,0:T(2,128)(2,1)}), bf16[64,36,2,128]{3,2,1,0:T(2,128)(2,1)S(1)}, u32[]{:S(2)}, u32[]{:S(2)}) async-start(bf16[64,36,2,128]{3,2,1,0:T(2,128)(2,1)} %bitcast.6), calls=%async_computation.2 | async-start | bytes 2359296 | tf_op jit(solution)/shard_map/all_to_all | solution.py:238
  81.7 2.0 %copy-start.4 = (s32[16]{0:T(128)S(1)}, s32[16]{0:T(128)}, u32[]{:S(2)}) copy-start(s32[16]{0:T(128)} %route_ref.1) | copy-start | bytes 196
  82.8 64.5 %copy-start.1 = (bf16[64,768]{1,0:T(8,128)(2,1)S(1)}, bf16[64,768]{1,0:T(8,128)(2,1)}, u32[]{:S(2)}) copy-start(bf16[64,768]{1,0:T(8,128)(2,1)} %q_ref.1) | copy-start | bytes 294916
  138.4 13.9 %copy-start = (bf16[16,8,2048]{2,1,0:T(8,128)(2,1)S(1)}, bf16[16,8,2048]{2,1,0:T(8,128)(2,1)}, u32[]{:S(2)}) copy-start(bf16[16,8,2048]{2,1,0:T(8,128)(2,1)} %x_ref.3) | copy-start | bytes 1572868
  138.4 13.9 %all-to-all-start.3 = ((bf16[8,16,2,2,128]{4,3,2,1,0:T(2,128)(2,1)}), bf16[8,16,2,2,128]{4,3,2,1,0:T(2,128)(2,1)S(1)}, u32[]{:S(2)}, u32[]{:S(2)}) async-start(bf16[8,16,2,2,128]{4,3,2,1,0:T(2,128)(2,1)} %bitcast.16), calls=%async_computation.3 | async-start | bytes 262144 | tf_op jit(solution)/shard_map/all_to_all | solution.py:252

commit v6 on v5

v6 whole, which is shorter than its diff:
```python
import functools
import math

import jax
import jax.numpy as jnp
from jax import lax
from jax.experimental import pallas as pl
from jax.experimental.pallas import tpu as pltpu
from jax.sharding import PartitionSpec as P

HD = 128
QH = 6
THETA = 1000000.0
CTX = 32
UNITS = 37
VMEM = pl.BlockSpec(memory_space=pltpu.VMEM)
SMEM = pl.BlockSpec(memory_space=pltpu.SMEM)
DISPATCH_SCRATCH = [
    pltpu.VMEM((8, 128), jnp.int32),
    pltpu.SMEM((8, 128), jnp.int32),
    pltpu.SemaphoreType.DMA,
]
ATTEND_SCRATCH = [
    pltpu.VMEM((2048, HD), jnp.bfloat16),
    pltpu.VMEM((2048, HD), jnp.bfloat16),
]
WHOLE = pltpu.CompilerParams(vmem_limit_bytes=66_400_000)
PARAMS = pltpu.CompilerParams(vmem_limit_bytes=40 * 1024 * 1024)


def spread_kernel(own_ref, x_ref, out_ref):
    y = own_ref[1]

    def step(g, carry):
        for k in range(2):
            block = lax.rem(g - y + 8, 8) + 8 * k
            for head in range(8):
                for kv in range(2):
                    lane = head * 256 + kv * 128
                    for pair in range(4):
                        dest = (kv * 32 + g * 4 + pair) * 8 + head
                        out_ref[dest, k] = x_ref[
                            block, pl.ds(2 * pair, 2), pl.ds(lane, 128)
                        ]
        return carry

    lax.fori_loop(0, 8, step, 0)


def dispatch_kernel(
    own_ref, route_ref, r_ref, back_ref, picks_ref, out_ref, slot_ref, packed, tabs, sem
):
    own = own_ref[0]
    route = route_ref[...]
    parts = [route if a == 0 else pltpu.roll(route, 128 - 16 * a, 1) for a in range(8)]
    lane = lax.broadcasted_iota(jnp.int32, (64, 128), 1)
    lanef = lane.astype(jnp.float32)
    ctrl = jnp.concatenate(parts, axis=0).astype(jnp.float32)
    counts = jnp.zeros((64, 128), jnp.float32)
    for l in range(16):
        counts = counts + jnp.where(ctrl[:, l : l + 1] == lanef, 1.0, 0.0)
    row = lax.broadcasted_iota(jnp.int32, (64, 64), 0)
    col = lax.broadcasted_iota(jnp.int32, (64, 64), 1)
    before = (col & 7) * 8 + (col >> 3) < (row & 7) * 8 + (row >> 3)
    starts = jnp.dot(
        jnp.where(before, 1.0, 0.0).astype(jnp.bfloat16), counts.astype(jnp.bfloat16),
        preferred_element_type=jnp.float32,
    ).astype(jnp.int32)
    routes = ctrl.astype(jnp.int32)
    within = jnp.zeros((64, 128), jnp.int32)
    for d in range(1, 16):
        same = (pltpu.roll(ctrl, d, 1) == ctrl) & (lane >= d)
        within = within + jnp.where(same, 1, 0)
    slot = jnp.take_along_axis(starts, routes, axis=1) + within
    first = jnp.sum(jnp.where(lane == own, starts, 0), axis=1, keepdims=True)
    place = routes * UNITS + slot + jnp.where(lane == 0, 4096 * first, 0)
    lane8 = lax.broadcasted_iota(jnp.int32, (8, 128), 1)
    packs = []
    for table in (place, slot):
        acc = table[:8]
        for a in range(1, 8):
            part = pltpu.roll(table[8 * a : 8 * a + 8], 16 * a, 1)
            acc = jnp.where(lane8 // 16 == a, part, acc)
        packs.append(acc)
    packed[...] = packs[0]
    copy = pltpu.make_async_copy(packed, tabs, sem)
    copy.start()
    slot_ref[...] = packs[1]
    copy.wait()
    g = lax.rem(own // 4, 8)

    def step(r, carry):
        for a in range(8):
            h = r * 8 + a
            head = tabs[r, a * 16]
            first = head >> 12
            for y in range(8):
                block = lax.rem(g - y + 8, 8)
                for k in range(2):
                    place = tabs[r, a * 16 + 8 * k + block] & 4095
                    out_ref[place] = r_ref[h * 8 + y, k]
            for s in range(2):
                at = jnp.minimum(first + s, CTX - 1)
                for kv in range(2):
                    out_ref[h * UNITS + CTX + 2 * s + kv] = back_ref[at, kv]
            out_ref[h * UNITS + CTX + 4] = picks_ref[jnp.minimum(first, CTX - 1)]
        return carry

    lax.fori_loop(0, 8, step, 0)


def attention_kernel(
    total_ref, recv_ref, q_ref, f0_ref, f1_ref, i0_ref, i1_ref,
    cos_ref, sin_ref, kpos_ref, qpos_ref, out_ref, keys, vals,
):
    total = total_ref[0]
    cos = cos_ref[...]
    sin = sin_ref[...]
    pick0 = i0_ref[...]
    pick1 = i1_ref[...]
    live = lax.broadcasted_iota(jnp.int32, (64, 128), 0) < 2 * total
    k0 = f0_ref[:, :128].astype(jnp.float32)
    k1 = f1_ref[:, :128].astype(jnp.float32)
    v0 = f0_ref[:, 128:].astype(jnp.float32)
    v1 = f1_ref[:, 128:].astype(jnp.float32)
    for i in range(32):
        at0 = pick0 == i
        at1 = pick1 == i
        k = recv_ref[i, :CTX].reshape(64, HD).astype(jnp.float32)
        k = k * cos + pltpu.roll(k, 64, 1) * sin
        k = jnp.where(at0, k0, jnp.where(at1, k1, k))
        keys[i * 64 : i * 64 + 64, :] = k.astype(jnp.bfloat16)
        v = recv_ref[32 + i, :CTX].reshape(64, HD).astype(jnp.float32)
        v = jnp.where(at0, v0, jnp.where(at1, v1, v))
        v = jnp.where(live, v, 0.0)
        vals[i * 64 : i * 64 + 64, :] = v.astype(jnp.bfloat16)
    allowed = kpos_ref[...] <= qpos_ref[...]
    rowlive = lax.broadcasted_iota(jnp.int32, (64, 128), 0) < 2 * total
    factor = math.log2(math.e) / math.sqrt(HD)
    group = 3
    for base in range(0, QH, group):
        heads = range(base, base + group)
        q = jnp.concatenate([q_ref[:, h * HD : h * HD + HD] for h in heads], axis=0)
        s = lax.dot_general(
            q, keys[...], (((1,), (1,)), ((), ())),
            preferred_element_type=jnp.float32,
        )
        s = jnp.where(allowed[None], s.reshape(group, 64, 2048), -1e30)
        peak = jnp.max(s, axis=2, keepdims=True)
        w = jnp.exp2((s - peak) * factor)
        norm = jnp.sum(w, axis=2, keepdims=True)
        mixed = jnp.dot(
            w.astype(jnp.bfloat16).reshape(group * 64, 2048), vals[...],
            preferred_element_type=jnp.float32,
        ).reshape(group, 64, HD)
        out = jnp.where(rowlive[None], mixed / norm, 0.0)
        for n, h in enumerate(heads):
            out_ref[:, h * HD : h * HD + HD] = out[n].astype(jnp.bfloat16)


def update_kernel(pos_ref, x_ref, rows_ref, out_ref):
    row = lax.broadcasted_iota(jnp.int32, (8, 128), 0)

    def step(l, carry):
        at0 = row == pos_ref[2 * l]
        at1 = row == pos_ref[2 * l + 1]
        for head in range(8):
            for kv in range(2):
                lanes = pl.ds(head * 256 + kv * 128, 128)
                pairf = rows_ref[head, l, kv].astype(jnp.float32)
                old = x_ref[l, :, lanes].astype(jnp.float32)
                new = jnp.where(at0, pairf[0:1], jnp.where(at1, pairf[1:2], old))
                out_ref[l, :, lanes] = new.astype(jnp.bfloat16)
        return carry

    lax.fori_loop(0, 16, step, 0)


def local(kv_cache, route, queries, fresh_kv, picked):
    own = lax.axis_index("inst").astype(jnp.int32)
    y = lax.axis_index("tp").astype(jnp.int32)
    me = jnp.stack([own, y])
    bf = jnp.bfloat16
    spread = pl.pallas_call(
        spread_kernel,
        out_shape=jax.ShapeDtypeStruct((512, 2, 2, 128), bf),
        in_specs=[SMEM, VMEM],
        out_specs=VMEM,
        compiler_params=WHOLE,
        name="spread",
    )(me, kv_cache)
    got = lax.all_to_all(
        spread, ("inst", "tp"), split_axis=0, concat_axis=0, tiled=True
    )
    routes = lax.psum(
        lax.dynamic_update_slice(jnp.zeros((1024,), jnp.int32), route, (own * 16,)),
        "inst",
    )

    half = HD // 2
    freqs = jnp.power(
        jnp.float32(THETA), -2.0 * jnp.arange(half, dtype=jnp.float32) / HD
    )
    shift = (jnp.arange(64, dtype=jnp.int32) // 2 * 64).astype(jnp.float32)
    angle = shift[:, None] * freqs[None, :]
    cos = jnp.cos(angle)
    sin = jnp.sin(angle)
    cos2 = jnp.concatenate([cos, cos], axis=1)
    sin2 = jnp.concatenate([-sin, sin], axis=1)

    fk = fresh_kv[:, :HD].astype(jnp.float32)
    swapped = jnp.concatenate([fk[:, half:], fk[:, :half]], axis=1)
    back_k = (fk * cos2 - swapped * sin2).astype(bf)
    back = jnp.stack(
        [back_k.reshape(32, 2, HD), fresh_kv[:, HD:].reshape(32, 2, HD)], axis=1
    )
    pairs = jnp.stack([picked, jnp.roll(picked, -1, axis=0)], axis=1)
    picks = jnp.pad(pairs.astype(bf), ((0, 0), (0, 0), (0, 126)))

    send, slots = pl.pallas_call(
        dispatch_kernel,
        out_shape=(
            jax.ShapeDtypeStruct((64 * UNITS, 2, 128), bf),
            jax.ShapeDtypeStruct((8, 128), jnp.int32),
        ),
        in_specs=[SMEM, VMEM, VMEM, VMEM, VMEM],
        out_specs=(VMEM, VMEM),
        scratch_shapes=DISPATCH_SCRATCH,
        compiler_params=PARAMS,
        name="dispatch",
    )(own[None], routes.reshape(8, 128), got, back, picks)
    recv = lax.all_to_all(
        send.reshape(64, UNITS, 2, 128), "inst", split_axis=0, concat_axis=0,
        tiled=True,
    )

    local_index = jnp.arange(16, dtype=jnp.int32)
    earlier = (route[:, None] == route[None, :]) & (
        local_index[:, None] > local_index[None, :]
    )
    within = jnp.sum(earlier.astype(jnp.int32), axis=1)
    unit = CTX + 2 * within[:, None] + jnp.arange(2, dtype=jnp.int32)
    rows = recv[
        jnp.broadcast_to(route[None, :, None], (8, 16, 2)),
        jnp.broadcast_to(unit[None], (8, 16, 2)),
    ]
    rows = lax.all_to_all(rows, "tp", split_axis=0, concat_axis=0, tiled=True)
    pos = recv[route, CTX + 4, within, :2].astype(jnp.int32).reshape(32) - 8 * y
    updated = pl.pallas_call(
        update_kernel,
        out_shape=jax.ShapeDtypeStruct(kv_cache.shape, bf),
        in_specs=[SMEM, VMEM, VMEM],
        out_specs=VMEM,
        compiler_params=PARAMS,
        name="update",
    )(pos, kv_cache, rows)

    here = routes == own
    total = jnp.sum(here.astype(jnp.int32))
    j32 = jnp.arange(32, dtype=jnp.int32)
    mine = here[None, :] & (slots.reshape(1, 1024) == j32[:, None])
    index = jnp.arange(1024, dtype=jnp.int32) % 16
    lj = jnp.sum(jnp.where(mine, index[None, :], 0), axis=1)
    g = jnp.arange(8, dtype=jnp.int32)[:, None, None, None]
    pair = jnp.arange(4, dtype=jnp.int32)[None, :, None, None]
    j = j32[None, None, :, None]
    r2 = jnp.arange(2, dtype=jnp.int32)
    kpos = j * 64 + ((g - lj[:, None]) & 7) * 8 + pair * 2 + r2
    kpos = jnp.where(j < total, kpos, 1 << 20).reshape(1, 2048)
    qpos = (j32[:, None] * 64 + picked).reshape(64, 1)
    at = ((picked // 8 + lj[:, None]) & 7) * 4 + (picked & 7) // 2
    hit = (picked & 1)[:, None, :] == r2[None, :, None]
    where = jnp.where(hit, at[:, None, :], -1).reshape(64, 2)
    i0 = jnp.broadcast_to(where[:, 0:1], (64, 128))
    i1 = jnp.broadcast_to(where[:, 1:2], (64, 128))
    fr = fresh_kv.reshape(32, 2, 256)
    f0 = jnp.repeat(fr[:, 0], 2, axis=0)
    f1 = jnp.repeat(fr[:, 1], 2, axis=0)
    attn_out = pl.pallas_call(
        attention_kernel,
        out_shape=jax.ShapeDtypeStruct(queries.shape, bf),
        in_specs=[SMEM] + [VMEM] * 10,
        out_specs=VMEM,
        scratch_shapes=ATTEND_SCRATCH,
        compiler_params=PARAMS,
        cost_estimate=pl.CostEstimate(
            flops=4 * 384 * 2048 * 128, bytes_accessed=1500000,
            transcendentals=384 * 2048,
        ),
        name="attend",
    )(
        total[None], recv, queries, f0, f1, i0, i1, cos2, sin2, kpos, qpos,
    )
    return attn_out, updated


def solution(mesh):
    placed = (P("inst", "tp", None), P("inst"), P("inst", "tp"), P("inst", "tp"), P("inst", None))
    return jax.shard_map(
        local,
        mesh=mesh,
        in_specs=placed,
        out_specs=(P("inst", "tp"), P("inst", "tp", None)),
        check_vma=False,
    )
```

time: 155 us -> 161 us (1.039)
  waiting for transfers between devices: 85 us -> 49.3 us
  blocking collectives: 21.4 us -> 40 us
  starting transfers between devices: 30.8 us -> 47.5 us
  other arithmetic: 0.53 us -> 3.42 us
  local copies, waits for them, and re-layouts: 2.67 us -> 5.37 us
    psum x0 -> x1, blocking collectives: none -> 40 us  [local(): lax.psum(lax.dynamic_update_slice(jnp.zeros((1024,), jnp.int32), route, (...]
    all_to_all x1, waiting for transfers between devices: 30.2 us -> 0.01 us  [local(): lax.all_to_all(spread, ('inst', 'tp'), split_axis=0, concat_axis=0, tiled...]
    all_to_all x1 -> x0, blocking collectives: 21.4 us -> none  [local(): got = lax.all_to_all(spread, 'tp', split_axis=0, concat_axis=0, tiled=True)]
    all_to_all x1, starting transfers between devices: 13.3 us -> 24.3 us  [local(): lax.all_to_all(spread, ('inst', 'tp'), split_axis=0, concat_axis=0, tiled...]
    all_to_all x1, waiting for transfers between devices: 52.7 us -> 49.3 us  [local(): lax.all_to_all(send.reshape(64, UNITS, 2, 128), 'inst', split_axis=0, con...]
    all_to_all x1, starting transfers between devices: 8.64 us -> 11.8 us  [local(): rows = lax.all_to_all(rows, 'tp', split_axis=0, concat_axis=0, tiled=True)]
    gather x1 -> x4, local copies, waits for them, and re-layouts: 0.62 us -> 3.31 us  [the longest x1 1.85 us: local(): recv[jnp.broadcast_to(route[None, :, None], (8, 16, 2)), jnp.broadcast_to...]
    all_to_all x1, starting transfers between devices: 8.85 us -> 11.4 us  [local(): lax.all_to_all(send.reshape(64, UNITS, 2, 128), 'inst', split_axis=0, con...]
  transfers between devices with their start and end apart: 3 -> 3, of which waited for: 3 -> 1; matrix products, arithmetic and copies ran while one was open for 2% -> 4% of each run, Pallas kernels for 2% -> 3%
where the time goes in v6:
time: 161 us
  waiting for transfers between devices  49.3 us (31%)
  starting transfers between devices  47.5 us (30%)
  blocking collectives  40 us (25%)
  Pallas kernels  14.4 us (9%)
  local copies, waits for them, and re-layouts  5.37 us (3%)
  other arithmetic  3.42 us (2%)
    all_to_all x1, waiting for transfers between devices, local(): lax.all_to_all(send.reshape(64, UNITS, 2, 128), 'inst', split_axis=0, con...  49.3 us
    psum x1, blocking collectives, local(): lax.psum(lax.dynamic_update_slice(jnp.zeros((1024,), jnp.int32), route, (...  40 us
    all_to_all x1, starting transfers between devices, local(): lax.all_to_all(spread, ('inst', 'tp'), split_axis=0, concat_axis=0, tiled...  24.3 us
    all_to_all x1, starting transfers between devices, local(): rows = lax.all_to_all(rows, 'tp', split_axis=0, concat_axis=0, tiled=True)  11.8 us
    all_to_all x1, starting transfers between devices, local(): lax.all_to_all(send.reshape(64, UNITS, 2, 128), 'inst', split_axis=0, con...  11.4 us
    pallas_call x1, Pallas kernels, local(): pl.pallas_call(dispatch_kernel, out_shape=(jax.ShapeDtypeStruct((64 * UNI...  5.64 us
    pallas_call x1, Pallas kernels, local(): pl.pallas_call(attention_kernel, out_shape=jax.ShapeDtypeStruct(queries.s...  4.54 us
  transfers between devices with their start and end apart: 3, of which 1 were waited for; matrix products, arithmetic and copies ran while one was open for 4% of the time, Pallas kernels for 3%

profile of v6, /device:TPU:1, one launch (start us, length us, event | category | flops | bytes accessed | tf_op | source)
XLA Modules:
  0.0 161.0 jit_solution(14367625022543452197)
XLA Ops:
  0.7 0.6 pad_add_fusion.own_ref
  1.3 2.5 %spread.1 = bf16[512,2,2,128]{3,2,1,0:T(2,128)(2,1)} custom-call(s32[2]{0:T(128)} %pad_add_fusion.own_ref, bf16[16,8,2048]{2,1,0:T(8,128)(2,1)} %x_ref.3), custom_call_target="tpu_custom_call" | custom-call | tf_op jit(solution)/shard_map/spread/pallas_call | solution.py:184
  3.8 24.3 %all-to-all-start = ((bf16[512,2,2,128]{3,2,1,0:T(2,128)(2,1)}), bf16[512,2,2,128]{3,2,1,0:T(2,128)(2,1)S(1)}, u32[]{:S(2)}, u32[]{:S(2)}) async-start(bf16[512,2,2,128]{3,2,1,0:T(2,128)(2,1)} %spread.1), calls=%async_computation | async-start | bytes 1048576 | tf_op jit(solution)/shard_map/all_to_all | solution.py:192
  28.2 0.1 maximum_bitcast_fusion
  28.3 0.1 copy.31
  28.5 0.2 dynamic_update_slice.3
  28.7 40.0 %psum.7 = s32[1024]{0:T(1024)S(1)} all-reduce(s32[1024]{0:T(1024)S(1)} %dynamic_update_slice.3), channel_id=1, replica_groups=mesh['inst'=64,'tp'=8] {'inst'}, use_global_device_ids=true, to_apply=%region_0.0 | all-reduce | flops 1024 | bytes 8192 | tf_op jit(solution)/shard_map/psum | solution.py:195
  68.8 0.2 fusion.3
  69.0 0.1 fusion.2
  69.2 5.6 %dispatch.1 = (bf16[2368,2,128]{2,1,0:T(2,128)(2,1)}, s32[8,128]{1,0:T(8,128)S(1)}) custom-call(s32[1]{0:T(128)} %bitcast.1.own_ref, s32[8,128]{1,0:T(8,128)S(1)} %bitcast.43, bf16[512,2,2,128]{3,2,1,0:T(2,128)(2,1)S(1)} %all-to-all-done.r_ref, bf16[32,2,2,128]{3,2,1,0:T(2,128)(2,1)S(1)} %pad_maximum_fusion.2.back_ref, bf16[32,2,128]{2,1,0:T(2,128)(2,1)S(1)} %pad.4.picks_ref), custom_call_target="tpu_custom_call" | custom-call | tf_op jit(solution)/shard_map/dispatch/pallas_call | solution.py:220
  74.8 11.4 %all-to-all-start.1 = ((bf16[64,37,2,128]{3,2,1,0:T(2,128)(2,1)}), bf16[64,37,2,128]{3,2,1,0:T(2,128)(2,1)S(1)}, u32[]{:S(2)}, u32[]{:S(2)}) async-start(bf16[64,37,2,128]{3,2,1,0:T(2,128)(2,1)} %bitcast.9), calls=%async_computation.1 | async-start | bytes 2424832 | tf_op jit(solution)/shard_map/all_to_all | solution.py:232
  86.5 0.1 eq.59
  86.6 0.1 eq.61
  86.7 0.1 copy.32
  86.9 0.2 convert_reduce_fusion
  87.2 0.1 shift-left_or_fusion
  87.3 0.1 reshape.224
  87.5 0.7 convert_reduce_fusion.1
  88.2 0.6 iota_compare_fusion.2
  89.0 0.1 select_reduce_fusion
  89.2 0.1 broadcast_in_dim.121
  89.4 0.2 add_select_fusion
  89.6 0.3 select_n.101.kpos_ref
  90.0 49.3 %all-to-all-done.1.recv_ref = bf16[64,37,2,128]{3,2,1,0:T(2,128)(2,1)S(1)} async-done(((bf16[64,37,2,128]{3,2,1,0:T(2,128)(2,1)}), bf16[64,37,2,128]{3,2,1,0:T(2,128)(2,1)S(1)}, u32[]{:S(2)}, u32[]{:S(2)}) %all-to-all-start.1) | async-done | bytes 1212448 | tf_op jit(solution)/shard_map/all_to_all | solution.py:232
  139.3 1.9 %gather_fusion = bf16[256,2,128]{2,1,0:T(2,128)(2,1)} fusion(bf16[64,37,2,128]{3,2,1,0:T(2,128)(2,1)S(1)} %all-to-all-done.1.recv_ref, s32[256]{0:T(256)S(1)} %reshape.224), kind=kCustom, calls=%fused_computation | custom fusion | bytes 264192 | tf_op jit(solution)/shard_map/gather | solution.py:243
  141.2 11.8 %all-to-all-start.2 = ((bf16[8,16,2,2,128]{4,3,2,1,0:T(2,128)(2,1)}), bf16[8,16,2,2,128]{4,3,2,1,0:T(2,128)(2,1)S(1)}, u32[]{:S(2)}, u32[]{:S(2)}) async-start(bf16[8,16,2,2,128]{4,3,2,1,0:T(2,128)(2,1)} %bitcast.19), calls=%async_computation.2 | async-start | bytes 262144 | tf_op jit(solution)/shard_map/all_to_all | solution.py:247
  153.0 0.7 gather_fusion.2
  153.7 0.7 gather_fusion.1
  154.4 0.1 copy.34
  154.5 0.1 sub.60.pos_ref
  154.8 4.5 %attend.1 = bf16[64,768]{1,0:T(8,128)(2,1)} custom-call(s32[1]{0:T(128)} %bitcast.total_ref, bf16[64,37,2,128]{3,2,1,0:T(2,128)(2,1)S(1)} %all-to-all-done.1.recv_ref, bf16[64,768]{1,0:T(8,128)(2,1)S(1)} %copy-done.1, bf16[64,256]{1,0:T(8,128)(2,1)S(1)} %reshape.221.f0_ref, bf16[64,256]{1,0:T(8,128)(2,1)S(1)} %reshape.222.f1_ref, ...), custom_call_target="tpu_custom_call" | custom-call | flops 402653184 | bytes 1500000 | tf_op jit(solution)/shard_map/attend/pallas_call | solution.py:279
  159.3 1.7 %update.1 = bf16[16,8,2048]{2,1,0:T(8,128)(2,1)} custom-call(s32[32]{0:T(128)S(1)} %sub.60.pos_ref, bf16[16,8,2048]{2,1,0:T(8,128)(2,1)S(1)} %copy-done, bf16[8,16,2,2,128]{4,3,2,1,0:T(2,128)(2,1)S(1)} %all-to-all-done.2.rows_ref), custom_call_target="tpu_custom_call" | custom-call | tf_op jit(solution)/shard_map/update/pallas_call | solution.py:249
  (57 shorter events, 1.1 us)
Async XLA Ops:
  0.6 27.5 %copy-start.3 = (s32[32,2]{0,1:T(2,128)S(1)}, s32[32,2]{0,1:T(2,128)}, u32[]{:S(2)}) copy-start(s32[32,2]{0,1:T(2,128)} %param.9) | copy-start | bytes 772
  0.6 27.8 %copy-start.4 = (s32[16]{0:T(128)S(1)}, s32[16]{0:T(128)}, u32[]{:S(2)}) copy-start(s32[16]{0:T(128)} %param.6) | copy-start | bytes 196
  0.7 68.1 %copy-start.2 = (bf16[64,256]{1,0:T(8,128)(2,1)S(1)}, bf16[64,256]{1,0:T(8,128)(2,1)}, u32[]{:S(2)}) copy-start(bf16[64,256]{1,0:T(8,128)(2,1)} %param.8) | copy-start | bytes 98308
  3.8 65.4 %all-to-all-start = ((bf16[512,2,2,128]{3,2,1,0:T(2,128)(2,1)}), bf16[512,2,2,128]{3,2,1,0:T(2,128)(2,1)S(1)}, u32[]{:S(2)}, u32[]{:S(2)}) async-start(bf16[512,2,2,128]{3,2,1,0:T(2,128)(2,1)} %spread.1), calls=%async_computation | async-start | bytes 1048576 | tf_op jit(solution)/shard_map/all_to_all | solution.py:192
  74.8 14.1 %copy-start.5 = (s32[4]{0:T(128)S(1)}, s32[4]{0:T(128)}, u32[]{:S(2)}) copy-start(s32[4]{0:T(128)} %constant.109) | copy-start | bytes 52
  74.8 14.0 %copy-start.6 = (s32[4]{0:T(128)S(1)}, s32[4]{0:T(128)}, u32[]{:S(2)}) copy-start(s32[4]{0:T(128)} %constant.107) | copy-start | bytes 52
  74.8 64.5 %all-to-all-start.1 = ((bf16[64,37,2,128]{3,2,1,0:T(2,128)(2,1)}), bf16[64,37,2,128]{3,2,1,0:T(2,128)(2,1)S(1)}, u32[]{:S(2)}, u32[]{:S(2)}) async-start(bf16[64,37,2,128]{3,2,1,0:T(2,128)(2,1)} %bitcast.9), calls=%async_computation.1 | async-start | bytes 2424832 | tf_op jit(solution)/shard_map/all_to_all | solution.py:232
  89.6 65.1 %copy-start.1 = (bf16[64,768]{1,0:T(8,128)(2,1)S(1)}, bf16[64,768]{1,0:T(8,128)(2,1)}, u32[]{:S(2)}) copy-start(bf16[64,768]{1,0:T(8,128)(2,1)} %q_ref.1) | copy-start | bytes 294916
  141.2 18.2 %all-to-all-start.2 = ((bf16[8,16,2,2,128]{4,3,2,1,0:T(2,128)(2,1)}), bf16[8,16,2,2,128]{4,3,2,1,0:T(2,128)(2,1)S(1)}, u32[]{:S(2)}, u32[]{:S(2)}) async-start(bf16[8,16,2,2,128]{4,3,2,1,0:T(2,128)(2,1)} %bitcast.19), calls=%async_computation.2 | async-start | bytes 262144 | tf_op jit(solution)/shard_map/all_to_all | solution.py:247
  153.7 5.6 %copy-start = (bf16[16,8,2048]{2,1,0:T(8,128)(2,1)S(1)}, bf16[16,8,2048]{2,1,0:T(8,128)(2,1)}, u32[]{:S(2)}) copy-start(bf16[16,8,2048]{2,1,0:T(8,128)(2,1)} %x_ref.3) | copy-start | bytes 1572868

commit v7 on v5

--- a/solution.py
+++ b/solution.py
@@ -12,7 +12,8 @@
 QH = 6
 THETA = 1000000.0
 CTX = 32
-UNITS = 36
+UNITS = 32
+STEP = (0, 1, 2, -1)
 VMEM = pl.BlockSpec(memory_space=pltpu.VMEM)
 SMEM = pl.BlockSpec(memory_space=pltpu.SMEM)
 DISPATCH_SCRATCH = [
@@ -56,7 +57,9 @@
     lax.fori_loop(0, 16, step, 0)
 
 
-def dispatch_kernel(own_ref, r_ref, back_ref, out_ref, tab_ref, total_ref, packed, tabs, sem):
+def dispatch_kernel(
+    own_ref, r_ref, back_ref, out_ref, ret_ref, tab_ref, total_ref, packed, tabs, sem
+):
     own = own_ref[0]
     ctrl = r_ref[:, 16, 0, :].astype(jnp.float32)
     lane = lax.broadcasted_iota(jnp.int32, (64, 128), 1)
@@ -74,11 +77,12 @@
         within = within + jnp.where(same, 1, 0)
     slot = jnp.take_along_axis(starts, routes, axis=1) + within
     place = routes * UNITS + slot
-    ret = routes * UNITS + CTX + 2 * within
-    tab_ref[...] = jnp.where(lane < 16, ret, pltpu.roll(slot, 16, 1))
-    own_lane = lane == own
-    first = jnp.sum(jnp.where(own_lane, starts, 0), axis=1, keepdims=True)
-    table = place + 4096 * first
+    tab_ref[...] = jnp.where(lane < 16, within, pltpu.roll(slot, 16, 1))
+    own_z = lax.rem(own, 16)
+    own_x = own // 16
+    column = jnp.where(lane < 4, lane * 16 + own_z, 0)
+    first = jnp.take_along_axis(starts, column, axis=1)
+    table = place + 4096 * jnp.where(lane < 4, first, 0)
     lane8 = lax.broadcasted_iota(jnp.int32, (8, 128), 1)
     acc = jnp.zeros((8, 128), jnp.int32)
     for a in range(8):
@@ -89,34 +93,38 @@
     packed[...] = acc
     copy = pltpu.make_async_copy(packed, tabs, sem)
     copy.start()
-    total = jnp.sum(jnp.where(own_lane, counts, 0.0)).astype(jnp.int32)
+    total = jnp.sum(jnp.where(lane == own, counts, 0.0)).astype(jnp.int32)
     total_ref[...] = jnp.full((1, 128), total, jnp.int32)
     copy.wait()
 
     def step(a, carry):
         for r in range(8):
             h = a * 8 + r
-            both = [tabs[r, a * 16 + l] for l in range(16)]
-            place = [v & 4095 for v in both]
+            place = [tabs[r, a * 16 + l] for l in range(16)]
             units = [r_ref[h, l] for l in range(16)]
-            first = both[0] >> 12
-            slots = [jnp.minimum(first + s, CTX - 1) for s in range(2)]
-            backs = [back_ref[slots[s], kv] for s in range(2) for kv in range(2)]
             for l in range(16):
-                out_ref[place[l]] = units[l]
-            for n in range(4):
-                out_ref[h * UNITS + CTX + n] = backs[n]
+                at = place[l] & 4095 if l < 4 else place[l]
+                out_ref[at] = units[l]
         return carry
 
     lax.fori_loop(0, 8, step, 0)
-
-
-def collect_kernel(info_ref, recv_ref, out_ref):
-    for l in range(16):
-        for kv in range(2):
-            unit = recv_ref[info_ref[l] + kv]
-            for t in range(8):
-                out_ref[t * 32 + l * 2 + kv] = unit
+    sign = own_ref[1]
+
+    def returns(u, carry):
+        for v in range(4):
+            z = lax.rem(own_z + sign * (4 * u + STEP[v]) + 32, 16)
+            h = own_x * 16 + z
+            for x in range(4):
+                away = lax.rem(own_x - x + 4, 4)
+                first = tabs[lax.rem(h, 8), h // 8 * 16 + x] >> 12
+                for n in range(2):
+                    at = jnp.minimum(first + n, CTX - 1)
+                    for kv in range(2):
+                        out = (v * 4 + u) * 16 + x * 4 + n * 2 + kv
+                        ret_ref[out] = back_ref[away, at, kv]
+        return carry
+
+    lax.fori_loop(0, 4, returns, 0)
 
 
 def attention_kernel(
@@ -201,8 +209,7 @@
         compiler_params=WHOLE,
         name="spread",
     )(kv_cache, route, picked.T)
-    got = lax.all_to_all(spread, "tp", split_axis=0, concat_axis=0, tiled=True)
-    got = lax.all_to_all(got, "inst", split_axis=0, concat_axis=0, tiled=True)
+    halfway = lax.all_to_all(spread, "tp", split_axis=0, concat_axis=0, tiled=True)
 
     half = HD // 2
     freqs = jnp.power(
@@ -222,34 +229,53 @@
         [back_k.reshape(32, 2, HD), fresh_kv[:, HD:].reshape(32, 2, HD)], axis=1
     )
 
-    send, tab, total = pl.pallas_call(
+    heads = tuple(range(8))
+    mesh_axes = ("inst", "tp")
+
+    def shifted(values, x_step, z_step):
+        pairs = []
+        for x in range(4):
+            for z in range(16):
+                for t in heads:
+                    to = (x + x_step) % 4 * 16 + (z + z_step * (1 - 2 * (t % 2))) % 16
+                    pairs.append(((x * 16 + z) * 8 + t, to * 8 + t))
+        return lax.ppermute(values, mesh_axes, pairs)
+
+    back, halfway = lax.optimization_barrier((back, halfway))
+    got = lax.all_to_all(halfway, "inst", split_axis=0, concat_axis=0, tiled=True)
+    backs = jnp.stack([back] + [shifted(back, n, 0) for n in (1, 2, 3)])
+
+    sign = 1 - 2 * (y % 2)
+    send, ret, tab, total = pl.pallas_call(
         dispatch_kernel,
         out_shape=(
             jax.ShapeDtypeStruct((64 * UNITS, 2, 128), bf),
+            jax.ShapeDtypeStruct((256, 2, 128), bf),
             jax.ShapeDtypeStruct((64, 128), jnp.int32),
             jax.ShapeDtypeStruct((1, 128), jnp.int32),
         ),
         in_specs=[SMEM, VMEM, VMEM],
-        out_specs=(VMEM, VMEM, VMEM),
+        out_specs=(VMEM, VMEM, VMEM, VMEM),
         scratch_shapes=DISPATCH_SCRATCH,
         compiler_params=PARAMS,
         name="dispatch",
-    )(own[None], got, back)
+    )(jnp.stack([own, sign]), got, backs)
     recv = lax.all_to_all(
         send.reshape(64, UNITS, 2, 128), "inst", split_axis=0, concat_axis=0,
         tiled=True,
     )
 
+    ret = ret.reshape(4, 4, 16, 2, 128)
+    ret = [ret[0]] + [shifted(ret[v], 0, STEP[v]) for v in (1, 2, 3)]
+    ret = [jnp.stack([part[u] for part in ret]) for u in range(4)]
+    ret = jnp.stack([ret[0]] + [shifted(ret[u], 0, 4 * u) for u in (1, 2, 3)])
     mine = lax.dynamic_index_in_dim(tab, own, 0, keepdims=False)
-    rows = pl.pallas_call(
-        collect_kernel,
-        out_shape=jax.ShapeDtypeStruct((256, 2, 128), bf),
-        in_specs=[SMEM, VMEM],
-        out_specs=VMEM,
-        compiler_params=PARAMS,
-        name="collect",
-    )(mine[:16], recv.reshape(64 * UNITS, 2, 128)).reshape(8, 16, 2, 2, 128)
-    rows = lax.all_to_all(rows, "tp", split_axis=0, concat_axis=0, tiled=True)
+    dz = (sign * (own % 16 - route % 16)) & 15
+    v = dz & 3
+    u = ((dz + 1) // 4) & 3
+    at = (u * 4 + v) * 8 + route // 16 * 2 + mine[:16]
+    rows = ret.reshape(128, 2, 2, 128)[at]
+    rows = lax.all_gather(rows, "tp", axis=0, tiled=False)
     picks = got[:, 16, 1, :64].reshape(64, 2, 32).astype(jnp.int32)
     pos = picks[route, :, mine[16:32]].reshape(32) - 8 * y
     updated = pl.pallas_call(

time: 155 us -> 175 us (1.13)
  starting transfers between devices: 30.8 us -> 75.5 us
  waiting for transfers between devices: 85 us -> 63.6 us
  blocking collectives: 21.4 us -> 16.1 us
  local copies, waits for them, and re-layouts: 2.67 us -> 4.77 us
    all_to_all x1, waiting for transfers between devices: 52.7 us -> 0.01 us  [local(): lax.all_to_all(send.reshape(64, UNITS, 2, 128), 'inst', split_axis=0, con...]
    ppermute x0 -> x9, starting transfers between devices: none -> 42.1 us  [shifted(): return lax.ppermute(values, mesh_axes, pairs)]
    ppermute x0 -> x9, waiting for transfers between devices: none -> 37.4 us  [shifted(): return lax.ppermute(values, mesh_axes, pairs)]
    all_to_all x1 -> x0, blocking collectives: 21.4 us -> none  [local(): got = lax.all_to_all(spread, 'tp', split_axis=0, concat_axis=0, tiled=True)]
    all_gather x0 -> x1, blocking collectives: none -> 16.1 us  [local(): rows = lax.all_gather(rows, 'tp', axis=0, tiled=False)]
    all_to_all x2, waiting for transfers between devices: 32.3 us -> 26.2 us  [the longest x1 16.7 us: local(): lax.all_to_all(halfway, 'inst', split_axis=0, concat_axis=0, tiled=True)]
    all_to_all x2, starting transfers between devices: 21.9 us -> 24.4 us  [the longest x1 13.3 us: local(): lax.all_to_all(halfway, 'inst', split_axis=0, concat_axis=0, tiled=True)]
  transfers between devices with their start and end apart: 3 -> 12, of which waited for: 3 -> 7; matrix products, arithmetic and copies ran while one was open for 2% -> 3% of each run, Pallas kernels for 2% -> 1%
where the time goes in v7:
time: 175 us
  starting transfers between devices  75.5 us (43%)
  waiting for transfers between devices  63.6 us (36%)
  blocking collectives  16.1 us (9%)
  Pallas kernels  12.1 us (7%)
  local copies, waits for them, and re-layouts  4.77 us (3%)
    ppermute x9, starting transfers between devices, shifted(): return lax.ppermute(values, mesh_axes, pairs)  42.1 us
    ppermute x9, waiting for transfers between devices, shifted(): return lax.ppermute(values, mesh_axes, pairs)  37.4 us
    all_to_all x1, waiting for transfers between devices, local(): lax.all_to_all(halfway, 'inst', split_axis=0, concat_axis=0, tiled=True)  16.7 us
    all_gather x1, blocking collectives, local(): rows = lax.all_gather(rows, 'tp', axis=0, tiled=False)  16.1 us
    all_to_all x1, starting transfers between devices, local(): lax.all_to_all(halfway, 'inst', split_axis=0, concat_axis=0, tiled=True)  13.3 us
    all_to_all x1, starting transfers between devices, local(): lax.all_to_all(spread, 'tp', split_axis=0, concat_axis=0, tiled=True)  11.1 us
    all_to_all x1, waiting for transfers between devices, local(): lax.all_to_all(spread, 'tp', split_axis=0, concat_axis=0, tiled=True)  9.55 us
    all_to_all x1, starting transfers between devices, local(): lax.all_to_all(send.reshape(64, UNITS, 2, 128), 'inst', split_axis=0, con...  9.08 us
  transfers between devices with their start and end apart: 12, of which 7 were waited for; matrix products, arithmetic and copies ran while one was open for 3% of the time, Pallas kernels for 1%

profile of v7, /device:TPU:1, one launch (start us, length us, event | category | flops | bytes accessed | tf_op | source)
XLA Modules:
  0.0 174.6 jit_solution(4096261671883770235)
XLA Ops:
  0.6 2.6 %spread.1 = bf16[64,17,2,128]{3,2,1,0:T(2,128)(2,1)} custom-call(bf16[16,8,2048]{2,1,0:T(8,128)(2,1)} %x_ref.3, s32[16]{0:T(128)} %route_ref.1, s32[2,32]{1,0:T(2,128)} %bitcast.79), custom_call_target="tpu_custom_call" | custom-call | tf_op jit(solution)/shard_map/spread/pallas_call | solution.py:204
  3.3 11.1 %all-to-all-start = ((bf16[64,17,2,128]{3,2,1,0:T(2,128)(2,1)}), bf16[64,17,2,128]{3,2,1,0:T(2,128)(2,1)}, u32[]{:S(2)}, u32[]{:S(2)}) async-start(bf16[64,17,2,128]{3,2,1,0:T(2,128)(2,1)} %spread.1), calls=%async_computation | async-start | bytes 1114112 | tf_op jit(solution)/shard_map/all_to_all | solution.py:212
  14.4 0.2 fusion.2
  14.8 9.5 %all-to-all-done = bf16[64,17,2,128]{3,2,1,0:T(2,128)(2,1)} async-done(((bf16[64,17,2,128]{3,2,1,0:T(2,128)(2,1)}), bf16[64,17,2,128]{3,2,1,0:T(2,128)(2,1)}, u32[]{:S(2)}, u32[]{:S(2)}) %all-to-all-start) | async-done | bytes 557088 | tf_op jit(solution)/shard_map/all_to_all | solution.py:212
  24.3 13.3 %all-to-all-start.1 = ((bf16[64,17,2,128]{3,2,1,0:T(2,128)(2,1)}), bf16[64,17,2,128]{3,2,1,0:T(2,128)(2,1)S(1)}, u32[]{:S(2)}, u32[]{:S(2)}) async-start(bf16[64,17,2,128]{3,2,1,0:T(2,128)(2,1)} %all-to-all-done), calls=%async_computation.1 | async-start | bytes 1114112 | tf_op jit(solution)/shard_map/all_to_all | solution.py:245
  37.6 4.3 %collective-permute-start.2 = (bf16[32,2,2,128]{3,2,1,0:T(2,128)(2,1)S(1)}, bf16[32,2,2,128]{3,2,1,0:T(2,128)(2,1)S(1)}, u32[]{:S(2)}, u32[]{:S(2)}) collective-permute-start(bf16[32,2,2,128]{3,2,1,0:T(2,128)(2,1)S(1)} %pad_maximum_fusion.4), channel_id=1, source_target_pairs={{0,384},{1,385},{2,386},{3,387},{4,388},{5,389},{6,390},{7,391},{8... | collective-permute-start | bytes 98312 | tf_op jit(solution)/shard_map/ppermute | solution.py:242
  41.9 2.3 %collective-permute-start.1 = (bf16[32,2,2,128]{3,2,1,0:T(2,128)(2,1)S(1)}, bf16[32,2,2,128]{3,2,1,0:T(2,128)(2,1)S(1)}, u32[]{:S(2)}, u32[]{:S(2)}) collective-permute-start(bf16[32,2,2,128]{3,2,1,0:T(2,128)(2,1)S(1)} %pad_maximum_fusion.4), channel_id=1, source_target_pairs={{0,256},{1,257},{2,258},{3,259},{4,260},{5,261},{6,262},{7,263},{8... | collective-permute-start | bytes 98312 | tf_op jit(solution)/shard_map/ppermute | solution.py:242
  44.2 2.6 %collective-permute-start = (bf16[32,2,2,128]{3,2,1,0:T(2,128)(2,1)S(1)}, bf16[32,2,2,128]{3,2,1,0:T(2,128)(2,1)S(1)}, u32[]{:S(2)}, u32[]{:S(2)}) collective-permute-start(bf16[32,2,2,128]{3,2,1,0:T(2,128)(2,1)S(1)} %pad_maximum_fusion.4), channel_id=1, source_target_pairs={{0,128},{1,129},{2,130},{3,131},{4,132},{5,133},{6,134},{7,135},{8... | collective-permute-start | bytes 98312 | tf_op jit(solution)/shard_map/ppermute | solution.py:242
  46.9 1.7 collective-permute-done.1
  48.6 2.4 %collective-permute-done = bf16[32,2,2,128]{3,2,1,0:T(2,128)(2,1)S(1)} collective-permute-done((bf16[32,2,2,128]{3,2,1,0:T(2,128)(2,1)S(1)}, bf16[32,2,2,128]{3,2,1,0:T(2,128)(2,1)S(1)}, u32[]{:S(2)}, u32[]{:S(2)}) %collective-permute-start) | collective-permute-done | bytes 32800 | tf_op jit(solution)/shard_map/ppermute | solution.py:242
  50.9 0.2 pad_maximum_fusion.back_ref
  51.2 16.7 %all-to-all-done.1.r_ref = bf16[64,17,2,128]{3,2,1,0:T(2,128)(2,1)S(1)} async-done(((bf16[64,17,2,128]{3,2,1,0:T(2,128)(2,1)}), bf16[64,17,2,128]{3,2,1,0:T(2,128)(2,1)S(1)}, u32[]{:S(2)}, u32[]{:S(2)}) %all-to-all-start.1) | async-done | bytes 557088 | tf_op jit(solution)/shard_map/all_to_all | solution.py:245
  67.9 4.9 %dispatch.1 = (bf16[2048,2,128]{2,1,0:T(2,128)(2,1)}, bf16[256,2,128]{2,1,0:T(2,128)(2,1)S(1)}, s32[64,128]{1,0:T(8,128)S(1)}, s32[1,128]{1,0:T(1,128)S(1)}) custom-call(s32[2]{0:T(128)S(1)} %pad_add_fusion.own_ref, bf16[64,17,2,128]{3,2,1,0:T(2,128)(2,1)S(1)} %all-to-all-done.1.r_ref, bf16[4,32,2,2,128]{4,3,2,1,0:T(2,128)(2,1)S(1)} %pad_maximum_fusion.back_ref), custom_call_target="tpu_custom_call" | custom-call | tf_op jit(solution)/shard_map/dispatch/pallas_call | solution.py:249
  72.8 9.1 %all-to-all-start.2 = ((bf16[64,32,2,128]{3,2,1,0:T(2,128)(2,1)}), bf16[64,32,2,128]{3,2,1,0:T(2,128)(2,1)S(1)}, u32[]{:S(2)}, u32[]{:S(2)}) async-start(bf16[64,32,2,128]{3,2,1,0:T(2,128)(2,1)} %bitcast.11), calls=%async_computation.2 | async-start | bytes 2097152 | tf_op jit(solution)/shard_map/all_to_all | solution.py:263
  82.0 0.7 copy-done.3
  83.7 2.9 %collective-permute-start.5 = (bf16[4,16,2,128]{3,2,1,0:T(2,128)(2,1)S(1)}, bf16[4,16,2,128]{3,2,1,0:T(2,128)(2,1)S(1)}, u32[]{:S(2)}, u32[]{:S(2)}) collective-permute-start(bf16[4,16,2,128]{3,2,1,0:T(2,128)(2,1)S(1)} %bitcast.72), channel_id=1, source_target_pairs={{0,120},{1,9},{2,122},{3,11},{4,124},{5,13},{6,126},{7,15},{8,0},{... | collective-permute-start | bytes 98312 | tf_op jit(solution)/shard_map/ppermute | solution.py:242
  86.6 3.6 %collective-permute-start.3 = (bf16[4,16,2,128]{3,2,1,0:T(2,128)(2,1)S(1)}, bf16[4,16,2,128]{3,2,1,0:T(2,128)(2,1)S(1)}, u32[]{:S(2)}, u32[]{:S(2)}) collective-permute-start(bf16[4,16,2,128]{3,2,1,0:T(2,128)(2,1)S(1)} %bitcast.71), channel_id=1, source_target_pairs={{0,8},{1,121},{2,10},{3,123},{4,12},{5,125},{6,14},{7,127},{8,16},... | collective-permute-start | bytes 98312 | tf_op jit(solution)/shard_map/ppermute | solution.py:242
  90.2 3.8 %collective-permute-start.4 = (bf16[4,16,2,128]{3,2,1,0:T(2,128)(2,1)S(1)}, bf16[4,16,2,128]{3,2,1,0:T(2,128)(2,1)S(1)}, u32[]{:S(2)}, u32[]{:S(2)}) collective-permute-start(bf16[4,16,2,128]{3,2,1,0:T(2,128)(2,1)S(1)} %bitcast.70), channel_id=1, source_target_pairs={{0,16},{1,113},{2,18},{3,115},{4,20},{5,117},{6,22},{7,119},{8,24}... | collective-permute-start | bytes 98312 | tf_op jit(solution)/shard_map/ppermute | solution.py:242
  94.1 1.0 copy.30
  95.1 0.6 copy-done.4
  95.8 0.6 gather_fusion
  96.6 28.9 %collective-permute-done.5 = bf16[4,16,2,128]{3,2,1,0:T(2,128)(2,1)S(1)} collective-permute-done((bf16[4,16,2,128]{3,2,1,0:T(2,128)(2,1)S(1)}, bf16[4,16,2,128]{3,2,1,0:T(2,128)(2,1)S(1)}, u32[]{:S(2)}, u32[]{:S(2)}) %collective-permute-start.5) | collective-permute-done | bytes 32800 | tf_op jit(solution)/shard_map/ppermute | solution.py:242
  125.6 2.2 %collective-permute-done.4 = bf16[4,16,2,128]{3,2,1,0:T(2,128)(2,1)S(1)} collective-permute-done((bf16[4,16,2,128]{3,2,1,0:T(2,128)(2,1)S(1)}, bf16[4,16,2,128]{3,2,1,0:T(2,128)(2,1)S(1)}, u32[]{:S(2)}, u32[]{:S(2)}) %collective-permute-start.4) | collective-permute-done | bytes 32800 | tf_op jit(solution)/shard_map/ppermute | solution.py:242
  127.9 8.2 %collective-permute-start.6 = (bf16[4,16,2,128]{3,2,1,0:T(2,128)(2,1)S(1)}, bf16[4,16,2,128]{3,2,1,0:T(2,128)(2,1)S(1)}, u32[]{:S(2)}, u32[]{:S(2)}) collective-permute-start(bf16[4,16,2,128]{3,2,1,0:T(2,128)(2,1)S(1)} %pad_maximum_fusion.5), channel_id=1, source_target_pairs={{0,32},{1,97},{2,34},{3,99},{4,36},{5,101},{6,38},{7,103},{8,40},{... | collective-permute-start | bytes 98312 | tf_op jit(solution)/shard_map/ppermute | solution.py:242
  136.2 7.1 %collective-permute-start.7 = (bf16[4,16,2,128]{3,2,1,0:T(2,128)(2,1)S(1)}, bf16[4,16,2,128]{3,2,1,0:T(2,128)(2,1)S(1)}, u32[]{:S(2)}, u32[]{:S(2)}) collective-permute-start(bf16[4,16,2,128]{3,2,1,0:T(2,128)(2,1)S(1)} %pad_maximum_fusion.6), channel_id=1, source_target_pairs={{0,64},{1,65},{2,66},{3,67},{4,68},{5,69},{6,70},{7,71},{8,72},{9,... | collective-permute-start | bytes 98312 | tf_op jit(solution)/shard_map/ppermute | solution.py:242
  143.3 7.3 %collective-permute-start.8 = (bf16[4,16,2,128]{3,2,1,0:T(2,128)(2,1)S(1)}, bf16[4,16,2,128]{3,2,1,0:T(2,128)(2,1)S(1)}, u32[]{:S(2)}, u32[]{:S(2)}) collective-permute-start(bf16[4,16,2,128]{3,2,1,0:T(2,128)(2,1)S(1)} %pad_maximum_fusion.7), channel_id=1, source_target_pairs={{0,96},{1,33},{2,98},{3,35},{4,100},{5,37},{6,102},{7,39},{8,104},... | collective-permute-start | bytes 98312 | tf_op jit(solution)/shard_map/ppermute | solution.py:242
  150.7 2.2 %collective-permute-done.8 = bf16[4,16,2,128]{3,2,1,0:T(2,128)(2,1)S(1)} collective-permute-done((bf16[4,16,2,128]{3,2,1,0:T(2,128)(2,1)S(1)}, bf16[4,16,2,128]{3,2,1,0:T(2,128)(2,1)S(1)}, u32[]{:S(2)}, u32[]{:S(2)}) %collective-permute-start.8) | collective-permute-done | bytes 32800 | tf_op jit(solution)/shard_map/ppermute | solution.py:242
  152.9 0.2 pad_maximum_fusion.1
  153.1 0.6 gather_fusion.1
  153.7 16.1 %all-gather = bf16[128,2,2,128]{3,2,1,0:T(2,128)(2,1)S(1)} all-gather(bf16[16,2,2,128]{3,2,1,0:T(2,128)(2,1)S(1)} %gather_fusion.1), channel_id=2, replica_groups=mesh['inst'=64,'tp'=8] {'tp'}, dimensions={0}, use_global_device_ids=true | all-gather | bytes 147456 | tf_op jit(solution)/shard_map/all_gather | solution.py:278
  169.9 1.7 update.1
  171.7 2.9 %attend.1 = bf16[64,768]{1,0:T(8,128)(2,1)} custom-call(s32[1]{0:T(128)S(1)} %bitcast.64, bf16[64,64,128]{2,1,0:T(8,128)(2,1)S(1)} %bitcast.62, bf16[64,768]{1,0:T(8,128)(2,1)S(1)} %copy-done.1, bf16[64,256]{1,0:T(8,128)(2,1)S(1)} %reshape.107.f0_ref, bf16[64,256]{1,0:T(8,128)(2,1)S(1)} %reshape.108.f1_ref, s32[64,128]{1,0:T(8,128)S(1)} %broadcast_in_dim.53.i0_ref, ...), custom_call_target="tpu_custom_call" | custom-call | flops 402653184 | bytes 1500000 | tf_op jit(solution)/shard_map/attend/pallas_call | solution.py:299
  (57 shorter events, 2.0 us)
Async XLA Ops:
  3.2 11.1 %copy-start.2 = (bf16[64,256]{1,0:T(8,128)(2,1)S(1)}, bf16[64,256]{1,0:T(8,128)(2,1)}, u32[]{:S(2)}) copy-start(bf16[64,256]{1,0:T(8,128)(2,1)} %param.8) | copy-start | bytes 98308
  3.3 21.0 %all-to-all-start = ((bf16[64,17,2,128]{3,2,1,0:T(2,128)(2,1)}), bf16[64,17,2,128]{3,2,1,0:T(2,128)(2,1)}, u32[]{:S(2)}, u32[]{:S(2)}) async-start(bf16[64,17,2,128]{3,2,1,0:T(2,128)(2,1)} %spread.1), calls=%async_computation | async-start | bytes 1114112 | tf_op jit(solution)/shard_map/all_to_all | solution.py:212
  24.3 43.6 %all-to-all-start.1 = ((bf16[64,17,2,128]{3,2,1,0:T(2,128)(2,1)}), bf16[64,17,2,128]{3,2,1,0:T(2,128)(2,1)S(1)}, u32[]{:S(2)}, u32[]{:S(2)}) async-start(bf16[64,17,2,128]{3,2,1,0:T(2,128)(2,1)} %all-to-all-done), calls=%async_computation.1 | async-start | bytes 1114112 | tf_op jit(solution)/shard_map/all_to_all | solution.py:245
  37.6 9.3 %collective-permute-start.2 = (bf16[32,2,2,128]{3,2,1,0:T(2,128)(2,1)S(1)}, bf16[32,2,2,128]{3,2,1,0:T(2,128)(2,1)S(1)}, u32[]{:S(2)}, u32[]{:S(2)}) collective-permute-start(bf16[32,2,2,128]{3,2,1,0:T(2,128)(2,1)S(1)} %pad_maximum_fusion.4), channel_id=1, source_target_pairs={{0,384},{1,385},{2,386},{3,387},{4,388},{5,389},{6,390},{7,391},{8... | collective-permute-start | bytes 98312 | tf_op jit(solution)/shard_map/ppermute | solution.py:242
  41.9 6.6 %collective-permute-start.1 = (bf16[32,2,2,128]{3,2,1,0:T(2,128)(2,1)S(1)}, bf16[32,2,2,128]{3,2,1,0:T(2,128)(2,1)S(1)}, u32[]{:S(2)}, u32[]{:S(2)}) collective-permute-start(bf16[32,2,2,128]{3,2,1,0:T(2,128)(2,1)S(1)} %pad_maximum_fusion.4), channel_id=1, source_target_pairs={{0,256},{1,257},{2,258},{3,259},{4,260},{5,261},{6,262},{7,263},{8... | collective-permute-start | bytes 98312 | tf_op jit(solution)/shard_map/ppermute | solution.py:242
  44.2 6.7 %collective-permute-start = (bf16[32,2,2,128]{3,2,1,0:T(2,128)(2,1)S(1)}, bf16[32,2,2,128]{3,2,1,0:T(2,128)(2,1)S(1)}, u32[]{:S(2)}, u32[]{:S(2)}) collective-permute-start(bf16[32,2,2,128]{3,2,1,0:T(2,128)(2,1)S(1)} %pad_maximum_fusion.4), channel_id=1, source_target_pairs={{0,128},{1,129},{2,130},{3,131},{4,132},{5,133},{6,134},{7,135},{8... | collective-permute-start | bytes 98312 | tf_op jit(solution)/shard_map/ppermute | solution.py:242
  72.8 98.7 %all-to-all-start.2 = ((bf16[64,32,2,128]{3,2,1,0:T(2,128)(2,1)}), bf16[64,32,2,128]{3,2,1,0:T(2,128)(2,1)S(1)}, u32[]{:S(2)}, u32[]{:S(2)}) async-start(bf16[64,32,2,128]{3,2,1,0:T(2,128)(2,1)} %bitcast.11), calls=%async_computation.2 | async-start | bytes 2097152 | tf_op jit(solution)/shard_map/all_to_all | solution.py:263
  81.9 0.7 copy-start.3
  83.7 41.8 %collective-permute-start.5 = (bf16[4,16,2,128]{3,2,1,0:T(2,128)(2,1)S(1)}, bf16[4,16,2,128]{3,2,1,0:T(2,128)(2,1)S(1)}, u32[]{:S(2)}, u32[]{:S(2)}) collective-permute-start(bf16[4,16,2,128]{3,2,1,0:T(2,128)(2,1)S(1)} %bitcast.72), channel_id=1, source_target_pairs={{0,120},{1,9},{2,122},{3,11},{4,124},{5,13},{6,126},{7,15},{8,0},{... | collective-permute-start | bytes 98312 | tf_op jit(solution)/shard_map/ppermute | solution.py:242
  86.6 38.9 %collective-permute-start.3 = (bf16[4,16,2,128]{3,2,1,0:T(2,128)(2,1)S(1)}, bf16[4,16,2,128]{3,2,1,0:T(2,128)(2,1)S(1)}, u32[]{:S(2)}, u32[]{:S(2)}) collective-permute-start(bf16[4,16,2,128]{3,2,1,0:T(2,128)(2,1)S(1)} %bitcast.71), channel_id=1, source_target_pairs={{0,8},{1,121},{2,10},{3,123},{4,12},{5,125},{6,14},{7,127},{8,16},... | collective-permute-start | bytes 98312 | tf_op jit(solution)/shard_map/ppermute | solution.py:242
  90.2 37.6 %collective-permute-start.4 = (bf16[4,16,2,128]{3,2,1,0:T(2,128)(2,1)S(1)}, bf16[4,16,2,128]{3,2,1,0:T(2,128)(2,1)S(1)}, u32[]{:S(2)}, u32[]{:S(2)}) collective-permute-start(bf16[4,16,2,128]{3,2,1,0:T(2,128)(2,1)S(1)} %bitcast.70), channel_id=1, source_target_pairs={{0,16},{1,113},{2,18},{3,115},{4,20},{5,117},{6,22},{7,119},{8,24}... | collective-permute-start | bytes 98312 | tf_op jit(solution)/shard_map/ppermute | solution.py:242
  95.0 0.7 copy-start.4
  96.4 73.5 %copy-start = (bf16[16,8,2048]{2,1,0:T(8,128)(2,1)S(1)}, bf16[16,8,2048]{2,1,0:T(8,128)(2,1)}, u32[]{:S(2)}) copy-start(bf16[16,8,2048]{2,1,0:T(8,128)(2,1)} %x_ref.3) | copy-start | bytes 1572868
  127.9 22.8 %collective-permute-start.6 = (bf16[4,16,2,128]{3,2,1,0:T(2,128)(2,1)S(1)}, bf16[4,16,2,128]{3,2,1,0:T(2,128)(2,1)S(1)}, u32[]{:S(2)}, u32[]{:S(2)}) collective-permute-start(bf16[4,16,2,128]{3,2,1,0:T(2,128)(2,1)S(1)} %pad_maximum_fusion.5), channel_id=1, source_target_pairs={{0,32},{1,97},{2,34},{3,99},{4,36},{5,101},{6,38},{7,103},{8,40},{... | collective-permute-start | bytes 98312 | tf_op jit(solution)/shard_map/ppermute | solution.py:242
  136.2 14.5 %collective-permute-start.7 = (bf16[4,16,2,128]{3,2,1,0:T(2,128)(2,1)S(1)}, bf16[4,16,2,128]{3,2,1,0:T(2,128)(2,1)S(1)}, u32[]{:S(2)}, u32[]{:S(2)}) collective-permute-start(bf16[4,16,2,128]{3,2,1,0:T(2,128)(2,1)S(1)} %pad_maximum_fusion.6), channel_id=1, source_target_pairs={{0,64},{1,65},{2,66},{3,67},{4,68},{5,69},{6,70},{7,71},{8,72},{9,... | collective-permute-start | bytes 98312 | tf_op jit(solution)/shard_map/ppermute | solution.py:242
  143.3 9.6 %collective-permute-start.8 = (bf16[4,16,2,128]{3,2,1,0:T(2,128)(2,1)S(1)}, bf16[4,16,2,128]{3,2,1,0:T(2,128)(2,1)S(1)}, u32[]{:S(2)}, u32[]{:S(2)}) collective-permute-start(bf16[4,16,2,128]{3,2,1,0:T(2,128)(2,1)S(1)} %pad_maximum_fusion.7), channel_id=1, source_target_pairs={{0,96},{1,33},{2,98},{3,35},{4,100},{5,37},{6,102},{7,39},{8,104},... | collective-permute-start | bytes 98312 | tf_op jit(solution)/shard_map/ppermute | solution.py:242
  169.8 1.8 %copy-start.1 = (bf16[64,768]{1,0:T(8,128)(2,1)S(1)}, bf16[64,768]{1,0:T(8,128)(2,1)}, u32[]{:S(2)}) copy-start(bf16[64,768]{1,0:T(8,128)(2,1)} %q_ref.1) | copy-start | bytes 294916

commit v8 on v5

--- a/solution.py
+++ b/solution.py
@@ -78,7 +78,7 @@
     tab_ref[...] = jnp.where(lane < 16, ret, pltpu.roll(slot, 16, 1))
     own_lane = lane == own
     first = jnp.sum(jnp.where(own_lane, starts, 0), axis=1, keepdims=True)
-    table = place + 4096 * first
+    table = place + jnp.where(lane == 0, 4096 * first, 0)
     lane8 = lax.broadcasted_iota(jnp.int32, (8, 128), 1)
     acc = jnp.zeros((8, 128), jnp.int32)
     for a in range(8):
@@ -96,10 +96,10 @@
     def step(a, carry):
         for r in range(8):
             h = a * 8 + r
-            both = [tabs[r, a * 16 + l] for l in range(16)]
-            place = [v & 4095 for v in both]
+            place = [tabs[r, a * 16 + l] for l in range(16)]
+            first = place[0] >> 12
+            place[0] = place[0] & 4095
             units = [r_ref[h, l] for l in range(16)]
-            first = both[0] >> 12
             slots = [jnp.minimum(first + s, CTX - 1) for s in range(2)]
             backs = [back_ref[slots[s], kv] for s in range(2) for kv in range(2)]
             for l in range(16):
@@ -109,14 +109,6 @@
         return carry
 
     lax.fori_loop(0, 8, step, 0)
-
-
-def collect_kernel(info_ref, recv_ref, out_ref):
-    for l in range(16):
-        for kv in range(2):
-            unit = recv_ref[info_ref[l] + kv]
-            for t in range(8):
-                out_ref[t * 32 + l * 2 + kv] = unit
 
 
 def attention_kernel(
@@ -171,22 +163,28 @@
             out_ref[:, h * HD : h * HD + HD] = out[n].astype(jnp.bfloat16)
 
 
-def update_kernel(pos_ref, x_ref, rows_ref, out_ref):
+def update_kernel(pos_ref, x_ref, rows_ref, out_ref, done, sems):
     row = lax.broadcasted_iota(jnp.int32, (8, 128), 0)
-
-    def step(l, carry):
+    copies = []
+    for l in range(16):
         at0 = row == pos_ref[2 * l]
         at1 = row == pos_ref[2 * l + 1]
         for head in range(8):
             for kv in range(2):
                 lanes = pl.ds(head * 256 + kv * 128, 128)
-                pairf = rows_ref[head, l, kv].astype(jnp.float32)
+                pair = rows_ref[head, l, kv].astype(jnp.float32)
                 old = x_ref[l, :, lanes].astype(jnp.float32)
-                new = jnp.where(at0, pairf[0:1], jnp.where(at1, pairf[1:2], old))
-                out_ref[l, :, lanes] = new.astype(jnp.bfloat16)
-        return carry
-
-    lax.fori_loop(0, 16, step, 0)
+                new = jnp.where(at0, pair[0:1], jnp.where(at1, pair[1:2], old))
+                done[l, :, lanes] = new.astype(jnp.bfloat16)
+        if l % 4 == 3:
+            part = pl.ds(l - 3, 4)
+            copy = pltpu.make_async_copy(
+                done.at[part], out_ref.at[part], sems.at[l // 4]
+            )
+            copy.start()
+            copies.append(copy)
+    for copy in copies:
+        copy.wait()
 
 
 def local(kv_cache, route, queries, fresh_kv, picked):
@@ -241,14 +239,11 @@
     )
 
     mine = lax.dynamic_index_in_dim(tab, own, 0, keepdims=False)
-    rows = pl.pallas_call(
-        collect_kernel,
-        out_shape=jax.ShapeDtypeStruct((256, 2, 128), bf),
-        in_specs=[SMEM, VMEM],
-        out_specs=VMEM,
-        compiler_params=PARAMS,
-        name="collect",
-    )(mine[:16], recv.reshape(64 * UNITS, 2, 128)).reshape(8, 16, 2, 2, 128)
+    units = recv.reshape(64, UNITS // 2, 2, 2, 128)
+    at = mine[:16] - route * UNITS
+    rows = units[
+        jnp.broadcast_to(route, (8, 16)), jnp.broadcast_to(at // 2, (8, 16))
+    ]
     rows = lax.all_to_all(rows, "tp", split_axis=0, concat_axis=0, tiled=True)
     picks = got[:, 16, 1, :64].reshape(64, 2, 32).astype(jnp.int32)
     pos = picks[route, :, mine[16:32]].reshape(32) - 8 * y
@@ -256,7 +251,10 @@
         update_kernel,
         out_shape=jax.ShapeDtypeStruct(kv_cache.shape, bf),
         in_specs=[SMEM, VMEM, VMEM],
-        out_specs=VMEM,
+        out_specs=pl.BlockSpec(memory_space=pl.ANY),
+        scratch_shapes=[
+            pltpu.VMEM(kv_cache.shape, bf), pltpu.SemaphoreType.DMA((4,)),
+        ],
         compiler_params=PARAMS,
         name="update",
     )(pos, kv_cache, rows)

time: 155 us -> 154 us (level)
  local copies, waits for them, and re-layouts: 2.67 us -> 4.39 us
  Pallas kernels: 12.8 us -> 11.1 us
    gather x0 -> x1, local copies, waits for them, and re-layouts: none -> 1.65 us  [local(): units[jnp.broadcast_to(route, (8, 16)), jnp.broadcast_to(at // 2, (8, 16))]]
where the time goes in v8:
time: 154 us
  waiting for transfers between devices  84.9 us (55%)
  starting transfers between devices  30.7 us (20%)
  blocking collectives  21.4 us (14%)
  Pallas kernels  11.1 us (7%)
  local copies, waits for them, and re-layouts  4.39 us (3%)
    all_to_all x1, waiting for transfers between devices, local(): lax.all_to_all(send.reshape(64, UNITS, 2, 128), 'inst', split_axis=0, con...  52.6 us
    all_to_all x1, waiting for transfers between devices, local(): got = lax.all_to_all(got, 'inst', split_axis=0, concat_axis=0, tiled=True)  30.2 us
    all_to_all x1, blocking collectives, local(): got = lax.all_to_all(spread, 'tp', split_axis=0, concat_axis=0, tiled=True)  21.4 us
    all_to_all x1, starting transfers between devices, local(): got = lax.all_to_all(got, 'inst', split_axis=0, concat_axis=0, tiled=True)  13.3 us
    all_to_all x1, starting transfers between devices, local(): lax.all_to_all(send.reshape(64, UNITS, 2, 128), 'inst', split_axis=0, con...  8.85 us
    all_to_all x1, starting transfers between devices, local(): rows = lax.all_to_all(rows, 'tp', split_axis=0, concat_axis=0, tiled=True)  8.51 us
    pallas_call x1, Pallas kernels, local(): pl.pallas_call(dispatch_kernel, out_shape=(jax.ShapeDtypeStruct((64 * UNI...  4.09 us
  transfers between devices with their start and end apart: 3, of which 3 were waited for; matrix products, arithmetic and copies ran while one was open for 2% of the time, Pallas kernels for 2%

profile of v8, /device:TPU:1, one launch (start us, length us, event | category | flops | bytes accessed | tf_op | source)
XLA Modules:
  0.0 153.9 jit_solution(13931635606828692458)
XLA Ops:
  0.6 2.6 %spread.1 = bf16[64,17,2,128]{3,2,1,0:T(2,128)(2,1)} custom-call(bf16[16,8,2048]{2,1,0:T(8,128)(2,1)} %x_ref.3, s32[16]{0:T(128)} %route_ref.1, s32[2,32]{1,0:T(2,128)} %bitcast.48), custom_call_target="tpu_custom_call" | custom-call | tf_op jit(solution)/shard_map/spread/pallas_call | solution.py:194
  3.2 21.4 %all_to_all.20 = bf16[64,17,2,128]{3,2,1,0:T(2,128)(2,1)} all-to-all(bf16[64,17,2,128]{3,2,1,0:T(2,128)(2,1)} %spread.1), channel_id=1, replica_groups=mesh['inst'=64,'tp'=8] {'tp'}, dimensions={0} | all-to-all | bytes 1114112 | tf_op jit(solution)/shard_map/all_to_all | solution.py:202
  24.6 13.3 %all-to-all-start.1 = ((bf16[64,17,2,128]{3,2,1,0:T(2,128)(2,1)}), bf16[64,17,2,128]{3,2,1,0:T(2,128)(2,1)S(1)}, u32[]{:S(2)}, u32[]{:S(2)}) async-start(bf16[64,17,2,128]{3,2,1,0:T(2,128)(2,1)} %all_to_all.20), calls=%async_computation.1 | async-start | bytes 1114112 | tf_op jit(solution)/shard_map/all_to_all | solution.py:203
  38.0 0.2 fusion.2
  38.2 0.1 fusion.1
  38.3 0.1 pad_maximum_fusion.2.back_ref
  38.3 30.2 %all-to-all-done.1.r_ref = bf16[64,17,2,128]{3,2,1,0:T(2,128)(2,1)S(1)} async-done(((bf16[64,17,2,128]{3,2,1,0:T(2,128)(2,1)}), bf16[64,17,2,128]{3,2,1,0:T(2,128)(2,1)S(1)}, u32[]{:S(2)}, u32[]{:S(2)}) %all-to-all-start.1) | async-done | bytes 557088 | tf_op jit(solution)/shard_map/all_to_all | solution.py:203
  68.5 4.1 %dispatch.1 = (bf16[2304,2,128]{2,1,0:T(2,128)(2,1)}, s32[64,128]{1,0:T(8,128)S(1)}, s32[1,128]{1,0:T(1,128)S(1)}) custom-call(s32[1]{0:T(128)} %bitcast.own_ref, bf16[64,17,2,128]{3,2,1,0:T(2,128)(2,1)S(1)} %all-to-all-done.1.r_ref, bf16[32,2,2,128]{3,2,1,0:T(2,128)(2,1)S(1)} %pad_maximum_fusion.2.back_ref), custom_call_target="tpu_custom_call" | custom-call | tf_op jit(solution)/shard_map/dispatch/pallas_call | solution.py:223
  72.7 8.9 %all-to-all-start.2 = ((bf16[64,36,2,128]{3,2,1,0:T(2,128)(2,1)}), bf16[64,36,2,128]{3,2,1,0:T(2,128)(2,1)S(1)}, u32[]{:S(2)}, u32[]{:S(2)}) async-start(bf16[64,36,2,128]{3,2,1,0:T(2,128)(2,1)} %bitcast.6), calls=%async_computation.2 | async-start | bytes 2359296 | tf_op jit(solution)/shard_map/all_to_all | solution.py:236
  81.6 0.1 copy.22
  81.7 0.1 reshape.218.qpos_ref
  81.7 0.1 eq.23
  81.8 0.1 eq.20
  81.9 0.1 eq.21
  82.0 0.1 broadcast_in_dim.66
  82.1 0.1 broadcast_in_dim.67
  82.2 0.1 fusion.9
  82.5 0.1 slice_convert_fusion
  82.5 0.1 copy.24
  82.7 0.1 reshape.207
  82.8 0.9 copy.25
  83.7 0.1 fusion.8
  83.8 0.6 gather_fusion
  84.4 52.6 %all-to-all-done.2 = bf16[64,36,2,128]{3,2,1,0:T(2,128)(2,1)S(1)} async-done(((bf16[64,36,2,128]{3,2,1,0:T(2,128)(2,1)}), bf16[64,36,2,128]{3,2,1,0:T(2,128)(2,1)S(1)}, u32[]{:S(2)}, u32[]{:S(2)}) %all-to-all-start.2) | async-done | bytes 1179680 | tf_op jit(solution)/shard_map/all_to_all | solution.py:236
  136.9 1.6 %gather_fusion.1 = bf16[128,2,2,128]{3,2,1,0:T(2,128)(2,1)} fusion(bf16[64,18,2,2,128]{4,3,2,1,0:T(2,128)(2,1)S(1)} %bitcast.42, s32[128]{0:T(128)S(1)} %reshape.207), kind=kCustom, calls=%fused_computation.1 | custom fusion | bytes 263168 | tf_op jit(solution)/shard_map/gather | solution.py:244
  138.6 8.5 %all-to-all-start.3 = ((bf16[8,16,2,2,128]{4,3,2,1,0:T(2,128)(2,1)}), bf16[8,16,2,2,128]{4,3,2,1,0:T(2,128)(2,1)S(1)}, u32[]{:S(2)}, u32[]{:S(2)}) async-start(bf16[8,16,2,2,128]{4,3,2,1,0:T(2,128)(2,1)} %bitcast.16), calls=%async_computation.3 | async-start | bytes 262144 | tf_op jit(solution)/shard_map/all_to_all | solution.py:247
  147.1 0.1 sub.41.pos_ref
  147.2 0.1 broadcast_in_dim.72.i1_ref
  147.3 0.1 broadcast_in_dim.70.i0_ref
  147.3 2.9 %attend.1 = bf16[64,768]{1,0:T(8,128)(2,1)} custom-call(s32[1]{0:T(128)S(1)} %bitcast.44, bf16[64,72,128]{2,1,0:T(8,128)(2,1)S(1)} %bitcast.43, bf16[64,768]{1,0:T(8,128)(2,1)S(1)} %copy-done.1, bf16[64,256]{1,0:T(8,128)(2,1)S(1)} %reshape.196.f0_ref, bf16[64,256]{1,0:T(8,128)(2,1)S(1)} %reshape.197.f1_ref, s32[64,128]{1,0:T(8,128)S(1)} %broadcast_in_dim.70.i0_ref, ...), custom_call_target="tpu_custom_call" | custom-call | flops 402653184 | bytes 1500000 | tf_op jit(solution)/shard_map/attend/pallas_call | solution.py:271
  150.2 2.1 %all-to-all-done.3.rows_ref = bf16[8,16,2,2,128]{4,3,2,1,0:T(2,128)(2,1)S(1)} async-done(((bf16[8,16,2,2,128]{4,3,2,1,0:T(2,128)(2,1)}), bf16[8,16,2,2,128]{4,3,2,1,0:T(2,128)(2,1)S(1)}, u32[]{:S(2)}, u32[]{:S(2)}) %all-to-all-start.3) | async-done | bytes 131104 | tf_op jit(solution)/shard_map/all_to_all | solution.py:247
  152.4 1.5 update.1
  (30 shorter events, 0.2 us)
Async XLA Ops:
  3.2 34.7 %copy-start.2 = (bf16[64,256]{1,0:T(8,128)(2,1)S(1)}, bf16[64,256]{1,0:T(8,128)(2,1)}, u32[]{:S(2)}) copy-start(bf16[64,256]{1,0:T(8,128)(2,1)} %param.8) | copy-start | bytes 98308
  24.6 43.9 %all-to-all-start.1 = ((bf16[64,17,2,128]{3,2,1,0:T(2,128)(2,1)}), bf16[64,17,2,128]{3,2,1,0:T(2,128)(2,1)S(1)}, u32[]{:S(2)}, u32[]{:S(2)}) async-start(bf16[64,17,2,128]{3,2,1,0:T(2,128)(2,1)} %all_to_all.20), calls=%async_computation.1 | async-start | bytes 1114112 | tf_op jit(solution)/shard_map/all_to_all | solution.py:203
  72.6 8.9 %copy-start.4 = (s32[32,2]{0,1:T(2,128)S(1)}, s32[32,2]{0,1:T(2,128)}, u32[]{:S(2)}) copy-start(s32[32,2]{0,1:T(2,128)} %param.9) | copy-start | bytes 772
  72.6 9.8 %copy-start.3 = (s32[16]{0:T(128)S(1)}, s32[16]{0:T(128)}, u32[]{:S(2)}) copy-start(s32[16]{0:T(128)} %route_ref.1) | copy-start | bytes 196
  72.7 64.3 %all-to-all-start.2 = ((bf16[64,36,2,128]{3,2,1,0:T(2,128)(2,1)}), bf16[64,36,2,128]{3,2,1,0:T(2,128)(2,1)S(1)}, u32[]{:S(2)}, u32[]{:S(2)}) async-start(bf16[64,36,2,128]{3,2,1,0:T(2,128)(2,1)} %bitcast.6), calls=%async_computation.2 | async-start | bytes 2359296 | tf_op jit(solution)/shard_map/all_to_all | solution.py:236
  82.3 65.0 %copy-start.1 = (bf16[64,768]{1,0:T(8,128)(2,1)S(1)}, bf16[64,768]{1,0:T(8,128)(2,1)}, u32[]{:S(2)}) copy-start(bf16[64,768]{1,0:T(8,128)(2,1)} %q_ref.1) | copy-start | bytes 294916
  83.8 68.6 %copy-start = (bf16[16,8,2048]{2,1,0:T(8,128)(2,1)S(1)}, bf16[16,8,2048]{2,1,0:T(8,128)(2,1)}, u32[]{:S(2)}) copy-start(bf16[16,8,2048]{2,1,0:T(8,128)(2,1)} %x_ref.3) | copy-start | bytes 1572868
  138.6 13.8 %all-to-all-start.3 = ((bf16[8,16,2,2,128]{4,3,2,1,0:T(2,128)(2,1)}), bf16[8,16,2,2,128]{4,3,2,1,0:T(2,128)(2,1)S(1)}, u32[]{:S(2)}, u32[]{:S(2)}) async-start(bf16[8,16,2,2,128]{4,3,2,1,0:T(2,128)(2,1)} %bitcast.16), calls=%async_computation.3 | async-start | bytes 262144 | tf_op jit(solution)/shard_map/all_to_all | solution.py:247

commit v9 on v8

--- a/solution.py
+++ b/solution.py
@@ -109,6 +109,14 @@
         return carry
 
     lax.fori_loop(0, 8, step, 0)
+
+
+def collect_kernel(info_ref, recv_ref, out_ref):
+    for l in range(16):
+        for kv in range(2):
+            unit = recv_ref[info_ref[l] + kv]
+            for t in range(8):
+                out_ref[t * 32 + l * 2 + kv] = unit
 
 
 def attention_kernel(
@@ -239,11 +247,14 @@
     )
 
     mine = lax.dynamic_index_in_dim(tab, own, 0, keepdims=False)
-    units = recv.reshape(64, UNITS // 2, 2, 2, 128)
-    at = mine[:16] - route * UNITS
-    rows = units[
-        jnp.broadcast_to(route, (8, 16)), jnp.broadcast_to(at // 2, (8, 16))
-    ]
+    rows = pl.pallas_call(
+        collect_kernel,
+        out_shape=jax.ShapeDtypeStruct((256, 2, 128), bf),
+        in_specs=[SMEM, VMEM],
+        out_specs=VMEM,
+        compiler_params=PARAMS,
+        name="collect",
+    )(mine[:16], recv.reshape(64 * UNITS, 2, 128)).reshape(8, 16, 2, 2, 128)
     rows = lax.all_to_all(rows, "tp", split_axis=0, concat_axis=0, tiled=True)
     picks = got[:, 16, 1, :64].reshape(64, 2, 32).astype(jnp.int32)
     pos = picks[route, :, mine[16:32]].reshape(32) - 8 * y

time: 154 us -> 154 us (level)
  local copies, waits for them, and re-layouts: 4.39 us -> 2.67 us
    gather x1 -> x0, local copies, waits for them, and re-layouts: 1.65 us -> none  [local(): units[jnp.broadcast_to(route, (8, 16)), jnp.broadcast_to(at // 2, (8, 16))]]
where the time goes in v9:
time: 154 us
  waiting for transfers between devices  85 us (55%)
  starting transfers between devices  30.8 us (20%)
  blocking collectives  21.4 us (14%)
  Pallas kernels  12.4 us (8%)
  local copies, waits for them, and re-layouts  2.67 us (2%)
    all_to_all x1, waiting for transfers between devices, local(): lax.all_to_all(send.reshape(64, UNITS, 2, 128), 'inst', split_axis=0, con...  52.7 us
    all_to_all x1, waiting for transfers between devices, local(): got = lax.all_to_all(got, 'inst', split_axis=0, concat_axis=0, tiled=True)  30.2 us
    all_to_all x1, blocking collectives, local(): got = lax.all_to_all(spread, 'tp', split_axis=0, concat_axis=0, tiled=True)  21.4 us
    all_to_all x1, starting transfers between devices, local(): got = lax.all_to_all(got, 'inst', split_axis=0, concat_axis=0, tiled=True)  13.3 us
    all_to_all x1, starting transfers between devices, local(): lax.all_to_all(send.reshape(64, UNITS, 2, 128), 'inst', split_axis=0, con...  8.85 us
    all_to_all x1, starting transfers between devices, local(): rows = lax.all_to_all(rows, 'tp', split_axis=0, concat_axis=0, tiled=True)  8.64 us
    pallas_call x1, Pallas kernels, local(): pl.pallas_call(dispatch_kernel, out_shape=(jax.ShapeDtypeStruct((64 * UNI...  4.09 us
  transfers between devices with their start and end apart: 3, of which 3 were waited for; matrix products, arithmetic and copies ran while one was open for 2% of the time, Pallas kernels for 2%

profile of v9, /device:TPU:1, one launch (start us, length us, event | category | flops | bytes accessed | tf_op | source)
XLA Modules:
  0.0 153.6 jit_solution(13972621688833609097)
XLA Ops:
  0.6 2.6 %spread.1 = bf16[64,17,2,128]{3,2,1,0:T(2,128)(2,1)} custom-call(bf16[16,8,2048]{2,1,0:T(8,128)(2,1)} %x_ref.3, s32[16]{0:T(128)} %route_ref.1, s32[2,32]{1,0:T(2,128)} %bitcast.45), custom_call_target="tpu_custom_call" | custom-call | tf_op jit(solution)/shard_map/spread/pallas_call | solution.py:202
  3.2 21.4 %all_to_all.20 = bf16[64,17,2,128]{3,2,1,0:T(2,128)(2,1)} all-to-all(bf16[64,17,2,128]{3,2,1,0:T(2,128)(2,1)} %spread.1), channel_id=1, replica_groups=mesh['inst'=64,'tp'=8] {'tp'}, dimensions={0} | all-to-all | bytes 1114112 | tf_op jit(solution)/shard_map/all_to_all | solution.py:210
  24.6 13.3 %all-to-all-start.1 = ((bf16[64,17,2,128]{3,2,1,0:T(2,128)(2,1)}), bf16[64,17,2,128]{3,2,1,0:T(2,128)(2,1)S(1)}, u32[]{:S(2)}, u32[]{:S(2)}) async-start(bf16[64,17,2,128]{3,2,1,0:T(2,128)(2,1)} %all_to_all.20), calls=%async_computation.1 | async-start | bytes 1114112 | tf_op jit(solution)/shard_map/all_to_all | solution.py:211
  38.0 0.2 fusion.2
  38.2 0.1 fusion.1
  38.3 0.1 pad_maximum_fusion.2.back_ref
  38.3 30.2 %all-to-all-done.1.r_ref = bf16[64,17,2,128]{3,2,1,0:T(2,128)(2,1)S(1)} async-done(((bf16[64,17,2,128]{3,2,1,0:T(2,128)(2,1)}), bf16[64,17,2,128]{3,2,1,0:T(2,128)(2,1)S(1)}, u32[]{:S(2)}, u32[]{:S(2)}) %all-to-all-start.1) | async-done | bytes 557088 | tf_op jit(solution)/shard_map/all_to_all | solution.py:211
  68.5 4.1 %dispatch.1 = (bf16[2304,2,128]{2,1,0:T(2,128)(2,1)}, s32[64,128]{1,0:T(8,128)S(1)}, s32[1,128]{1,0:T(1,128)S(1)}) custom-call(s32[1]{0:T(128)} %bitcast.own_ref, bf16[64,17,2,128]{3,2,1,0:T(2,128)(2,1)S(1)} %all-to-all-done.1.r_ref, bf16[32,2,2,128]{3,2,1,0:T(2,128)(2,1)S(1)} %pad_maximum_fusion.2.back_ref), custom_call_target="tpu_custom_call" | custom-call | tf_op jit(solution)/shard_map/dispatch/pallas_call | solution.py:231
  72.6 0.0 copy-start.3
  72.6 8.9 %all-to-all-start.2 = ((bf16[64,36,2,128]{3,2,1,0:T(2,128)(2,1)}), bf16[64,36,2,128]{3,2,1,0:T(2,128)(2,1)S(1)}, u32[]{:S(2)}, u32[]{:S(2)}) async-start(bf16[64,36,2,128]{3,2,1,0:T(2,128)(2,1)} %bitcast.6), calls=%async_computation.2 | async-start | bytes 2359296 | tf_op jit(solution)/shard_map/all_to_all | solution.py:244
  81.6 0.1 copy.22
  81.7 0.1 reshape.114.qpos_ref
  81.7 0.1 eq.23
  81.8 0.1 eq.20
  81.9 0.1 eq.21
  82.0 0.1 broadcast_in_dim.50
  82.1 0.1 broadcast_in_dim.51
  82.2 0.1 fusion.12
  82.4 0.1 slice_convert_fusion
  82.5 0.1 copy.24
  82.6 0.9 copy.25
  83.5 0.1 fusion.11
  83.6 0.6 gather_fusion
  84.2 52.7 %all-to-all-done.2 = bf16[64,36,2,128]{3,2,1,0:T(2,128)(2,1)S(1)} async-done(((bf16[64,36,2,128]{3,2,1,0:T(2,128)(2,1)}), bf16[64,36,2,128]{3,2,1,0:T(2,128)(2,1)S(1)}, u32[]{:S(2)}, u32[]{:S(2)}) %all-to-all-start.2) | async-done | bytes 1179680 | tf_op jit(solution)/shard_map/all_to_all | solution.py:244
  136.9 1.3 collect.1
  138.2 8.6 %all-to-all-start.3 = ((bf16[8,16,2,2,128]{4,3,2,1,0:T(2,128)(2,1)}), bf16[8,16,2,2,128]{4,3,2,1,0:T(2,128)(2,1)S(1)}, u32[]{:S(2)}, u32[]{:S(2)}) async-start(bf16[8,16,2,2,128]{4,3,2,1,0:T(2,128)(2,1)} %bitcast.16), calls=%async_computation.3 | async-start | bytes 262144 | tf_op jit(solution)/shard_map/all_to_all | solution.py:258
  146.8 0.1 sub.34.pos_ref
  146.9 0.1 broadcast_in_dim.56.i1_ref
  147.0 0.1 broadcast_in_dim.54.i0_ref
  147.1 2.9 %attend.1 = bf16[64,768]{1,0:T(8,128)(2,1)} custom-call(s32[1]{0:T(128)S(1)} %bitcast.41, bf16[64,72,128]{2,1,0:T(8,128)(2,1)S(1)} %bitcast.40, bf16[64,768]{1,0:T(8,128)(2,1)S(1)} %copy-done.1, bf16[64,256]{1,0:T(8,128)(2,1)S(1)} %reshape.97.f0_ref, bf16[64,256]{1,0:T(8,128)(2,1)S(1)} %reshape.98.f1_ref, s32[64,128]{1,0:T(8,128)S(1)} %broadcast_in_dim.54.i0_ref, ...), custom_call_target="tpu_custom_call" | custom-call | flops 402653184 | bytes 1500000 | tf_op jit(solution)/shard_map/attend/pallas_call | solution.py:282
  150.0 2.1 %all-to-all-done.3.rows_ref = bf16[8,16,2,2,128]{4,3,2,1,0:T(2,128)(2,1)S(1)} async-done(((bf16[8,16,2,2,128]{4,3,2,1,0:T(2,128)(2,1)}), bf16[8,16,2,2,128]{4,3,2,1,0:T(2,128)(2,1)S(1)}, u32[]{:S(2)}, u32[]{:S(2)}) %all-to-all-start.3) | async-done | bytes 131104 | tf_op jit(solution)/shard_map/all_to_all | solution.py:258
  152.1 1.5 update.1
  (26 shorter events, 0.2 us)
Async XLA Ops:
  3.2 34.7 %copy-start.2 = (bf16[64,256]{1,0:T(8,128)(2,1)S(1)}, bf16[64,256]{1,0:T(8,128)(2,1)}, u32[]{:S(2)}) copy-start(bf16[64,256]{1,0:T(8,128)(2,1)} %param.8) | copy-start | bytes 98308
  24.6 43.9 %all-to-all-start.1 = ((bf16[64,17,2,128]{3,2,1,0:T(2,128)(2,1)}), bf16[64,17,2,128]{3,2,1,0:T(2,128)(2,1)S(1)}, u32[]{:S(2)}, u32[]{:S(2)}) async-start(bf16[64,17,2,128]{3,2,1,0:T(2,128)(2,1)} %all_to_all.20), calls=%async_computation.1 | async-start | bytes 1114112 | tf_op jit(solution)/shard_map/all_to_all | solution.py:211
  72.6 8.9 %copy-start.3 = (s32[32,2]{0,1:T(2,128)S(1)}, s32[32,2]{0,1:T(2,128)}, u32[]{:S(2)}) copy-start(s32[32,2]{0,1:T(2,128)} %param.9) | copy-start | bytes 772
  72.6 64.3 %all-to-all-start.2 = ((bf16[64,36,2,128]{3,2,1,0:T(2,128)(2,1)}), bf16[64,36,2,128]{3,2,1,0:T(2,128)(2,1)S(1)}, u32[]{:S(2)}, u32[]{:S(2)}) async-start(bf16[64,36,2,128]{3,2,1,0:T(2,128)(2,1)} %bitcast.6), calls=%async_computation.2 | async-start | bytes 2359296 | tf_op jit(solution)/shard_map/all_to_all | solution.py:244
  81.5 2.0 %copy-start.4 = (s32[16]{0:T(128)S(1)}, s32[16]{0:T(128)}, u32[]{:S(2)}) copy-start(s32[16]{0:T(128)} %route_ref.1) | copy-start | bytes 196
  82.6 64.5 %copy-start.1 = (bf16[64,768]{1,0:T(8,128)(2,1)S(1)}, bf16[64,768]{1,0:T(8,128)(2,1)}, u32[]{:S(2)}) copy-start(bf16[64,768]{1,0:T(8,128)(2,1)} %q_ref.1) | copy-start | bytes 294916
  138.2 13.9 %copy-start = (bf16[16,8,2048]{2,1,0:T(8,128)(2,1)S(1)}, bf16[16,8,2048]{2,1,0:T(8,128)(2,1)}, u32[]{:S(2)}) copy-start(bf16[16,8,2048]{2,1,0:T(8,128)(2,1)} %x_ref.3) | copy-start | bytes 1572868
  138.2 13.9 %all-to-all-start.3 = ((bf16[8,16,2,2,128]{4,3,2,1,0:T(2,128)(2,1)}), bf16[8,16,2,2,128]{4,3,2,1,0:T(2,128)(2,1)S(1)}, u32[]{:S(2)}, u32[]{:S(2)}) async-start(bf16[8,16,2,2,128]{4,3,2,1,0:T(2,128)(2,1)} %bitcast.16), calls=%async_computation.3 | async-start | bytes 262144 | tf_op jit(solution)/shard_map/all_to_all | solution.py:258
